TPU v7x, 256 devices: a whole 4x4x8 slice. The times are simulated.
256 devices in a mesh: section: 8 (over z_lo, core), ctx: 32 (over y, z_hi, x).
Axes of the slice: x: 4, y: 4, z: 8 (z_hi: 2, z_lo: 4; z = z_hi * 4 + z_lo), core: 2. Of those that a mesh axis runs over, the one named last changes fastest.
Arguments:
- sent_queries: bfloat16 [8, 4096, 4096], P('section', 'ctx'), may hold values from -60 to 60
- sent_keyvals: bfloat16 [8, 4096, 2, 512], P('section', 'ctx'), may hold values from -5 to 5
- forward_lengths: int32 [8, 16], P('section'), may hold values from 1 to 512, 4096 in all within a row
- kept_queries: bfloat16 [8, 4096, 4096], P('section', 'ctx'), may hold values from -60 to 60
- kept_keyvals: bfloat16 [8, 4096, 2, 512], P('section', 'ctx'), may hold values from -5 to 5
- sent_grad: bfloat16 [8, 4096, 4096], P('section', 'ctx'), may hold values from -6 to 6
- backward_lengths: int32 [8, 16], P('section'), may hold values from 1 to 512, 4096 in all within a row
Outputs:
- attention_out: bfloat16 [8, 4096, 4096], P('section', 'ctx')
- query_grad: bfloat16 [8, 4096, 4096], P('section', 'ctx')
- keyval_grad: bfloat16 [8, 4096, 2, 512], P('section', 'ctx')
Inputs may be any that keep to these rules, and one draw needn't show every extreme that they name: `forward_lengths`: each row of 16 lengths sums to 4096; the longest document has exactly 512 tokens. `backward_lengths`: each row of 16 lengths sums to 4096; the longest document has exactly 512 tokens.
All inputs are finite; a program needn't handle non-finite values.
Results may differ from a plain program's by a relative error of at most 0.04.
Values may be sent and summed in bfloat16 or wider, within the bound.
No kernel may reach another device: no remote copies, remote signals or barrier semaphores. Data moves between devices by JAX's collectives and lax.ppermute only.
A program may use at most 128 MiB of HBM per device.

v0:
```python
import math

import jax
import jax.numpy as jnp
from jax import lax
from jax.sharding import PartitionSpec as P

QUERY_HEADS = 32
LOCAL_KV_HEADS = 4
HEAD_WIDTH = 128
REACH = 4


masked_value = -1e30


def passed_along(block, axis, distance):
    devices = range(lax.axis_size(axis))
    route = [((i - distance) % len(devices), i) for i in devices]
    return lax.ppermute(block, axis, route)


def passed_along_2(block, axis, distance):
    devices = range(lax.axis_size(axis))
    route = [(i - distance, i) for i in devices if i - distance in devices]
    return lax.ppermute(block, axis, route)


def rounded_output(values):
    return lax.optimization_barrier(values.astype(jnp.bfloat16)).astype(jnp.float32)


def document_of(lengths, positions):
    doc_ends = jnp.cumsum(lengths)
    return jnp.sum((positions[:, None] >= doc_ends[None, :]).astype(jnp.int32), axis=1)


def make_frame(query_matrix, lengths, first_row):
    local_tokens = query_matrix.shape[0]
    query_heads_input = query_matrix.reshape(
        local_tokens, LOCAL_KV_HEADS, QUERY_HEADS // LOCAL_KV_HEADS, HEAD_WIDTH
    )
    query_pos = first_row + jnp.arange(local_tokens, dtype=jnp.int32)
    return (query_heads_input, query_pos, document_of(lengths, query_pos), lengths)


def visible(query_frame, key_start, block_len):
    query_heads_input, query_pos, query_doc, lengths = query_frame
    key_pos = key_start + jnp.arange(block_len, dtype=jnp.int32)
    key_doc = document_of(lengths, key_pos)
    same_doc = query_doc[:, None] == key_doc[None, :]
    return same_doc & (key_pos[None, :] <= query_pos[:, None]) & (key_pos[None, :] >= 0)


def block_scores(query_heads_input, key_matrix, allowed):
    attention_scores = jnp.einsum(
        "wofu,aou->ofwa", query_heads_input, key_matrix, preferred_element_type=jnp.float32
    ) * (1.0 / math.sqrt(HEAD_WIDTH))
    return jnp.where(allowed, attention_scores, masked_value)


def empty_state(local_tokens):
    statistic_shape = (LOCAL_KV_HEADS, QUERY_HEADS // LOCAL_KV_HEADS, local_tokens)
    return (
        jnp.full(statistic_shape, masked_value, jnp.float32),
        jnp.zeros(statistic_shape, jnp.float32),
        jnp.zeros(statistic_shape + (HEAD_WIDTH,), jnp.float32),
    )


def attend_segment(running, keyvalue_segment, segment_start, query_frame):
    key_total = keyvalue_segment.shape[0]
    block_list = keyvalue_segment.reshape(
        key_total // key_total, key_total, 2, LOCAL_KV_HEADS, HEAD_WIDTH
    )
    query_heads_input = query_frame[0]

    def attend_block(running, block_item):
        keyvalue_block, block_index = block_item
        allowed = visible(query_frame, segment_start + block_index * key_total, key_total)

        def update(running):
            row_top, row_total, weighted_values = running
            attention_scores = block_scores(query_heads_input, keyvalue_block[:, 0], allowed)
            new_top = jnp.maximum(row_top, jnp.max(attention_scores, axis=-1))
            rescale = jnp.exp(row_top - new_top)
            exponent_weights = jnp.where(
                allowed, jnp.exp(attention_scores - new_top[..., None]), 0.0
            )
            row_total = row_total * rescale + jnp.sum(exponent_weights, axis=-1)
            product = jnp.einsum(
                "qmoe,eqx->qmox",
                exponent_weights.astype(jnp.bfloat16),
                keyvalue_block[:, 1],
                preferred_element_type=jnp.float32,
            )
            return (new_top, row_total, weighted_values * rescale[..., None] + product)

        def unchanged(running):
            return running

        return (lax.cond(jnp.any(allowed), update, unchanged, running), None)

    block_numbers = jnp.arange(block_list.shape[0], dtype=jnp.int32)
    return lax.scan(attend_block, running, (block_list, block_numbers))[0]


def finish(running):
    row_top, row_total, weighted_values = running
    local_tokens = weighted_values.shape[2]
    attended_rows = (
        (weighted_values / row_total[..., None])
        .transpose(2, 0, 1, 3)
        .reshape(local_tokens, QUERY_HEADS * HEAD_WIDTH)
        .astype(jnp.bfloat16)
    )
    return (attended_rows, row_top + jnp.log(row_total))


def grad_segment(
    keyvalue_segment, segment_start, query_frame, incoming_gradient, log_total, delta_rows
):
    key_total = keyvalue_segment.shape[0]
    block_list = keyvalue_segment.reshape(
        key_total // key_total, key_total, 2, LOCAL_KV_HEADS, HEAD_WIDTH
    )
    query_heads_input = query_frame[0]
    logit_scale = 1.0 / math.sqrt(HEAD_WIDTH)

    def grad_block(query_gradients, block_item):
        keyvalue_block, block_index = block_item
        allowed = visible(query_frame, segment_start + block_index * key_total, key_total)

        def work_on(query_gradients):
            attention_scores = block_scores(query_heads_input, keyvalue_block[:, 0], allowed)
            softmax_probabilities = jnp.where(
                allowed, jnp.exp(attention_scores - log_total[..., None]), 0.0
            )
            value_gradients = jnp.einsum(
                "cvby,bcvi->yci",
                softmax_probabilities.astype(jnp.bfloat16),
                incoming_gradient,
                preferred_element_type=jnp.float32,
            )
            probability_gradients = jnp.einsum(
                "wofu,aou->ofwa",
                incoming_gradient,
                keyvalue_block[:, 1],
                preferred_element_type=jnp.float32,
            )
            score_gradients = (
                softmax_probabilities * (probability_gradients - delta_rows[..., None])
            ).astype(jnp.bfloat16)
            query_step = (
                jnp.einsum(
                    "oqbh,hou->boqu",
                    score_gradients,
                    keyvalue_block[:, 0],
                    preferred_element_type=jnp.float32,
                )
                * logit_scale
            )
            key_gradients = (
                jnp.einsum(
                    "cvby,bcvi->yci",
                    score_gradients,
                    query_heads_input,
                    preferred_element_type=jnp.float32,
                )
                * logit_scale
            )
            return (
                query_gradients + query_step,
                jnp.stack([key_gradients, value_gradients], axis=1),
            )

        def skipped(query_gradients):
            return (
                query_gradients,
                jnp.zeros((key_total, 2, LOCAL_KV_HEADS, HEAD_WIDTH), jnp.float32),
            )

        return lax.cond(jnp.any(allowed), work_on, skipped, query_gradients)

    block_numbers = jnp.arange(block_list.shape[0], dtype=jnp.int32)
    query_gradients, keyvalue_gradients = lax.scan(
        grad_block, jnp.zeros(query_heads_input.shape, jnp.float32), (block_list, block_numbers)
    )
    return (query_gradients, keyvalue_gradients.reshape(key_total, 2, LOCAL_KV_HEADS * HEAD_WIDTH))


def body(
    sent_queries,
    sent_keyvals,
    forward_lengths,
    kept_queries,
    kept_keyvals,
    sent_grad,
    backward_lengths,
):
    local_tokens = sent_queries.shape[1]
    first_row = lax.axis_index("ctx") * local_tokens
    window_start = first_row - REACH * local_tokens
    arrived_queries, arrived_keyvals = passed_along((sent_queries, sent_keyvals), "section", 1)
    gradient_rows = passed_along(sent_grad, "section", -1)
    own_keyvals = arrived_keyvals[0]
    query_frame = make_frame(arrived_queries[0], forward_lengths[0], first_row)
    near_pieces = [
        passed_along_2(own_keyvals, "ctx", hop_count) for hop_count in range(REACH, 0, -1)
    ]
    near_window = jnp.concatenate(near_pieces + [own_keyvals], axis=0)
    running = attend_segment(empty_state(local_tokens), near_window, window_start, query_frame)
    attention_out = finish(running)[0]
    kept_frame = make_frame(kept_queries[0], backward_lengths[0], first_row)
    kept_rows = kept_keyvals[0]
    back_pieces = [passed_along_2(kept_rows, "ctx", hop_count) for hop_count in range(REACH, 0, -1)]
    key_segment = jnp.concatenate(back_pieces + [kept_rows], axis=0)
    recomputed_output, log_total = finish(
        attend_segment(empty_state(local_tokens), key_segment, window_start, kept_frame)
    )
    incoming_gradient = gradient_rows[0].reshape(
        local_tokens, LOCAL_KV_HEADS, QUERY_HEADS // LOCAL_KV_HEADS, HEAD_WIDTH
    )
    recomputed_heads = recomputed_output.reshape(
        local_tokens, LOCAL_KV_HEADS, QUERY_HEADS // LOCAL_KV_HEADS, HEAD_WIDTH
    ).astype(jnp.float32)
    delta_rows = jnp.sum(
        incoming_gradient.astype(jnp.float32) * recomputed_heads, axis=-1
    ).transpose(1, 2, 0)
    query_gradients, keyvalue_gradients = grad_segment(
        key_segment, window_start, kept_frame, incoming_gradient, log_total, delta_rows
    )
    kv_terms = rounded_output(keyvalue_gradients)
    summed = kv_terms[REACH * local_tokens :]
    for hop_count in range(1, REACH + 1):
        offset_rows = (REACH - hop_count) * local_tokens
        outgoing = kv_terms[offset_rows : offset_rows + local_tokens].astype(jnp.bfloat16)
        returned = passed_along_2(outgoing, "ctx", -hop_count)
        summed = summed + returned.astype(jnp.float32)
    query_grad = query_gradients.reshape(local_tokens, QUERY_HEADS * HEAD_WIDTH).astype(
        jnp.bfloat16
    )
    return (attention_out[None], query_grad[None], summed.astype(jnp.bfloat16)[None])


def solution(mesh):
    placed = (
        P("section", "ctx", None),
        P("section", "ctx", None, None),
        P("section", None),
        P("section", "ctx", None),
        P("section", "ctx", None, None),
        P("section", "ctx", None),
        P("section", None),
    )
    return jax.shard_map(
        body,
        mesh=mesh,
        in_specs=placed,
        out_specs=(
            P("section", "ctx", None),
            P("section", "ctx", None),
            P("section", "ctx", None, None),
        ),
        check_vma=False,
    )
```

profile of v0, /device:TPU:109, one launch (start us, length us, event | category | flops | bytes accessed | tf_op | source)
XLA Modules:
  0.0 225.4 jit_solution(393059980325452636)
XLA Ops:
  4.7 6.4 %collective-permute-start.8 = (bf16[128,2,512]{0,2,1:T(8,128)(2,1)S(1)}, bf16[128,2,512]{0,2,1:T(8,128)(2,1)S(1)}, u32[]{:S(2)}, u32[]{:S(2)}) collective-permute-start(bf16[128,2,512]{0,2,1:T(8,128)(2,1)S(1)} %bitcast.152), channel_id=1, source_target_pairs={{0,2},{1,3},{2,4},{3,5},{4,6},{5,7},{6,8},{7,9},{8,10},{9,11},{10,... | collective-permute-start | bytes 786440 | tf_op jit(solution)/shard_map/ppermute | solution.py:26
  11.1 4.7 %collective-permute-start.7 = (bf16[128,2,512]{0,2,1:T(8,128)(2,1)S(1)}, bf16[128,2,512]{0,2,1:T(8,128)(2,1)S(1)}, u32[]{:S(2)}, u32[]{:S(2)}) collective-permute-start(bf16[128,2,512]{0,2,1:T(8,128)(2,1)S(1)} %bitcast.153), channel_id=1, source_target_pairs={{0,3},{1,4},{2,5},{3,6},{4,7},{5,8},{6,9},{7,10},{8,11},{9,12},{10... | collective-permute-start | bytes 786440 | tf_op jit(solution)/shard_map/ppermute | solution.py:26
  15.7 6.1 %collective-permute-start.6 = (bf16[128,2,512]{0,2,1:T(8,128)(2,1)S(1)}, bf16[128,2,512]{0,2,1:T(8,128)(2,1)}, u32[]{:S(2)}, u32[]{:S(2)}) collective-permute-start(bf16[128,2,512]{0,2,1:T(8,128)(2,1)S(1)} %bitcast.154), channel_id=1, source_target_pairs={{0,4},{1,5},{2,6},{3,7},{4,8},{5,9},{6,10},{7,11},{8,12},{9,13},{1... | collective-permute-start | bytes 786440 | tf_op jit(solution)/shard_map/ppermute | solution.py:26
  23.7 3.3 %collective-permute-start = (bf16[1,128,2,512]{1,3,2,0:T(8,128)(2,1)}, bf16[1,128,2,512]{1,3,2,0:T(8,128)(2,1)}, u32[]{:S(2)}, u32[]{:S(2)}) collective-permute-start(bf16[1,128,2,512]{1,3,2,0:T(8,128)(2,1)} %copy.45), channel_id=1, source_target_pairs={{224,0},{0,32},{32,64},{64,96},{96,128},{128,160},{160,192},{192,2... | collective-permute-start | bytes 786440 | tf_op jit(solution)/shard_map/ppermute | solution.py:20
  36.1 11.8 %collective-permute-done.6 = bf16[128,2,512]{0,2,1:T(8,128)(2,1)} collective-permute-done((bf16[128,2,512]{0,2,1:T(8,128)(2,1)S(1)}, bf16[128,2,512]{0,2,1:T(8,128)(2,1)}, u32[]{:S(2)}, u32[]{:S(2)}) %collective-permute-start.6) | collective-permute-done | bytes 262176 | tf_op jit(solution)/shard_map/ppermute | solution.py:26
  47.9 4.2 %collective-permute-start.10 = (bf16[1,128,4096]{1,2,0:T(8,128)(2,1)}, bf16[1,128,4096]{1,2,0:T(8,128)(2,1)}, u32[]{:S(2)}, u32[]{:S(2)}) collective-permute-start(bf16[1,128,4096]{1,2,0:T(8,128)(2,1)} %copy.54), channel_id=1, source_target_pairs={{32,0},{64,32},{96,64},{128,96},{160,128},{192,160},{224,192},{0,2... | collective-permute-start | bytes 3145736 | tf_op jit(solution)/shard_map/ppermute | solution.py:20
  56.5 5.1 %collective-permute-start.1 = (bf16[128,2,512]{0,2,1:T(8,128)(2,1)}, bf16[128,2,512]{0,2,1:T(8,128)(2,1)}, u32[]{:S(2)}, u32[]{:S(2)}) collective-permute-start(bf16[128,2,512]{0,2,1:T(8,128)(2,1)} %bitcast.32), channel_id=1, source_target_pairs={{0,4},{1,5},{2,6},{3,7},{4,8},{5,9},{6,10},{7,11},{8,12},{9,13},{1... | collective-permute-start | bytes 786440 | tf_op jit(solution)/shard_map/ppermute | solution.py:26
  62.4 19.4 %collective-permute-start.2 = (bf16[128,2,512]{0,2,1:T(8,128)(2,1)}, bf16[128,2,512]{0,2,1:T(8,128)(2,1)}, u32[]{:S(2)}, u32[]{:S(2)}) collective-permute-start(bf16[128,2,512]{0,2,1:T(8,128)(2,1)} %bitcast.32), channel_id=1, source_target_pairs={{0,3},{1,4},{2,5},{3,6},{4,7},{5,8},{6,9},{7,10},{8,11},{9,12},{10... | collective-permute-start | bytes 786440 | tf_op jit(solution)/shard_map/ppermute | solution.py:26
  83.3 13.3 %conditional.4 = (f32[4,8,128]{2,1,0:T(8,128)}, f32[4,8,128]{2,1,0:T(8,128)S(1)}, f32[4,8,128,128]{3,2,1,0:T(8,128)S(1)}) conditional(s32[]{:T(128)} %convert_element_type.116, (f32[4,8,128]{2,1,0:T(8,128)S(1)}, f32[4,8,128]{2,1,0:T(8,128)S(1)}, f32[4,8,128,128]{3,2,1,0:T(8,128)}) %tuple.54, (pred[128,640]{0,1:T(8,128)(4,1)S(1)}, ...), branch_computations={%region_12.13_spmd, %region_13.16_spmd} | conditional | flops 1377312768 | bytes 51593296 | solution.py:102
  87.2 3.5 %fusion.15 = f32[4,8,128]{2,1,0:T(8,128)S(1)} fusion(f32[4,640,128,8]{2,1,3,0:T(8,128)S(1)} %get-tuple-element.277, f32[4,8,128]{2,1,0:T(8,128)} %max.6, pred[128,640]{0,1:T(8,128)(4,1)S(1)} %get-tuple-element.185), kind=kLoop, calls=%fused_computation.21 | loop fusion | flops 13103104 | bytes 10600448 | tf_op jit(solution)/shard_map/while/body/eval_jaxpr/cond/branch_1_fun/reduce_sum | solution.py:90
  91.4 5.1 %multiply_add_fusion.2 = f32[4,8,128,128]{3,2,1,0:T(8,128)S(1)} fusion(f32[4,8,128,128]{3,2,1,0:T(8,128)} %get-tuple-element.189, f32[4,640,128,8]{2,1,3,0:T(8,128)S(1)} %get-tuple-element.277, f32[4,8,128]{2,1,0:T(8,128)} %max.6, pred[128,640]{0,1:T(8,128)(4,1)S(1)} %get-tuple-element.185, f32[4,8,128]{2,1,0:T(8,128)S(1)} %get-tuple-element.269, ...), kind=kOutput, calls=%fused_computation.24 | convolution fusion | flops 685244416 | bytes 15450112 | tf_op jit(solution)/shard_map/while/body/eval_jaxpr/cond/branch_1_fun/qmoe,eqx->qmox/dot_general | solution.py:91
  99.8 9.6 %collective-permute-done.1 = bf16[128,2,512]{0,2,1:T(8,128)(2,1)} collective-permute-done((bf16[128,2,512]{0,2,1:T(8,128)(2,1)}, bf16[128,2,512]{0,2,1:T(8,128)(2,1)}, u32[]{:S(2)}, u32[]{:S(2)}) %collective-permute-start.1) | collective-permute-done | bytes 262176 | tf_op jit(solution)/shard_map/ppermute | solution.py:26
  109.4 13.4 %collective-permute-start.4 = (bf16[128,2,512]{0,2,1:T(8,128)(2,1)}, bf16[128,2,512]{0,2,1:T(8,128)(2,1)S(1)}, u32[]{:S(2)}, u32[]{:S(2)}) collective-permute-start(bf16[128,2,512]{0,2,1:T(8,128)(2,1)} %bitcast.32), channel_id=1, source_target_pairs={{0,1},{1,2},{2,3},{3,4},{4,5},{5,6},{6,7},{7,8},{8,9},{9,10},{10,1... | collective-permute-start | bytes 786440 | tf_op jit(solution)/shard_map/ppermute | solution.py:26
  132.3 20.2 %conditional.5 = (f32[128,4,8,128]{3,0,2,1:T(8,128)S(1)}, bf16[640,2,4,128]{3,0,2,1:T(8,128)(2,1)}) conditional(s32[]{:T(128)} %convert_element_type.116, f32[128,4,8,128]{3,0,2,1:T(8,128)S(1)} %broadcast_in_dim.99, (pred[128,640]{0,1:T(8,128)(4,1)S(1)}, bf16[640,2,4,128]{0,3,2,1:T(8,128)(2,1)}, bf16[128,4,8,128]{0,3,2,1:T(8,128)(2,1)S(1)}, ...), branch_computations={%region_17.18_spmd, %region_18.19_spmd} | conditional | flops 3389263872 | bytes 69599280 | solution.py:183
  138.2 3.8 %fusion.36 = bf16[640,1,4,128]{3,0,2,1:T(8,128)(2,1)S(1)} fusion(bf16[128,4,8,128]{0,3,2,1:T(8,128)(2,1)} %get-tuple-element.256, f32[4,640,128,8]{2,1,3,0:T(8,128)S(1)} %fusion.39, f32[4,8,128]{2,1,0:T(8,128)S(1)} %add.75, pred[128,640]{0,1:T(8,128)(4,1)S(1)} %get-tuple-element.191), kind=kOutput, calls=%fused_computation.48 | convolution fusion | flops 684195840 | bytes 12288000 | tf_op jit(solution)/shard_map/while/body/eval_jaxpr/cond/branch_1_fun/cvby,bcvi->yci/dot_general | solution.py:139
  142.0 5.0 %fusion.26 = bf16[4,8,128,640]{2,3,1,0:T(8,128)(2,1)S(1)} fusion(f32[4,640,128,8]{2,1,3,0:T(8,128)S(1)} %fusion.39, f32[4,8,128]{2,1,0:T(8,128)S(1)} %get-tuple-element.197, f32[4,8,128]{2,1,0:T(8,128)S(1)} %add.75, pred[128,640]{0,1:T(8,128)(4,1)S(1)} %get-tuple-element.191, bf16[128,4,8,128]{0,3,2,1:T(8,128)(2,1)} %get-tuple-element.256, ...), kind=kOutput, calls=%fused_computation.35 | convolution fusion | flops 689438720 | bytes 17547264 | tf_op jit(solution)/shard_map/while/body/eval_jaxpr/cond/branch_1_fun/wofu,aou->ofwa/dot_general | solution.py:145
  152.5 3.4 %copy.60 = bf16[640,2,4,128]{3,2,1,0:T(4,128)(2,1)} copy(bf16[640,2,4,128]{3,0,2,1:T(8,128)(2,1)} %get-tuple-element.214) | data formatting | bytes 2621440 | tf_op jit(solution)/shard_map/convert_element_type | solution.py:30
  155.9 3.9 %convert_element_type.124 = bf16[640,2,512]{2,1,0:T(2,128)(2,1)} reshape(bf16[640,2,4,128]{3,2,1,0:T(4,128)(2,1)} %copy.60) | data formatting | bytes 2621440 | tf_op jit(solution)/shard_map/convert_element_type | solution.py:30
  166.4 5.1 %collective-permute-start.13 = (bf16[128,2,512]{2,1,0:T(2,128)(2,1)}, bf16[128,2,512]{2,1,0:T(2,128)(2,1)}, u32[]{:S(2)}, u32[]{:S(2)}) collective-permute-start(bf16[128,2,512]{2,1,0:T(2,128)(2,1)} %get-tuple-element.280), channel_id=1, source_target_pairs={{3,0},{4,1},{5,2},{6,3},{7,4},{8,5},{9,6},{10,7},{11,8},{12,9},{13... | collective-permute-start | bytes 786440 | tf_op jit(solution)/shard_map/ppermute | solution.py:26
  171.6 4.1 %collective-permute-start.12 = (bf16[128,2,512]{2,1,0:T(2,128)(2,1)}, bf16[128,2,512]{2,1,0:T(2,128)(2,1)}, u32[]{:S(2)}, u32[]{:S(2)}) collective-permute-start(bf16[128,2,512]{2,1,0:T(2,128)(2,1)} %get-tuple-element.281), channel_id=1, source_target_pairs={{2,0},{3,1},{4,2},{5,3},{6,4},{7,5},{8,6},{9,7},{10,8},{11,9},{12,... | collective-permute-start | bytes 786440 | tf_op jit(solution)/shard_map/ppermute | solution.py:26
  175.7 15.8 %conditional.3 = ((f32[4,8,128]{2,1,0:T(8,128)S(1)}, f32[4,8,128,128]{3,2,1,0:T(8,128)})) conditional(s32[]{:T(128)} %convert_element_type.110, (f32[4,8,128]{2,1,0:T(8,128)S(1)}, f32[4,8,128,128]{3,2,1,0:T(8,128)}) %tuple.52, (pred[128,640]{0,1:T(8,128)(4,1)S(1)}, bf16[640,2,4,128]{0,3,2,1:T(8,128)(2,1)}, bf16[1,128,4096]{2,1,0:T(8,128)(2,1)}, ...), branch_computations={%region_4.5_spmd, %region_5.8_spmd} | conditional | flops 1377312768 | bytes 48447540 | solution.py:102
  185.5 6.0 %multiply_add_fusion = f32[4,8,128,128]{3,2,1,0:T(8,128)} fusion(f32[4,8,128,128]{3,2,1,0:T(8,128)} %get-tuple-element.183, f32[4,640,128,8]{2,1,3,0:T(8,128)S(1)} %get-tuple-element.275, f32[4,8,128]{2,1,0:T(8,128)S(1)} %max.5, pred[128,640]{0,1:T(8,128)(4,1)S(1)} %get-tuple-element.180, f32[4,8,128]{2,1,0:T(8,128)S(1)} %get-tuple-element.267, ...), kind=kOutput, calls=%fused_computation.7 | convolution fusion | flops 685244416 | bytes 15450112 | tf_op jit(solution)/shard_map/while/body/eval_jaxpr/cond/branch_1_fun/qmoe,eqx->qmox/dot_general | solution.py:91
  197.6 8.5 %collective-permute-done.13 = bf16[128,2,512]{2,1,0:T(2,128)(2,1)} collective-permute-done((bf16[128,2,512]{2,1,0:T(2,128)(2,1)}, bf16[128,2,512]{2,1,0:T(2,128)(2,1)}, u32[]{:S(2)}, u32[]{:S(2)}) %collective-permute-start.13) | collective-permute-done | bytes 262176 | tf_op jit(solution)/shard_map/ppermute | solution.py:26
  206.1 16.6 %collective-permute-done.12 = bf16[128,2,512]{2,1,0:T(2,128)(2,1)} collective-permute-done((bf16[128,2,512]{2,1,0:T(2,128)(2,1)}, bf16[128,2,512]{2,1,0:T(2,128)(2,1)}, u32[]{:S(2)}, u32[]{:S(2)}) %collective-permute-start.12) | collective-permute-done | bytes 262176 | tf_op jit(solution)/shard_map/ppermute | solution.py:26
  (85 shorter events, 73.6 us)
Async XLA Ops:
  0.6 32.6 %copy-start.5 = (bf16[1,128,4096]{2,1,0:T(8,128)(2,1)S(1)}, bf16[1,128,4096]{2,1,0:T(8,128)(2,1)}, u32[]{:S(2)}) copy-start(bf16[1,128,4096]{2,1,0:T(8,128)(2,1)} %param.18) | copy-start | bytes 3145732
  1.9 60.5 %collective-permute-start.9 = (bf16[128,2,512]{0,2,1:T(8,128)(2,1)S(1)}, bf16[128,2,512]{0,2,1:T(8,128)(2,1)S(1)}, u32[]{:S(2)}, u32[]{:S(2)}) collective-permute-start(bf16[128,2,512]{0,2,1:T(8,128)(2,1)S(1)} %bitcast.151), channel_id=1, source_target_pairs={{0,1},{1,2},{2,3},{3,4},{4,5},{5,6},{6,7},{7,8},{8,9},{9,10},{10,1... | collective-permute-start | bytes 786440 | tf_op jit(solution)/shard_map/ppermute | solution.py:26
  4.7 51.8 %collective-permute-start.8 = (bf16[128,2,512]{0,2,1:T(8,128)(2,1)S(1)}, bf16[128,2,512]{0,2,1:T(8,128)(2,1)S(1)}, u32[]{:S(2)}, u32[]{:S(2)}) collective-permute-start(bf16[128,2,512]{0,2,1:T(8,128)(2,1)S(1)} %bitcast.152), channel_id=1, source_target_pairs={{0,2},{1,3},{2,4},{3,5},{4,6},{5,7},{6,8},{7,9},{8,10},{9,11},{10,... | collective-permute-start | bytes 786440 | tf_op jit(solution)/shard_map/ppermute | solution.py:26
  11.1 42.8 %collective-permute-start.7 = (bf16[128,2,512]{0,2,1:T(8,128)(2,1)S(1)}, bf16[128,2,512]{0,2,1:T(8,128)(2,1)S(1)}, u32[]{:S(2)}, u32[]{:S(2)}) collective-permute-start(bf16[128,2,512]{0,2,1:T(8,128)(2,1)S(1)} %bitcast.153), channel_id=1, source_target_pairs={{0,3},{1,4},{2,5},{3,6},{4,7},{5,8},{6,9},{7,10},{8,11},{9,12},{10... | collective-permute-start | bytes 786440 | tf_op jit(solution)/shard_map/ppermute | solution.py:26
  15.7 32.2 %collective-permute-start.6 = (bf16[128,2,512]{0,2,1:T(8,128)(2,1)S(1)}, bf16[128,2,512]{0,2,1:T(8,128)(2,1)}, u32[]{:S(2)}, u32[]{:S(2)}) collective-permute-start(bf16[128,2,512]{0,2,1:T(8,128)(2,1)S(1)} %bitcast.154), channel_id=1, source_target_pairs={{0,4},{1,5},{2,6},{3,7},{4,8},{5,9},{6,10},{7,11},{8,12},{9,13},{1... | collective-permute-start | bytes 786440 | tf_op jit(solution)/shard_map/ppermute | solution.py:26
  23.7 30.1 %collective-permute-start = (bf16[1,128,2,512]{1,3,2,0:T(8,128)(2,1)}, bf16[1,128,2,512]{1,3,2,0:T(8,128)(2,1)}, u32[]{:S(2)}, u32[]{:S(2)}) collective-permute-start(bf16[1,128,2,512]{1,3,2,0:T(8,128)(2,1)} %copy.45), channel_id=1, source_target_pairs={{224,0},{0,32},{32,64},{64,96},{96,128},{128,160},{160,192},{192,2... | collective-permute-start | bytes 786440 | tf_op jit(solution)/shard_map/ppermute | solution.py:20
  47.9 82.4 %collective-permute-start.10 = (bf16[1,128,4096]{1,2,0:T(8,128)(2,1)}, bf16[1,128,4096]{1,2,0:T(8,128)(2,1)}, u32[]{:S(2)}, u32[]{:S(2)}) collective-permute-start(bf16[1,128,4096]{1,2,0:T(8,128)(2,1)} %copy.54), channel_id=1, source_target_pairs={{32,0},{64,32},{96,64},{128,96},{160,128},{192,160},{224,192},{0,2... | collective-permute-start | bytes 3145736 | tf_op jit(solution)/shard_map/ppermute | solution.py:20
  53.8 121.9 %collective-permute-start.5 = (bf16[1,128,4096]{2,1,0:T(8,128)(2,1)}, bf16[1,128,4096]{2,1,0:T(8,128)(2,1)}, u32[]{:S(2)}, u32[]{:S(2)}) collective-permute-start(bf16[1,128,4096]{2,1,0:T(8,128)(2,1)} %param.13), channel_id=1, source_target_pairs={{224,0},{0,32},{32,64},{64,96},{96,128},{128,160},{160,192},{192,2... | collective-permute-start | bytes 3145736 | tf_op jit(solution)/shard_map/ppermute | solution.py:20
  53.8 72.4 %collective-permute-start.3 = (bf16[128,2,512]{0,2,1:T(8,128)(2,1)}, bf16[128,2,512]{0,2,1:T(8,128)(2,1)}, u32[]{:S(2)}, u32[]{:S(2)}) collective-permute-start(bf16[128,2,512]{0,2,1:T(8,128)(2,1)} %bitcast.32), channel_id=1, source_target_pairs={{0,2},{1,3},{2,4},{3,5},{4,6},{5,7},{6,8},{7,9},{8,10},{9,11},{10,... | collective-permute-start | bytes 786440 | tf_op jit(solution)/shard_map/ppermute | solution.py:26
  56.5 52.9 %collective-permute-start.1 = (bf16[128,2,512]{0,2,1:T(8,128)(2,1)}, bf16[128,2,512]{0,2,1:T(8,128)(2,1)}, u32[]{:S(2)}, u32[]{:S(2)}) collective-permute-start(bf16[128,2,512]{0,2,1:T(8,128)(2,1)} %bitcast.32), channel_id=1, source_target_pairs={{0,4},{1,5},{2,6},{3,7},{4,8},{5,9},{6,10},{7,11},{8,12},{9,13},{1... | collective-permute-start | bytes 786440 | tf_op jit(solution)/shard_map/ppermute | solution.py:26
  62.4 62.1 %collective-permute-start.2 = (bf16[128,2,512]{0,2,1:T(8,128)(2,1)}, bf16[128,2,512]{0,2,1:T(8,128)(2,1)}, u32[]{:S(2)}, u32[]{:S(2)}) collective-permute-start(bf16[128,2,512]{0,2,1:T(8,128)(2,1)} %bitcast.32), channel_id=1, source_target_pairs={{0,3},{1,4},{2,5},{3,6},{4,7},{5,8},{6,9},{7,10},{8,11},{9,12},{10... | collective-permute-start | bytes 786440 | tf_op jit(solution)/shard_map/ppermute | solution.py:26
  85.0 1.6 copy-start.3
  87.2 4.2 %copy-start.4 = (bf16[640,2,4,128]{3,0,2,1:T(8,128)(2,1)S(1)}, bf16[640,2,4,128]{3,0,2,1:T(8,128)(2,1)}, u32[]{:S(2)}) copy-start(bf16[640,2,4,128]{3,0,2,1:T(8,128)(2,1)} %copy-done.3) | copy-start | bytes 3932164 | tf_op jit(solution)/shard_map/while/body/eval_jaxpr/cond
  96.6 1.3 copy-start
  109.4 18.5 %collective-permute-start.4 = (bf16[128,2,512]{0,2,1:T(8,128)(2,1)}, bf16[128,2,512]{0,2,1:T(8,128)(2,1)S(1)}, u32[]{:S(2)}, u32[]{:S(2)}) collective-permute-start(bf16[128,2,512]{0,2,1:T(8,128)(2,1)} %bitcast.32), channel_id=1, source_target_pairs={{0,1},{1,2},{2,3},{3,4},{4,5},{5,6},{6,7},{7,8},{8,9},{9,10},{10,1... | collective-permute-start | bytes 786440 | tf_op jit(solution)/shard_map/ppermute | solution.py:26
  138.2 3.8 %copy-start.1 = (bf16[640,2,4,128]{3,0,2,1:T(8,128)(2,1)S(1)}, bf16[640,2,4,128]{3,0,2,1:T(8,128)(2,1)}, u32[]{:S(2)}) copy-start(bf16[640,2,4,128]{3,0,2,1:T(8,128)(2,1)} %copy.56) | copy-start | bytes 3932164 | tf_op jit(solution)/shard_map/while/body/eval_jaxpr/cond
  162.6 35.0 %collective-permute-start.11 = (bf16[128,2,512]{2,1,0:T(2,128)(2,1)}, bf16[128,2,512]{2,1,0:T(2,128)(2,1)}, u32[]{:S(2)}, u32[]{:S(2)}) collective-permute-start(bf16[128,2,512]{2,1,0:T(2,128)(2,1)} %get-tuple-element.278), channel_id=1, source_target_pairs={{1,0},{2,1},{3,2},{4,3},{5,4},{6,5},{7,6},{8,7},{9,8},{10,9},{11,1... | collective-permute-start | bytes 786440 | tf_op jit(solution)/shard_map/ppermute | solution.py:26
  164.5 33.1 %collective-permute-start.14 = (bf16[128,2,512]{2,1,0:T(2,128)(2,1)}, bf16[128,2,512]{2,1,0:T(2,128)(2,1)}, u32[]{:S(2)}, u32[]{:S(2)}) collective-permute-start(bf16[128,2,512]{2,1,0:T(2,128)(2,1)} %get-tuple-element.279), channel_id=1, source_target_pairs={{4,0},{5,1},{6,2},{7,3},{8,4},{9,5},{10,6},{11,7},{12,8},{13,9},{1... | collective-permute-start | bytes 786440 | tf_op jit(solution)/shard_map/ppermute | solution.py:26
  166.4 39.7 %collective-permute-start.13 = (bf16[128,2,512]{2,1,0:T(2,128)(2,1)}, bf16[128,2,512]{2,1,0:T(2,128)(2,1)}, u32[]{:S(2)}, u32[]{:S(2)}) collective-permute-start(bf16[128,2,512]{2,1,0:T(2,128)(2,1)} %get-tuple-element.280), channel_id=1, source_target_pairs={{3,0},{4,1},{5,2},{6,3},{7,4},{8,5},{9,6},{10,7},{11,8},{12,9},{13... | collective-permute-start | bytes 786440 | tf_op jit(solution)/shard_map/ppermute | solution.py:26
  171.6 51.1 %collective-permute-start.12 = (bf16[128,2,512]{2,1,0:T(2,128)(2,1)}, bf16[128,2,512]{2,1,0:T(2,128)(2,1)}, u32[]{:S(2)}, u32[]{:S(2)}) collective-permute-start(bf16[128,2,512]{2,1,0:T(2,128)(2,1)} %get-tuple-element.281), channel_id=1, source_target_pairs={{2,0},{3,1},{4,2},{5,3},{6,4},{7,5},{8,6},{9,7},{10,8},{11,9},{12,... | collective-permute-start | bytes 786440 | tf_op jit(solution)/shard_map/ppermute | solution.py:26
  182.8 2.7 %copy-start.2 = (bf16[640,2,4,128]{3,0,2,1:T(8,128)(2,1)S(1)}, bf16[640,2,4,128]{3,0,2,1:T(8,128)(2,1)}, u32[]{:S(2)}) copy-start(bf16[640,2,4,128]{3,0,2,1:T(8,128)(2,1)} %copy.46) | copy-start | bytes 3932164 | tf_op jit(solution)/shard_map/while/body/eval_jaxpr/cond
where the time goes:
time: 227 us; the launch traced here: 225 us
  starting transfers between devices  80.3 us (35%)
  local copies, waits for them, and re-layouts  46.9 us (21%)
  waiting for transfers between devices  46.6 us (21%)
  matrix products  31.4 us (14%)
  other arithmetic  17.5 us (8%)
    ppermute x12, starting transfers between devices, passed_along_2(): return lax.ppermute(block, axis, route)  72.8 us
    ppermute x12, waiting for transfers between devices, passed_along_2(): return lax.ppermute(block, axis, route)  46.5 us
    unnamed x16, local copies, waits for them, and re-layouts  17.1 us
    dot_general x2, matrix products, update(): jnp.einsum('qmoe,eqx->qmox', exponent_weights.astype(jnp.bfloat16), keyva...  11.1 us
    another operation x8, local copies, waits for them, and re-layouts  9.68 us
    ppermute x3, starting transfers between devices, passed_along(): return lax.ppermute(block, axis, route)  7.49 us
    convert_element_type x2, local copies, waits for them, and re-layouts, rounded_output(): values.astype(jnp.bfloat16)  7.33 us
    dot_general x3, matrix products, block_scores(): jnp.einsum('wofu,aou->ofwa', query_heads_input, key_matrix, preferred_ele...  7.17 us
  transfers between devices with their start and end apart: 15, of which 4 were waited for; matrix products, arithmetic and copies ran while one was open for 40% of the time, Pallas kernels for 0%

commit v1 on v0

v1 whole, which is shorter than its diff:
```python
import math

import jax
import jax.numpy as jnp
from jax import lax
from jax.experimental import pallas as pl
from jax.experimental.pallas import tpu as pltpu
from jax.sharding import PartitionSpec as P

QUERY_HEADS = 32
KV_HEADS = 4
GROUP = QUERY_HEADS // KV_HEADS
WIDTH = 128
REACH = 4
ROW = 4
LOGIT_SCALE = 1.0 / math.sqrt(WIDTH)
EXP2_SCALE = LOGIT_SCALE * math.log2(math.e)
MASKED = -1e30
CHUNK_HEADS = 2

SMEM = pl.BlockSpec(memory_space=pltpu.SMEM)


def along_section(block, distance):
    size = lax.axis_size("section")
    return lax.ppermute(
        block, "section", [(i, (i + distance) % size) for i in range(size)]
    )


def across_rows(block, distance):
    size = lax.axis_size("ctx")
    return lax.ppermute(
        block,
        "ctx",
        [(i, i + distance) for i in range(size) if 0 <= i + distance < size],
    )


def across_rows_and_section(block, distance):
    sections, size = lax.axis_size("section"), lax.axis_size("ctx")
    route = [
        (s * size + c, (s + 1) % sections * size + c + distance)
        for s in range(sections)
        for c in range(size)
        if 0 <= c + distance < size
    ]
    return lax.ppermute(block, ("section", "ctx"), route)


def in_row(block, distance):
    size = lax.axis_size("ctx")
    return lax.ppermute(
        block,
        "ctx",
        [(c, c // ROW * ROW + (c + distance) % ROW) for c in range(size)],
    )


def after(values, earlier):
    return lax.optimization_barrier((values, earlier))[0]


def nt_dot(a, b):
    return lax.dot_general(a, b, (((1,), (1,)), ((), ())), preferred_element_type=jnp.float32)


def nn_dot(a, b):
    return jnp.dot(a, b, preferred_element_type=jnp.float32)


def write_bias(lengths_ref, bias_ref):
    tokens = bias_ref.shape[1]
    first_row = lax.axis_index("ctx") * tokens
    query = first_row + lax.broadcasted_iota(jnp.int32, (1, tokens), 1)
    start = jnp.zeros((1, tokens), jnp.int32)
    end = jnp.int32(0)
    for k in range(lengths_ref.shape[1]):
        end = end + lengths_ref[0, k]
        start = jnp.where(query >= end, end, start)
    for b in range(REACH + 1):
        key = (
            first_row
            + (b - REACH) * tokens
            + lax.broadcasted_iota(jnp.int32, (tokens, tokens), 0)
        )
        allowed = (key >= start) & (key <= query)
        bias_ref[b * tokens : (b + 1) * tokens, :] = jnp.where(allowed, 0.0, MASKED)


def head_rows(ref, first, count):
    return jnp.concatenate(
        [ref[:, h * WIDTH : (h + 1) * WIDTH] for h in range(first, first + count)], axis=0
    )


def window(block_refs, index):
    return jnp.concatenate([ref[index] for ref in block_refs], axis=0)


def exponentials(keys, queries, bias_ref):
    scores = nt_dot(keys, queries) * EXP2_SCALE + jnp.concatenate(
        [bias_ref[...]] * CHUNK_HEADS, axis=1
    )
    return jnp.exp2(scores - jnp.max(scores, axis=0, keepdims=True))


def forward_kernel(lengths_ref, q_ref, *refs):
    block_refs, (out_ref, bias_ref) = refs[: REACH + 1], refs[REACH + 1 :]

    @pl.when(pl.program_id(0) == 0)
    def _():
        write_bias(lengths_ref, bias_ref)

    keys = window(block_refs, 0)
    values_t = window(block_refs, 1).T
    for first in range(0, GROUP, CHUNK_HEADS):
        e = exponentials(keys, head_rows(q_ref, first, CHUNK_HEADS), bias_ref)
        total = jnp.sum(e, axis=0, keepdims=True)
        out_t = nn_dot(values_t, e.astype(jnp.bfloat16)) / total
        for k in range(CHUNK_HEADS):
            at = (first + k) * WIDTH
            out_ref[:, at : at + WIDTH] = out_t[:, k * WIDTH : (k + 1) * WIDTH].T.astype(
                jnp.bfloat16
            )


def backward_kernel(lengths_ref, q_ref, g_ref, *refs):
    block_refs, refs = refs[: REACH + 1], refs[REACH + 1 :]
    dq_ref, refs = refs[0], refs[1:]
    grad_refs, (bias_ref, p_ref, ds_ref) = refs[: REACH + 1], refs[REACH + 1 :]
    tokens = q_ref.shape[0]

    @pl.when(pl.program_id(0) == 0)
    def _():
        write_bias(lengths_ref, bias_ref)

    keys = window(block_refs, 0)
    values = window(block_refs, 1)
    keys_t = keys.T
    for first in range(0, GROUP, CHUNK_HEADS):
        lanes = slice(first * tokens, (first + CHUNK_HEADS) * tokens)
        e = exponentials(keys, head_rows(q_ref, first, CHUNK_HEADS), bias_ref)
        prob_grad = nt_dot(values, head_rows(g_ref, first, CHUNK_HEADS))
        inverse = 1.0 / jnp.sum(e, axis=0, keepdims=True)
        delta = jnp.sum(e * prob_grad, axis=0, keepdims=True) * inverse
        probs = e * inverse
        p_ref[:, lanes] = probs.astype(jnp.bfloat16)
        score_grad = (probs * (prob_grad - delta)).astype(jnp.bfloat16)
        ds_ref[:, lanes] = score_grad
        dq_t = nn_dot(keys_t, score_grad) * LOGIT_SCALE
        for k in range(CHUNK_HEADS):
            at = (first + k) * WIDTH
            dq_ref[:, at : at + WIDTH] = dq_t[:, k * WIDTH : (k + 1) * WIDTH].T.astype(
                jnp.bfloat16
            )
    value_grad = nn_dot(p_ref[...], head_rows(g_ref, 0, GROUP))
    key_grad = nn_dot(ds_ref[...], head_rows(q_ref, 0, GROUP)) * LOGIT_SCALE
    for b, ref in enumerate(grad_refs):
        rows = slice(b * tokens, (b + 1) * tokens)
        ref[0] = key_grad[rows].astype(ref.dtype)
        ref[1] = value_grad[rows].astype(ref.dtype)


def specs(tokens):
    group_cols = pl.BlockSpec((tokens, GROUP * WIDTH), lambda g: (0, g))
    pair = pl.BlockSpec((2, tokens, WIDTH), lambda g: (0, 0, g))
    return group_cols, pair


def forward(lengths, queries, blocks):
    tokens, width = queries.shape
    group_cols, pair = specs(tokens)
    keys = (REACH + 1) * tokens
    return pl.pallas_call(
        forward_kernel,
        grid=(KV_HEADS,),
        in_specs=[SMEM, group_cols] + [pair] * len(blocks),
        out_specs=group_cols,
        out_shape=jax.ShapeDtypeStruct((tokens, width), jnp.bfloat16),
        scratch_shapes=[pltpu.VMEM((keys, tokens), jnp.float32)],
        compiler_params=pltpu.CompilerParams(vmem_limit_bytes=40 * 1024 * 1024),
        cost_estimate=pl.CostEstimate(
            flops=4 * tokens * keys * width, bytes_accessed=4 << 20, transcendentals=0
        ),
        name="forward",
    )(lengths, queries, *blocks)


def backward(lengths, queries, grads, blocks):
    tokens, width = queries.shape
    group_cols, pair = specs(tokens)
    keys = (REACH + 1) * tokens
    kinds = [jnp.float32] + [jnp.bfloat16] * (REACH - 1) + [jnp.float32]
    return pl.pallas_call(
        backward_kernel,
        grid=(KV_HEADS,),
        in_specs=[SMEM, group_cols, group_cols] + [pair] * len(blocks),
        out_specs=[group_cols] + [pair] * len(blocks),
        out_shape=[jax.ShapeDtypeStruct((tokens, width), jnp.bfloat16)]
        + [jax.ShapeDtypeStruct(blocks[0].shape, kind) for kind in kinds],
        scratch_shapes=[
            pltpu.VMEM((keys, tokens), jnp.float32),
            pltpu.VMEM((keys, GROUP * tokens), jnp.bfloat16),
            pltpu.VMEM((keys, GROUP * tokens), jnp.bfloat16),
        ],
        compiler_params=pltpu.CompilerParams(vmem_limit_bytes=40 * 1024 * 1024),
        cost_estimate=pl.CostEstimate(
            flops=10 * tokens * keys * width, bytes_accessed=8 << 20, transcendentals=0
        ),
        name="backward",
    )(lengths, queries, grads, *blocks)


def gather_window(own, previous):
    place = lax.axis_index("ctx") % ROW
    blocks = [own]
    for distance in range(1, ROW):
        sent = jnp.where(place + distance < ROW, own, previous)
        blocks.insert(0, in_row(sent, distance))
    return [previous] + blocks


def return_terms(terms):
    place = lax.axis_index("ctx") % ROW
    previous, own = terms[0], terms[REACH]
    for distance in range(1, ROW):
        back = in_row(terms[REACH - distance], -distance).astype(jnp.float32)
        here = place + distance < ROW
        own = own + jnp.where(here, back, 0.0)
        previous = previous + jnp.where(here, 0.0, back)
    crossed = across_rows(previous.astype(jnp.bfloat16), -ROW)
    return own, crossed


def body(
    sent_queries,
    sent_keyvals,
    forward_lengths,
    kept_queries,
    kept_keyvals,
    sent_grad,
    backward_lengths,
):
    kept = kept_keyvals[0].transpose(1, 0, 2)
    kept_previous = across_rows(kept, ROW)
    grads = along_section(sent_grad[0], -1)
    sent = sent_keyvals[0].transpose(1, 0, 2)
    sent, queries = after((sent, sent_queries[0]), kept_previous)
    arrived_previous = across_rows_and_section(sent, ROW)
    arrived = along_section(sent, 1)
    arrived_queries = along_section(queries, 1)

    kept_window = gather_window(kept, kept_previous)
    results = backward(backward_lengths, kept_queries[0], grads, kept_window)
    own, crossed = return_terms(results[1:])

    attention_out = forward(
        forward_lengths, arrived_queries, gather_window(arrived, arrived_previous)
    )
    keyval_grad = (own + crossed.astype(jnp.float32)).astype(jnp.bfloat16).transpose(1, 0, 2)
    return attention_out[None], results[0][None], keyval_grad[None]


def solution(mesh):
    placed = (
        P("section", "ctx", None),
        P("section", "ctx", None, None),
        P("section", None),
        P("section", "ctx", None),
        P("section", "ctx", None, None),
        P("section", "ctx", None),
        P("section", None),
    )
    return jax.shard_map(
        body,
        mesh=mesh,
        in_specs=placed,
        out_specs=(
            P("section", "ctx", None),
            P("section", "ctx", None),
            P("section", "ctx", None, None),
        ),
        check_vma=False,
    )
```

time: 227 us -> 102 us (0.45)
  the two profiles are of different devices: /device:TPU:109 before, /device:TPU:56 now
where the time goes in v1:
time: 102 us; the launch traced here: 101 us
  starting transfers between devices  42.3 us (41%)
  waiting for transfers between devices  31.3 us (31%)
  Pallas kernels  24.3 us (24%)
  local copies, waits for them, and re-layouts  2.01 us (2%)
    ppermute x9, starting transfers between devices, in_row(): lax.ppermute(block, 'ctx', [(c, c // ROW * ROW + (c + distance) % ROW) fo...  18.7 us
    ppermute x2, waiting for transfers between devices, across_rows(): lax.ppermute(block, 'ctx', [(i, i + distance) for i in range(size) if 0 <...  18.5 us
    ppermute x2, starting transfers between devices, across_rows(): lax.ppermute(block, 'ctx', [(i, i + distance) for i in range(size) if 0 <...  14.1 us
    pallas_call x1, Pallas kernels, backward(): pl.pallas_call(backward_kernel, grid=(KV_HEADS,), in_specs=[SMEM, group_c...  14 us
    ppermute x9, waiting for transfers between devices, in_row(): lax.ppermute(block, 'ctx', [(c, c // ROW * ROW + (c + distance) % ROW) fo...  12.8 us
    pallas_call x1, Pallas kernels, forward(): pl.pallas_call(forward_kernel, grid=(KV_HEADS,), in_specs=[SMEM, group_co...  10.3 us
    ppermute x1, starting transfers between devices, across_rows_and_section(): return lax.ppermute(block, ('section', 'ctx'), route)  6.11 us
    ppermute x3, starting transfers between devices, along_section(): lax.ppermute(block, 'section', [(i, (i + distance) % size) for i in range...  3.45 us
  transfers between devices with their start and end apart: 15, of which 6 were waited for; matrix products, arithmetic and copies ran while one was open for 1% of the time, Pallas kernels for 24%

profile of v1, /device:TPU:56, one launch (start us, length us, event | category | flops | bytes accessed | tf_op | source)
XLA Modules:
  0.0 101.2 jit_solution(7039255148707042400)
XLA Ops:
  0.7 1.0 copy.21
  1.7 8.8 %collective-permute-start = (bf16[2,128,512]{2,1,0:T(8,128)(2,1)S(1)}, bf16[2,128,512]{2,1,0:T(8,128)(2,1)S(1)}, u32[]{:S(2)}, u32[]{:S(2)}) collective-permute-start(bf16[2,128,512]{2,1,0:T(8,128)(2,1)S(1)} %bitcast.25), channel_id=1, source_target_pairs={{0,4},{1,5},{2,6},{3,7},{4,8},{5,9},{6,10},{7,11},{8,12},{9,13},{1... | collective-permute-start | bytes 786440 | tf_op jit(solution)/shard_map/ppermute | solution.py:33
  10.5 18.5 %collective-permute-done.refs_0_ = bf16[2,128,512]{2,1,0:T(8,128)(2,1)S(1)} collective-permute-done((bf16[2,128,512]{2,1,0:T(8,128)(2,1)S(1)}, bf16[2,128,512]{2,1,0:T(8,128)(2,1)S(1)}, u32[]{:S(2)}, u32[]{:S(2)}) %collective-permute-start) | collective-permute-done | bytes 262176 | tf_op jit(solution)/shard_map/ppermute | solution.py:33
  29.1 1.6 %collective-permute-start.10 = (bf16[2,128,512]{2,1,0:T(8,128)(2,1)S(1)}, bf16[2,128,512]{2,1,0:T(8,128)(2,1)S(1)}, u32[]{:S(2)}, u32[]{:S(2)}) collective-permute-start(bf16[2,128,512]{2,1,0:T(8,128)(2,1)S(1)} %get-tuple-element.22), channel_id=1, source_target_pairs={{0,1},{1,2},{2,3},{3,0},{4,5},{5,6},{6,7},{7,4},{8,9},{9,10},{10,1... | collective-permute-start | bytes 786440 | tf_op jit(solution)/shard_map/ppermute | solution.py:53
  30.7 1.7 %collective-permute-start.8 = (bf16[2,128,512]{2,1,0:T(8,128)(2,1)S(1)}, bf16[2,128,512]{2,1,0:T(8,128)(2,1)S(1)}, u32[]{:S(2)}, u32[]{:S(2)}) collective-permute-start(bf16[2,128,512]{2,1,0:T(8,128)(2,1)S(1)} %get-tuple-element.24), channel_id=1, source_target_pairs={{0,3},{1,0},{2,1},{3,2},{4,7},{5,4},{6,5},{7,6},{8,11},{9,8},{10,9... | collective-permute-start | bytes 786440 | tf_op jit(solution)/shard_map/ppermute | solution.py:53
  32.4 1.8 %collective-permute-start.9 = (bf16[2,128,512]{2,1,0:T(8,128)(2,1)S(1)}, bf16[2,128,512]{2,1,0:T(8,128)(2,1)S(1)}, u32[]{:S(2)}, u32[]{:S(2)}) collective-permute-start(bf16[2,128,512]{2,1,0:T(8,128)(2,1)S(1)} %get-tuple-element.23), channel_id=1, source_target_pairs={{0,2},{1,3},{2,0},{3,1},{4,6},{5,7},{6,4},{7,5},{8,10},{9,11},{10,... | collective-permute-start | bytes 786440 | tf_op jit(solution)/shard_map/ppermute | solution.py:53
  34.4 2.4 %collective-permute-done.10.refs_3_ = bf16[2,128,512]{2,1,0:T(8,128)(2,1)S(1)} collective-permute-done((bf16[2,128,512]{2,1,0:T(8,128)(2,1)S(1)}, bf16[2,128,512]{2,1,0:T(8,128)(2,1)S(1)}, u32[]{:S(2)}, u32[]{:S(2)}) %collective-permute-start.10) | collective-permute-done | bytes 262176 | tf_op jit(solution)/shard_map/ppermute | solution.py:53
  36.8 6.1 %collective-permute-start.2 = (bf16[2,128,512]{2,1,0:T(8,128)(2,1)S(1)}, bf16[2,128,512]{2,1,0:T(8,128)(2,1)S(1)}, u32[]{:S(2)}, u32[]{:S(2)}) collective-permute-start(bf16[2,128,512]{2,1,0:T(8,128)(2,1)S(1)} %bitcast.28), channel_id=1, source_target_pairs={{0,36},{1,37},{2,38},{3,39},{4,40},{5,41},{6,42},{7,43},{8,44},{9,... | collective-permute-start | bytes 786440 | tf_op jit(solution)/shard_map/ppermute | solution.py:48
  42.9 3.3 %collective-permute-start.3 = (bf16[2,128,512]{2,1,0:T(8,128)(2,1)S(1)}, bf16[2,128,512]{2,1,0:T(8,128)(2,1)S(1)}, u32[]{:S(2)}, u32[]{:S(2)}) collective-permute-start(bf16[2,128,512]{2,1,0:T(8,128)(2,1)S(1)} %bitcast.29), channel_id=1, source_target_pairs={{0,32},{32,64},{64,96},{96,128},{128,160},{160,192},{192,224},{224... | collective-permute-start | bytes 786440 | tf_op jit(solution)/shard_map/ppermute | solution.py:26
  46.2 14.0 %backward.1 = (bf16[128,4096]{1,0:T(8,128)(2,1)}, f32[2,128,512]{2,1,0:T(8,128)S(1)}, bf16[2,128,512]{2,1,0:T(8,128)(2,1)S(1)}, bf16[2,128,512]{2,1,0:T(8,128)(2...) custom-call(s32[1,16]{1,0:T(1,128)S(1)} %copy-done.1, bf16[128,4096]{1,0:T(8,128)(2,1)S(1)} %bitcast.27, ...), custom_call_target="tpu_custom_call" | custom-call | flops 3355443200 | bytes 8388608 | tf_op jit(solution)/shard_map/backward/pallas_call | solution.py:195
  60.2 2.5 %collective-permute-start.11 = (bf16[2,128,512]{2,1,0:T(8,128)(2,1)S(1)}, bf16[2,128,512]{2,1,0:T(8,128)(2,1)S(1)}, u32[]{:S(2)}, u32[]{:S(2)}) collective-permute-start(bf16[2,128,512]{2,1,0:T(8,128)(2,1)S(1)} %get-tuple-element.15), channel_id=1, source_target_pairs={{0,3},{1,0},{2,1},{3,2},{4,7},{5,4},{6,5},{7,6},{8,11},{9,8},{10,9... | collective-permute-start | bytes 786440 | tf_op jit(solution)/shard_map/ppermute | solution.py:53
  62.7 0.8 collective-permute-start.12
  63.5 0.9 collective-permute-start.13
  64.4 2.4 %collective-permute-start.4 = (bf16[2,128,512]{2,1,0:T(8,128)(2,1)S(1)}, bf16[2,128,512]{2,1,0:T(8,128)(2,1)S(1)}, u32[]{:S(2)}, u32[]{:S(2)}) collective-permute-start(bf16[2,128,512]{2,1,0:T(8,128)(2,1)S(1)} %get-tuple-element.27), channel_id=1, source_target_pairs={{0,3},{1,0},{2,1},{3,2},{4,7},{5,4},{6,5},{7,6},{8,11},{9,8},{10,9... | collective-permute-start | bytes 786440 | tf_op jit(solution)/shard_map/ppermute | solution.py:53
  66.8 0.3 collective-permute-done.11
  67.1 3.3 %collective-permute-start.5 = (bf16[2,128,512]{2,1,0:T(8,128)(2,1)S(1)}, bf16[2,128,512]{2,1,0:T(8,128)(2,1)S(1)}, u32[]{:S(2)}, u32[]{:S(2)}) collective-permute-start(bf16[2,128,512]{2,1,0:T(8,128)(2,1)S(1)} %get-tuple-element.26), channel_id=1, source_target_pairs={{0,2},{1,3},{2,0},{3,1},{4,6},{5,7},{6,4},{7,5},{8,10},{9,11},{10,... | collective-permute-start | bytes 786440 | tf_op jit(solution)/shard_map/ppermute | solution.py:53
  70.5 0.2 collective-permute-done.12
  70.6 3.6 %collective-permute-start.6 = (bf16[2,128,512]{2,1,0:T(8,128)(2,1)S(1)}, bf16[2,128,512]{2,1,0:T(8,128)(2,1)S(1)}, u32[]{:S(2)}, u32[]{:S(2)}) collective-permute-start(bf16[2,128,512]{2,1,0:T(8,128)(2,1)S(1)} %get-tuple-element.25), channel_id=1, source_target_pairs={{0,1},{1,2},{2,3},{3,0},{4,5},{5,6},{6,7},{7,4},{8,9},{9,10},{10,1... | collective-permute-start | bytes 786440 | tf_op jit(solution)/shard_map/ppermute | solution.py:53
  74.2 7.4 %collective-permute-done.13 = bf16[2,128,512]{2,1,0:T(8,128)(2,1)S(1)} collective-permute-done((bf16[2,128,512]{2,1,0:T(8,128)(2,1)S(1)}, bf16[2,128,512]{2,1,0:T(8,128)(2,1)S(1)}, u32[]{:S(2)}, u32[]{:S(2)}) %collective-permute-start.13) | collective-permute-done | bytes 262176 | tf_op jit(solution)/shard_map/ppermute | solution.py:53
  81.9 5.3 %collective-permute-start.14 = (bf16[2,128,512]{2,1,0:T(8,128)(2,1)S(1)}, bf16[2,128,512]{2,1,0:T(8,128)(2,1)S(1)}, u32[]{:S(2)}, u32[]{:S(2)}) collective-permute-start(bf16[2,128,512]{2,1,0:T(8,128)(2,1)S(1)} %fusion.8), channel_id=1, source_target_pairs={{4,0},{5,1},{6,2},{7,3},{8,4},{9,5},{10,6},{11,7},{12,8},{13,9},{1... | collective-permute-start | bytes 786440 | tf_op jit(solution)/shard_map/ppermute | solution.py:33
  87.2 2.5 %collective-permute-done.6.refs_3_ = bf16[2,128,512]{2,1,0:T(8,128)(2,1)S(1)} collective-permute-done((bf16[2,128,512]{2,1,0:T(8,128)(2,1)S(1)}, bf16[2,128,512]{2,1,0:T(8,128)(2,1)S(1)}, u32[]{:S(2)}, u32[]{:S(2)}) %collective-permute-start.6) | collective-permute-done | bytes 262176 | tf_op jit(solution)/shard_map/ppermute | solution.py:53
  89.7 10.3 %forward.1 = bf16[128,4096]{1,0:T(8,128)(2,1)} custom-call(s32[1,16]{1,0:T(1,128)S(1)} %copy-done.2, bf16[128,4096]{1,0:T(8,128)(2,1)S(1)} %collective-permute-done.1.q_ref, bf16[2,128,512]{2,1,0:T(8,128)(2,1)S(1)} %collective-permute-done.2.refs_0_, bf16[2,128,512]{2,1,0:T(8,128)(2,1)S(1)} %collective-permute-done.4.refs_1_, ...), custom_call_target="tpu_custom_call" | custom-call | flops 1342177280 | bytes 4194304 | tf_op jit(solution)/shard_map/forward/pallas_call | solution.py:175
  100.0 0.2 fusion.9
  100.2 1.0 copy.12
  (25 shorter events, 0.5 us)
Async XLA Ops:
  0.6 28.4 %copy-start.3 = (bf16[1,128,2,512]{3,2,1,0:T(2,128)(2,1)S(1)}, bf16[1,128,2,512]{3,2,1,0:T(2,128)(2,1)}, u32[]{:S(2)}) copy-start(bf16[1,128,2,512]{3,2,1,0:T(2,128)(2,1)} %param.11) | copy-start | bytes 786436
  0.6 45.5 %collective-permute-start.7 = (bf16[128,4096]{1,0:T(8,128)(2,1)}, bf16[128,4096]{1,0:T(8,128)(2,1)S(1)}, u32[]{:S(2)}, u32[]{:S(2)}) collective-permute-start(bf16[128,4096]{1,0:T(8,128)(2,1)} %bitcast.30), channel_id=1, source_target_pairs={{0,224},{32,0},{64,32},{96,64},{128,96},{160,128},{192,160},{224,1... | collective-permute-start | bytes 3145736 | tf_op jit(solution)/shard_map/ppermute | solution.py:26
  1.7 44.5 %copy-start = (bf16[1,128,4096]{2,1,0:T(8,128)(2,1)S(1)}, bf16[1,128,4096]{2,1,0:T(8,128)(2,1)}, u32[]{:S(2)}) copy-start(bf16[1,128,4096]{2,1,0:T(8,128)(2,1)} %param.10) | copy-start | bytes 3145732
  1.7 27.3 %collective-permute-start = (bf16[2,128,512]{2,1,0:T(8,128)(2,1)S(1)}, bf16[2,128,512]{2,1,0:T(8,128)(2,1)S(1)}, u32[]{:S(2)}, u32[]{:S(2)}) collective-permute-start(bf16[2,128,512]{2,1,0:T(8,128)(2,1)S(1)} %bitcast.25), channel_id=1, source_target_pairs={{0,4},{1,5},{2,6},{3,7},{4,8},{5,9},{6,10},{7,11},{8,12},{9,13},{1... | collective-permute-start | bytes 786440 | tf_op jit(solution)/shard_map/ppermute | solution.py:33
  10.5 23.7 %copy-start.4 = (bf16[1,128,2,512]{3,2,1,0:T(2,128)(2,1)S(1)}, bf16[1,128,2,512]{3,2,1,0:T(2,128)(2,1)}, u32[]{:S(2)}) copy-start(bf16[1,128,2,512]{3,2,1,0:T(2,128)(2,1)} %param.8) | copy-start | bytes 786436
  29.1 7.7 %collective-permute-start.10 = (bf16[2,128,512]{2,1,0:T(8,128)(2,1)S(1)}, bf16[2,128,512]{2,1,0:T(8,128)(2,1)S(1)}, u32[]{:S(2)}, u32[]{:S(2)}) collective-permute-start(bf16[2,128,512]{2,1,0:T(8,128)(2,1)S(1)} %get-tuple-element.22), channel_id=1, source_target_pairs={{0,1},{1,2},{2,3},{3,0},{4,5},{5,6},{6,7},{7,4},{8,9},{9,10},{10,1... | collective-permute-start | bytes 786440 | tf_op jit(solution)/shard_map/ppermute | solution.py:53
  30.7 12.2 %collective-permute-start.8 = (bf16[2,128,512]{2,1,0:T(8,128)(2,1)S(1)}, bf16[2,128,512]{2,1,0:T(8,128)(2,1)S(1)}, u32[]{:S(2)}, u32[]{:S(2)}) collective-permute-start(bf16[2,128,512]{2,1,0:T(8,128)(2,1)S(1)} %get-tuple-element.24), channel_id=1, source_target_pairs={{0,3},{1,0},{2,1},{3,2},{4,7},{5,4},{6,5},{7,6},{8,11},{9,8},{10,9... | collective-permute-start | bytes 786440 | tf_op jit(solution)/shard_map/ppermute | solution.py:53
  32.4 13.8 %collective-permute-start.9 = (bf16[2,128,512]{2,1,0:T(8,128)(2,1)S(1)}, bf16[2,128,512]{2,1,0:T(8,128)(2,1)S(1)}, u32[]{:S(2)}, u32[]{:S(2)}) collective-permute-start(bf16[2,128,512]{2,1,0:T(8,128)(2,1)S(1)} %get-tuple-element.23), channel_id=1, source_target_pairs={{0,2},{1,3},{2,0},{3,1},{4,6},{5,7},{6,4},{7,5},{8,10},{9,11},{10,... | collective-permute-start | bytes 786440 | tf_op jit(solution)/shard_map/ppermute | solution.py:53
  34.3 11.9 %copy-start.1 = (s32[1,16]{1,0:T(1,128)S(1)}, s32[1,16]{1,0:T(1,128)}, u32[]{:S(2)}) copy-start(s32[1,16]{1,0:T(1,128)} %lengths_ref.3) | copy-start | bytes 196
  34.3 55.4 %collective-permute-start.1 = (bf16[128,4096]{1,0:T(8,128)(2,1)}, bf16[128,4096]{1,0:T(8,128)(2,1)S(1)}, u32[]{:S(2)}, u32[]{:S(2)}) collective-permute-start(bf16[128,4096]{1,0:T(8,128)(2,1)} %bitcast.31), channel_id=1, source_target_pairs={{0,32},{32,64},{64,96},{96,128},{128,160},{160,192},{192,224},{224... | collective-permute-start | bytes 3145736 | tf_op jit(solution)/shard_map/ppermute | solution.py:26
  36.8 26.7 %collective-permute-start.2 = (bf16[2,128,512]{2,1,0:T(8,128)(2,1)S(1)}, bf16[2,128,512]{2,1,0:T(8,128)(2,1)S(1)}, u32[]{:S(2)}, u32[]{:S(2)}) collective-permute-start(bf16[2,128,512]{2,1,0:T(8,128)(2,1)S(1)} %bitcast.28), channel_id=1, source_target_pairs={{0,36},{1,37},{2,38},{3,39},{4,40},{5,41},{6,42},{7,43},{8,44},{9,... | collective-permute-start | bytes 786440 | tf_op jit(solution)/shard_map/ppermute | solution.py:48
  42.9 21.5 %collective-permute-start.3 = (bf16[2,128,512]{2,1,0:T(8,128)(2,1)S(1)}, bf16[2,128,512]{2,1,0:T(8,128)(2,1)S(1)}, u32[]{:S(2)}, u32[]{:S(2)}) collective-permute-start(bf16[2,128,512]{2,1,0:T(8,128)(2,1)S(1)} %bitcast.29), channel_id=1, source_target_pairs={{0,32},{32,64},{64,96},{96,128},{128,160},{160,192},{192,224},{224... | collective-permute-start | bytes 786440 | tf_op jit(solution)/shard_map/ppermute | solution.py:26
  60.2 6.9 %collective-permute-start.11 = (bf16[2,128,512]{2,1,0:T(8,128)(2,1)S(1)}, bf16[2,128,512]{2,1,0:T(8,128)(2,1)S(1)}, u32[]{:S(2)}, u32[]{:S(2)}) collective-permute-start(bf16[2,128,512]{2,1,0:T(8,128)(2,1)S(1)} %get-tuple-element.15), channel_id=1, source_target_pairs={{0,3},{1,0},{2,1},{3,2},{4,7},{5,4},{6,5},{7,6},{8,11},{9,8},{10,9... | collective-permute-start | bytes 786440 | tf_op jit(solution)/shard_map/ppermute | solution.py:53
  62.7 8.0 %collective-permute-start.12 = (bf16[2,128,512]{2,1,0:T(8,128)(2,1)S(1)}, bf16[2,128,512]{2,1,0:T(8,128)(2,1)S(1)}, u32[]{:S(2)}, u32[]{:S(2)}) collective-permute-start(bf16[2,128,512]{2,1,0:T(8,128)(2,1)S(1)} %get-tuple-element.16), channel_id=1, source_target_pairs={{0,2},{1,3},{2,0},{3,1},{4,6},{5,7},{6,4},{7,5},{8,10},{9,11},{10,... | collective-permute-start | bytes 786440 | tf_op jit(solution)/shard_map/ppermute | solution.py:53
  63.5 18.2 %collective-permute-start.13 = (bf16[2,128,512]{2,1,0:T(8,128)(2,1)S(1)}, bf16[2,128,512]{2,1,0:T(8,128)(2,1)S(1)}, u32[]{:S(2)}, u32[]{:S(2)}) collective-permute-start(bf16[2,128,512]{2,1,0:T(8,128)(2,1)S(1)} %get-tuple-element.17), channel_id=1, source_target_pairs={{0,1},{1,2},{2,3},{3,0},{4,5},{5,6},{6,7},{7,4},{8,9},{9,10},{10,1... | collective-permute-start | bytes 786440 | tf_op jit(solution)/shard_map/ppermute | solution.py:53
  64.4 22.7 %collective-permute-start.4 = (bf16[2,128,512]{2,1,0:T(8,128)(2,1)S(1)}, bf16[2,128,512]{2,1,0:T(8,128)(2,1)S(1)}, u32[]{:S(2)}, u32[]{:S(2)}) collective-permute-start(bf16[2,128,512]{2,1,0:T(8,128)(2,1)S(1)} %get-tuple-element.27), channel_id=1, source_target_pairs={{0,3},{1,0},{2,1},{3,2},{4,7},{5,4},{6,5},{7,6},{8,11},{9,8},{10,9... | collective-permute-start | bytes 786440 | tf_op jit(solution)/shard_map/ppermute | solution.py:53
  67.1 20.1 %collective-permute-start.5 = (bf16[2,128,512]{2,1,0:T(8,128)(2,1)S(1)}, bf16[2,128,512]{2,1,0:T(8,128)(2,1)S(1)}, u32[]{:S(2)}, u32[]{:S(2)}) collective-permute-start(bf16[2,128,512]{2,1,0:T(8,128)(2,1)S(1)} %get-tuple-element.26), channel_id=1, source_target_pairs={{0,2},{1,3},{2,0},{3,1},{4,6},{5,7},{6,4},{7,5},{8,10},{9,11},{10,... | collective-permute-start | bytes 786440 | tf_op jit(solution)/shard_map/ppermute | solution.py:53
  70.6 19.1 %collective-permute-start.6 = (bf16[2,128,512]{2,1,0:T(8,128)(2,1)S(1)}, bf16[2,128,512]{2,1,0:T(8,128)(2,1)S(1)}, u32[]{:S(2)}, u32[]{:S(2)}) collective-permute-start(bf16[2,128,512]{2,1,0:T(8,128)(2,1)S(1)} %get-tuple-element.25), channel_id=1, source_target_pairs={{0,1},{1,2},{2,3},{3,0},{4,5},{5,6},{6,7},{7,4},{8,9},{9,10},{10,1... | collective-permute-start | bytes 786440 | tf_op jit(solution)/shard_map/ppermute | solution.py:53
  81.7 8.0 %copy-start.2 = (s32[1,16]{1,0:T(1,128)S(1)}, s32[1,16]{1,0:T(1,128)}, u32[]{:S(2)}) copy-start(s32[1,16]{1,0:T(1,128)} %lengths_ref.2) | copy-start | bytes 196
  81.9 18.2 %collective-permute-start.14 = (bf16[2,128,512]{2,1,0:T(8,128)(2,1)S(1)}, bf16[2,128,512]{2,1,0:T(8,128)(2,1)S(1)}, u32[]{:S(2)}, u32[]{:S(2)}) collective-permute-start(bf16[2,128,512]{2,1,0:T(8,128)(2,1)S(1)} %fusion.8), channel_id=1, source_target_pairs={{4,0},{5,1},{6,2},{7,3},{8,4},{9,5},{10,6},{11,7},{12,8},{13,9},{1... | collective-permute-start | bytes 786440 | tf_op jit(solution)/shard_map/ppermute | solution.py:33

commit v2 on v1

--- a/solution.py
+++ b/solution.py
@@ -16,7 +16,7 @@
 LOGIT_SCALE = 1.0 / math.sqrt(WIDTH)
 EXP2_SCALE = LOGIT_SCALE * math.log2(math.e)
 MASKED = -1e30
-CHUNK_HEADS = 2
+CHUNK_HEADS = 8
 
 SMEM = pl.BlockSpec(memory_space=pltpu.SMEM)
 
@@ -212,18 +212,19 @@
     )(lengths, queries, grads, *blocks)
 
 
-def gather_window(own, previous):
+def window_sends(own, previous):
     place = lax.axis_index("ctx") % ROW
-    blocks = [own]
-    for distance in range(1, ROW):
-        sent = jnp.where(place + distance < ROW, own, previous)
-        blocks.insert(0, in_row(sent, distance))
-    return [previous] + blocks
-
-
-def return_terms(terms):
+    return [jnp.where(place + d < ROW, own, previous) for d in range(1, ROW)]
+
+
+def gather_window(own, previous, sends):
+    moved = [in_row(sent, d) for d, sent in enumerate(sends, 1)]
+    return [previous] + moved[::-1] + [own]
+
+
+def return_terms(terms, earlier):
     place = lax.axis_index("ctx") % ROW
-    previous, own = terms[0], terms[REACH]
+    previous, own = after(terms[0], earlier), terms[REACH]
     for distance in range(1, ROW):
         back = in_row(terms[REACH - distance], -distance).astype(jnp.float32)
         here = place + distance < ROW
@@ -243,21 +244,22 @@
     backward_lengths,
 ):
     kept = kept_keyvals[0].transpose(1, 0, 2)
+    sent = sent_keyvals[0].transpose(1, 0, 2)
+    sent, grads = after((sent, sent_grad[0]), kept)
     kept_previous = across_rows(kept, ROW)
-    grads = along_section(sent_grad[0], -1)
-    sent = sent_keyvals[0].transpose(1, 0, 2)
-    sent, queries = after((sent, sent_queries[0]), kept_previous)
+    grads = along_section(grads, -1)
     arrived_previous = across_rows_and_section(sent, ROW)
     arrived = along_section(sent, 1)
-    arrived_queries = along_section(queries, 1)
-
-    kept_window = gather_window(kept, kept_previous)
-    results = backward(backward_lengths, kept_queries[0], grads, kept_window)
-    own, crossed = return_terms(results[1:])
-
-    attention_out = forward(
-        forward_lengths, arrived_queries, gather_window(arrived, arrived_previous)
-    )
+    kept_sends = window_sends(kept, kept_previous)
+    kept_window = gather_window(kept, kept_previous, kept_sends)
+    arrived, arrived_previous = after((arrived, arrived_previous), (kept_window[1:REACH], grads))
+    arrived_sends = window_sends(arrived, arrived_previous)
+    arrived_queries = along_section(after(sent_queries[0], arrived_sends), 1)
+    kept_rows = after(kept_queries[0], arrived_sends)
+    arrived_window = gather_window(arrived, arrived_previous, arrived_sends)
+    results = backward(backward_lengths, kept_rows, grads, kept_window)
+    attention_out = forward(forward_lengths, arrived_queries, arrived_window)
+    own, crossed = return_terms(results[1:], attention_out)
     keyval_grad = (own + crossed.astype(jnp.float32)).astype(jnp.bfloat16).transpose(1, 0, 2)
     return attention_out[None], results[0][None], keyval_grad[None]
 

time: 102 us -> 104 us (1.020)
  waiting for transfers between devices: 31.3 us -> 54.3 us
  starting transfers between devices: 42.3 us -> 27.8 us
  Pallas kernels: 24.3 us -> 18.6 us
    ppermute x2, waiting for transfers between devices: 18.5 us -> 41.1 us  [across_rows(): lax.ppermute(block, 'ctx', [(i, i + distance) for i in range(size) if 0 <...]
    ppermute x9, starting transfers between devices: 18.7 us -> 12.2 us  [in_row(): lax.ppermute(block, 'ctx', [(c, c // ROW * ROW + (c + distance) % ROW) fo...]
    ppermute x1, starting transfers between devices: 6.11 us -> 2 us  [across_rows_and_section(): return lax.ppermute(block, ('section', 'ctx'), route)]
    pallas_call x1, Pallas kernels: 10.3 us -> 6.56 us  [forward(): pl.pallas_call(forward_kernel, grid=(KV_HEADS,), in_specs=[SMEM, group_co...]
    ppermute x3, starting transfers between devices: 3.45 us -> 0.25 us  [along_section(): lax.ppermute(block, 'section', [(i, (i + distance) % size) for i in range...]
    pallas_call x1, Pallas kernels: 14 us -> 12 us  [backward(): pl.pallas_call(backward_kernel, grid=(KV_HEADS,), in_specs=[SMEM, group_c...]
    transpose x0 -> x1, local copies, waits for them, and re-layouts: none -> 1.13 us  [body(): kept = kept_keyvals[0].transpose(1, 0, 2)]
  transfers between devices with their start and end apart: 15 -> 15, of which waited for: 6 -> 8; matrix products, arithmetic and copies ran while one was open for 1% -> 0% of each run, Pallas kernels for 24% -> 18%
where the time goes in v2:
time: 104 us
  waiting for transfers between devices  54.3 us (52%)
  starting transfers between devices  27.8 us (27%)
  Pallas kernels  18.6 us (18%)
  local copies, waits for them, and re-layouts  2.13 us (2%)
    ppermute x2, waiting for transfers between devices, across_rows(): lax.ppermute(block, 'ctx', [(i, i + distance) for i in range(size) if 0 <...  41.1 us
    ppermute x2, starting transfers between devices, across_rows(): lax.ppermute(block, 'ctx', [(i, i + distance) for i in range(size) if 0 <...  13.4 us
    ppermute x9, waiting for transfers between devices, in_row(): lax.ppermute(block, 'ctx', [(c, c // ROW * ROW + (c + distance) % ROW) fo...  13.3 us
    ppermute x9, starting transfers between devices, in_row(): lax.ppermute(block, 'ctx', [(c, c // ROW * ROW + (c + distance) % ROW) fo...  12.2 us
    pallas_call x1, Pallas kernels, backward(): pl.pallas_call(backward_kernel, grid=(KV_HEADS,), in_specs=[SMEM, group_c...  12 us
    pallas_call x1, Pallas kernels, forward(): pl.pallas_call(forward_kernel, grid=(KV_HEADS,), in_specs=[SMEM, group_co...  6.56 us
  transfers between devices with their start and end apart: 15, of which 8 were waited for; matrix products, arithmetic and copies ran while one was open for 0% of the time, Pallas kernels for 18%

profile of v2, /device:TPU:56, one launch (start us, length us, event | category | flops | bytes accessed | tf_op | source)
XLA Modules:
  0.0 104.1 jit_solution(7215579896421907997)
XLA Ops:
  0.6 1.1 %copy_bitcast_fusion = (bf16[2,128,512]{2,1,0:T(8,128)(2,1)S(1)}, bf16[2,128,512]{2,1,0:T(8,128)(2,1)S(1)}) fusion(bf16[1,128,2,512]{3,2,1,0:T(2,128)(2,1)} %param.11, bf16[1,128,2,512]{3,2,1,0:T(2,128)(2,1)} %param.8), kind=kLoop, calls=%fused_computation.16 | loop fusion | bytes 1048576 | tf_op jit(solution)/shard_map/transpose | solution.py:246
  1.9 8.6 %collective-permute-start.2 = (bf16[2,128,512]{2,1,0:T(8,128)(2,1)S(1)}, bf16[2,128,512]{2,1,0:T(8,128)(2,1)S(1)}, u32[]{:S(2)}, u32[]{:S(2)}) collective-permute-start(bf16[2,128,512]{2,1,0:T(8,128)(2,1)S(1)} %get-tuple-element.38.refs_4_), channel_id=1, source_target_pairs={{0,4},{1,5},{2,6},{3,7},{4,8},{5,9},{6,10},{7,11},{8,12},{9,13},{1... | collective-permute-start | bytes 786440 | tf_op jit(solution)/shard_map/ppermute | solution.py:33
  10.6 2.0 %collective-permute-start.1 = (bf16[2,128,512]{2,1,0:T(8,128)(2,1)S(1)}, bf16[2,128,512]{2,1,0:T(8,128)(2,1)S(1)}, u32[]{:S(2)}, u32[]{:S(2)}) collective-permute-start(bf16[2,128,512]{2,1,0:T(8,128)(2,1)S(1)} %get-tuple-element.16), channel_id=1, source_target_pairs={{0,36},{1,37},{2,38},{3,39},{4,40},{5,41},{6,42},{7,43},{8,44},{9,... | collective-permute-start | bytes 786440 | tf_op jit(solution)/shard_map/ppermute | solution.py:48
  12.6 26.0 %collective-permute-done.2.refs_0_ = bf16[2,128,512]{2,1,0:T(8,128)(2,1)S(1)} collective-permute-done((bf16[2,128,512]{2,1,0:T(8,128)(2,1)S(1)}, bf16[2,128,512]{2,1,0:T(8,128)(2,1)S(1)}, u32[]{:S(2)}, u32[]{:S(2)}) %collective-permute-start.2) | collective-permute-done | bytes 262176 | tf_op jit(solution)/shard_map/ppermute | solution.py:33
  38.7 2.8 %collective-permute-start.3 = (bf16[2,128,512]{2,1,0:T(8,128)(2,1)S(1)}, bf16[2,128,512]{2,1,0:T(8,128)(2,1)S(1)}, u32[]{:S(2)}, u32[]{:S(2)}) collective-permute-start(bf16[2,128,512]{2,1,0:T(8,128)(2,1)S(1)} %get-tuple-element.37), channel_id=1, source_target_pairs={{0,3},{1,0},{2,1},{3,2},{4,7},{5,4},{6,5},{7,6},{8,11},{9,8},{10,9... | collective-permute-start | bytes 786440 | tf_op jit(solution)/shard_map/ppermute | solution.py:53
  41.5 0.8 collective-permute-start.4
  42.3 0.9 collective-permute-start.5
  43.2 5.0 %collective-permute-done.3.refs_1_ = bf16[2,128,512]{2,1,0:T(8,128)(2,1)S(1)} collective-permute-done((bf16[2,128,512]{2,1,0:T(8,128)(2,1)S(1)}, bf16[2,128,512]{2,1,0:T(8,128)(2,1)S(1)}, u32[]{:S(2)}, u32[]{:S(2)}) %collective-permute-start.3) | collective-permute-done | bytes 262176 | tf_op jit(solution)/shard_map/ppermute | solution.py:53
  48.3 1.2 %collective-permute-done.4.refs_2_ = bf16[2,128,512]{2,1,0:T(8,128)(2,1)S(1)} collective-permute-done((bf16[2,128,512]{2,1,0:T(8,128)(2,1)S(1)}, bf16[2,128,512]{2,1,0:T(8,128)(2,1)S(1)}, u32[]{:S(2)}, u32[]{:S(2)}) %collective-permute-start.4) | collective-permute-done | bytes 262176 | tf_op jit(solution)/shard_map/ppermute | solution.py:53
  49.5 2.7 %collective-permute-done.5.refs_3_ = bf16[2,128,512]{2,1,0:T(8,128)(2,1)S(1)} collective-permute-done((bf16[2,128,512]{2,1,0:T(8,128)(2,1)S(1)}, bf16[2,128,512]{2,1,0:T(8,128)(2,1)S(1)}, u32[]{:S(2)}, u32[]{:S(2)}) %collective-permute-start.5) | collective-permute-done | bytes 262176 | tf_op jit(solution)/shard_map/ppermute | solution.py:53
  52.4 0.7 collective-permute-start.8
  53.1 0.8 collective-permute-start.9
  53.8 0.8 collective-permute-start.10
  54.7 12.0 %backward.1 = (bf16[128,4096]{1,0:T(8,128)(2,1)}, f32[2,128,512]{2,1,0:T(8,128)S(1)}, bf16[2,128,512]{2,1,0:T(8,128)(2,1)S(1)}, bf16[2,128,512]{2,1,0:T(8,128)(2...) custom-call(s32[1,16]{1,0:T(1,128)S(1)} %copy-done.1, bf16[128,4096]{1,0:T(8,128)(2,1)S(1)} %bitcast.23, ...), custom_call_target="tpu_custom_call" | custom-call | flops 3355443200 | bytes 8388608 | tf_op jit(solution)/shard_map/backward/pallas_call | solution.py:195
  66.7 2.5 %collective-permute-start.11 = (bf16[2,128,512]{2,1,0:T(8,128)(2,1)S(1)}, bf16[2,128,512]{2,1,0:T(8,128)(2,1)S(1)}, u32[]{:S(2)}, u32[]{:S(2)}) collective-permute-start(bf16[2,128,512]{2,1,0:T(8,128)(2,1)S(1)} %get-tuple-element.24), channel_id=1, source_target_pairs={{0,3},{1,0},{2,1},{3,2},{4,7},{5,4},{6,5},{7,6},{8,11},{9,8},{10,9... | collective-permute-start | bytes 786440 | tf_op jit(solution)/shard_map/ppermute | solution.py:53
  69.2 1.5 %collective-permute-start.12 = (bf16[2,128,512]{2,1,0:T(8,128)(2,1)S(1)}, bf16[2,128,512]{2,1,0:T(8,128)(2,1)S(1)}, u32[]{:S(2)}, u32[]{:S(2)}) collective-permute-start(bf16[2,128,512]{2,1,0:T(8,128)(2,1)S(1)} %get-tuple-element.25), channel_id=1, source_target_pairs={{0,2},{1,3},{2,0},{3,1},{4,6},{5,7},{6,4},{7,5},{8,10},{9,11},{10,... | collective-permute-start | bytes 786440 | tf_op jit(solution)/shard_map/ppermute | solution.py:53
  70.7 1.3 %collective-permute-start.13 = (bf16[2,128,512]{2,1,0:T(8,128)(2,1)S(1)}, bf16[2,128,512]{2,1,0:T(8,128)(2,1)S(1)}, u32[]{:S(2)}, u32[]{:S(2)}) collective-permute-start(bf16[2,128,512]{2,1,0:T(8,128)(2,1)S(1)} %get-tuple-element.26), channel_id=1, source_target_pairs={{0,1},{1,2},{2,3},{3,0},{4,5},{5,6},{6,7},{7,4},{8,9},{9,10},{10,1... | collective-permute-start | bytes 786440 | tf_op jit(solution)/shard_map/ppermute | solution.py:53
  72.1 6.6 %forward.1 = bf16[128,4096]{1,0:T(8,128)(2,1)} custom-call(s32[1,16]{1,0:T(1,128)S(1)} %copy-done.2, bf16[128,4096]{1,0:T(8,128)(2,1)S(1)} %collective-permute-done.7.q_ref, bf16[2,128,512]{2,1,0:T(8,128)(2,1)S(1)} %collective-permute-done.1.refs_0_, bf16[2,128,512]{2,1,0:T(8,128)(2,1)S(1)} %collective-permute-done.8.refs_1_, ...), custom_call_target="tpu_custom_call" | custom-call | flops 1342177280 | bytes 4194304 | tf_op jit(solution)/shard_map/forward/pallas_call | solution.py:175
  78.6 0.6 collective-permute-done.11
  79.2 0.8 collective-permute-done.12
  80.0 2.9 %collective-permute-done.13 = bf16[2,128,512]{2,1,0:T(8,128)(2,1)S(1)} collective-permute-done((bf16[2,128,512]{2,1,0:T(8,128)(2,1)S(1)}, bf16[2,128,512]{2,1,0:T(8,128)(2,1)S(1)}, u32[]{:S(2)}, u32[]{:S(2)}) %collective-permute-start.13) | collective-permute-done | bytes 262176 | tf_op jit(solution)/shard_map/ppermute | solution.py:53
  83.1 4.8 %collective-permute-start.14 = (bf16[2,128,512]{2,1,0:T(8,128)(2,1)S(1)}, bf16[2,128,512]{2,1,0:T(8,128)(2,1)S(1)}, u32[]{:S(2)}, u32[]{:S(2)}) collective-permute-start(bf16[2,128,512]{2,1,0:T(8,128)(2,1)S(1)} %fusion.8), channel_id=1, source_target_pairs={{4,0},{5,1},{6,2},{7,3},{8,4},{9,5},{10,6},{11,7},{12,8},{13,9},{1... | collective-permute-start | bytes 786440 | tf_op jit(solution)/shard_map/ppermute | solution.py:33
  87.8 15.1 %collective-permute-done.14 = bf16[2,128,512]{2,1,0:T(8,128)(2,1)S(1)} collective-permute-done((bf16[2,128,512]{2,1,0:T(8,128)(2,1)S(1)}, bf16[2,128,512]{2,1,0:T(8,128)(2,1)S(1)}, u32[]{:S(2)}, u32[]{:S(2)}) %collective-permute-start.14) | collective-permute-done | bytes 262176 | tf_op jit(solution)/shard_map/ppermute | solution.py:33
  103.1 1.0 copy.12
  (24 shorter events, 0.8 us)
Async XLA Ops:
  0.6 38.0 %copy-start.3 = (bf16[1,128,2,512]{3,2,1,0:T(2,128)(2,1)S(1)}, bf16[1,128,2,512]{3,2,1,0:T(2,128)(2,1)}, u32[]{:S(2)}) copy-start(bf16[1,128,2,512]{3,2,1,0:T(2,128)(2,1)} %param.11) | copy-start | bytes 786436
  1.8 50.4 %collective-permute-start.6 = (bf16[128,4096]{1,0:T(8,128)(2,1)}, bf16[128,4096]{1,0:T(8,128)(2,1)S(1)}, u32[]{:S(2)}, u32[]{:S(2)}) collective-permute-start(bf16[128,4096]{1,0:T(8,128)(2,1)} %bitcast.24), channel_id=1, source_target_pairs={{0,224},{32,0},{64,32},{96,64},{128,96},{160,128},{192,160},{224,1... | collective-permute-start | bytes 3145736 | tf_op jit(solution)/shard_map/ppermute | solution.py:26
  1.9 36.8 %collective-permute-start.2 = (bf16[2,128,512]{2,1,0:T(8,128)(2,1)S(1)}, bf16[2,128,512]{2,1,0:T(8,128)(2,1)S(1)}, u32[]{:S(2)}, u32[]{:S(2)}) collective-permute-start(bf16[2,128,512]{2,1,0:T(8,128)(2,1)S(1)} %get-tuple-element.38.refs_4_), channel_id=1, source_target_pairs={{0,4},{1,5},{2,6},{3,7},{4,8},{5,9},{6,10},{7,11},{8,12},{9,13},{1... | collective-permute-start | bytes 786440 | tf_op jit(solution)/shard_map/ppermute | solution.py:33
  10.5 31.8 %collective-permute-start = (bf16[2,128,512]{2,1,0:T(8,128)(2,1)S(1)}, bf16[2,128,512]{2,1,0:T(8,128)(2,1)S(1)}, u32[]{:S(2)}, u32[]{:S(2)}) collective-permute-start(bf16[2,128,512]{2,1,0:T(8,128)(2,1)S(1)} %get-tuple-element.16), channel_id=1, source_target_pairs={{0,32},{32,64},{64,96},{96,128},{128,160},{160,192},{192,224},{224... | collective-permute-start | bytes 786440 | tf_op jit(solution)/shard_map/ppermute | solution.py:26
  10.6 32.6 %collective-permute-start.1 = (bf16[2,128,512]{2,1,0:T(8,128)(2,1)S(1)}, bf16[2,128,512]{2,1,0:T(8,128)(2,1)S(1)}, u32[]{:S(2)}, u32[]{:S(2)}) collective-permute-start(bf16[2,128,512]{2,1,0:T(8,128)(2,1)S(1)} %get-tuple-element.16), channel_id=1, source_target_pairs={{0,36},{1,37},{2,38},{3,39},{4,40},{5,41},{6,42},{7,43},{8,44},{9,... | collective-permute-start | bytes 786440 | tf_op jit(solution)/shard_map/ppermute | solution.py:48
  12.6 39.7 %copy-start.4 = (bf16[1,128,4096]{2,1,0:T(8,128)(2,1)S(1)}, bf16[1,128,4096]{2,1,0:T(8,128)(2,1)}, u32[]{:S(2)}) copy-start(bf16[1,128,4096]{2,1,0:T(8,128)(2,1)} %param.7) | copy-start | bytes 3145732
  12.6 42.1 %copy-start = (bf16[1,128,4096]{2,1,0:T(8,128)(2,1)S(1)}, bf16[1,128,4096]{2,1,0:T(8,128)(2,1)}, u32[]{:S(2)}) copy-start(bf16[1,128,4096]{2,1,0:T(8,128)(2,1)} %param.10) | copy-start | bytes 3145732
  38.7 9.6 %collective-permute-start.3 = (bf16[2,128,512]{2,1,0:T(8,128)(2,1)S(1)}, bf16[2,128,512]{2,1,0:T(8,128)(2,1)S(1)}, u32[]{:S(2)}, u32[]{:S(2)}) collective-permute-start(bf16[2,128,512]{2,1,0:T(8,128)(2,1)S(1)} %get-tuple-element.37), channel_id=1, source_target_pairs={{0,3},{1,0},{2,1},{3,2},{4,7},{5,4},{6,5},{7,6},{8,11},{9,8},{10,9... | collective-permute-start | bytes 786440 | tf_op jit(solution)/shard_map/ppermute | solution.py:53
  41.5 8.0 %collective-permute-start.4 = (bf16[2,128,512]{2,1,0:T(8,128)(2,1)S(1)}, bf16[2,128,512]{2,1,0:T(8,128)(2,1)S(1)}, u32[]{:S(2)}, u32[]{:S(2)}) collective-permute-start(bf16[2,128,512]{2,1,0:T(8,128)(2,1)S(1)} %get-tuple-element.36), channel_id=1, source_target_pairs={{0,2},{1,3},{2,0},{3,1},{4,6},{5,7},{6,4},{7,5},{8,10},{9,11},{10,... | collective-permute-start | bytes 786440 | tf_op jit(solution)/shard_map/ppermute | solution.py:53
  42.3 9.9 %collective-permute-start.5 = (bf16[2,128,512]{2,1,0:T(8,128)(2,1)S(1)}, bf16[2,128,512]{2,1,0:T(8,128)(2,1)S(1)}, u32[]{:S(2)}, u32[]{:S(2)}) collective-permute-start(bf16[2,128,512]{2,1,0:T(8,128)(2,1)S(1)} %get-tuple-element.35), channel_id=1, source_target_pairs={{0,1},{1,2},{2,3},{3,0},{4,5},{5,6},{6,7},{7,4},{8,9},{9,10},{10,1... | collective-permute-start | bytes 786440 | tf_op jit(solution)/shard_map/ppermute | solution.py:53
  52.3 2.4 %copy-start.1 = (s32[1,16]{1,0:T(1,128)S(1)}, s32[1,16]{1,0:T(1,128)}, u32[]{:S(2)}) copy-start(s32[1,16]{1,0:T(1,128)} %lengths_ref.3) | copy-start | bytes 196
  52.3 19.8 %collective-permute-start.7 = (bf16[128,4096]{1,0:T(8,128)(2,1)S(1)}, bf16[128,4096]{1,0:T(8,128)(2,1)S(1)}, u32[]{:S(2)}, u32[]{:S(2)}) collective-permute-start(bf16[128,4096]{1,0:T(8,128)(2,1)S(1)} %bitcast.25), channel_id=1, source_target_pairs={{0,32},{32,64},{64,96},{96,128},{128,160},{160,192},{192,224},{224... | collective-permute-start | bytes 3145736 | tf_op jit(solution)/shard_map/ppermute | solution.py:26
  52.4 16.8 %collective-permute-start.8 = (bf16[2,128,512]{2,1,0:T(8,128)(2,1)S(1)}, bf16[2,128,512]{2,1,0:T(8,128)(2,1)S(1)}, u32[]{:S(2)}, u32[]{:S(2)}) collective-permute-start(bf16[2,128,512]{2,1,0:T(8,128)(2,1)S(1)} %get-tuple-element.32), channel_id=1, source_target_pairs={{0,3},{1,0},{2,1},{3,2},{4,7},{5,4},{6,5},{7,6},{8,11},{9,8},{10,9... | collective-permute-start | bytes 786440 | tf_op jit(solution)/shard_map/ppermute | solution.py:53
  53.1 17.7 %collective-permute-start.9 = (bf16[2,128,512]{2,1,0:T(8,128)(2,1)S(1)}, bf16[2,128,512]{2,1,0:T(8,128)(2,1)S(1)}, u32[]{:S(2)}, u32[]{:S(2)}) collective-permute-start(bf16[2,128,512]{2,1,0:T(8,128)(2,1)S(1)} %get-tuple-element.33), channel_id=1, source_target_pairs={{0,2},{1,3},{2,0},{3,1},{4,6},{5,7},{6,4},{7,5},{8,10},{9,11},{10,... | collective-permute-start | bytes 786440 | tf_op jit(solution)/shard_map/ppermute | solution.py:53
  53.8 18.2 %collective-permute-start.10 = (bf16[2,128,512]{2,1,0:T(8,128)(2,1)S(1)}, bf16[2,128,512]{2,1,0:T(8,128)(2,1)S(1)}, u32[]{:S(2)}, u32[]{:S(2)}) collective-permute-start(bf16[2,128,512]{2,1,0:T(8,128)(2,1)S(1)} %get-tuple-element.34), channel_id=1, source_target_pairs={{0,1},{1,2},{2,3},{3,0},{4,5},{5,6},{6,7},{7,4},{8,9},{9,10},{10,1... | collective-permute-start | bytes 786440 | tf_op jit(solution)/shard_map/ppermute | solution.py:53
  66.7 12.5 %collective-permute-start.11 = (bf16[2,128,512]{2,1,0:T(8,128)(2,1)S(1)}, bf16[2,128,512]{2,1,0:T(8,128)(2,1)S(1)}, u32[]{:S(2)}, u32[]{:S(2)}) collective-permute-start(bf16[2,128,512]{2,1,0:T(8,128)(2,1)S(1)} %get-tuple-element.24), channel_id=1, source_target_pairs={{0,3},{1,0},{2,1},{3,2},{4,7},{5,4},{6,5},{7,6},{8,11},{9,8},{10,9... | collective-permute-start | bytes 786440 | tf_op jit(solution)/shard_map/ppermute | solution.py:53
  69.2 2.9 %copy-start.2 = (s32[1,16]{1,0:T(1,128)S(1)}, s32[1,16]{1,0:T(1,128)}, u32[]{:S(2)}) copy-start(s32[1,16]{1,0:T(1,128)} %lengths_ref.2) | copy-start | bytes 196
  69.2 10.8 %collective-permute-start.12 = (bf16[2,128,512]{2,1,0:T(8,128)(2,1)S(1)}, bf16[2,128,512]{2,1,0:T(8,128)(2,1)S(1)}, u32[]{:S(2)}, u32[]{:S(2)}) collective-permute-start(bf16[2,128,512]{2,1,0:T(8,128)(2,1)S(1)} %get-tuple-element.25), channel_id=1, source_target_pairs={{0,2},{1,3},{2,0},{3,1},{4,6},{5,7},{6,4},{7,5},{8,10},{9,11},{10,... | collective-permute-start | bytes 786440 | tf_op jit(solution)/shard_map/ppermute | solution.py:53
  70.7 12.2 %collective-permute-start.13 = (bf16[2,128,512]{2,1,0:T(8,128)(2,1)S(1)}, bf16[2,128,512]{2,1,0:T(8,128)(2,1)S(1)}, u32[]{:S(2)}, u32[]{:S(2)}) collective-permute-start(bf16[2,128,512]{2,1,0:T(8,128)(2,1)S(1)} %get-tuple-element.26), channel_id=1, source_target_pairs={{0,1},{1,2},{2,3},{3,0},{4,5},{5,6},{6,7},{7,4},{8,9},{9,10},{10,1... | collective-permute-start | bytes 786440 | tf_op jit(solution)/shard_map/ppermute | solution.py:53
  83.1 19.8 %collective-permute-start.14 = (bf16[2,128,512]{2,1,0:T(8,128)(2,1)S(1)}, bf16[2,128,512]{2,1,0:T(8,128)(2,1)S(1)}, u32[]{:S(2)}, u32[]{:S(2)}) collective-permute-start(bf16[2,128,512]{2,1,0:T(8,128)(2,1)S(1)} %fusion.8), channel_id=1, source_target_pairs={{4,0},{5,1},{6,2},{7,3},{8,4},{9,5},{10,6},{11,7},{12,8},{13,9},{1... | collective-permute-start | bytes 786440 | tf_op jit(solution)/shard_map/ppermute | solution.py:33

commit v3 on v1

--- a/solution.py
+++ b/solution.py
@@ -17,6 +17,7 @@
 EXP2_SCALE = LOGIT_SCALE * math.log2(math.e)
 MASKED = -1e30
 CHUNK_HEADS = 2
+STEP_GROUPS = 2
 
 SMEM = pl.BlockSpec(memory_space=pltpu.SMEM)
 
@@ -94,87 +95,108 @@
     )
 
 
-def window(block_refs, index):
-    return jnp.concatenate([ref[index] for ref in block_refs], axis=0)
-
-
-def exponentials(keys, queries, bias_ref):
-    scores = nt_dot(keys, queries) * EXP2_SCALE + jnp.concatenate(
-        [bias_ref[...]] * CHUNK_HEADS, axis=1
-    )
+def window(block_refs, index, group):
+    columns = slice(group * WIDTH, (group + 1) * WIDTH)
+    return jnp.concatenate([ref[index, :, columns] for ref in block_refs], axis=0)
+
+
+def write_heads(ref, first, count, transposed):
+    for k in range(count):
+        at = (first + k) * WIDTH
+        ref[:, at : at + WIDTH] = transposed[:, k * WIDTH : (k + 1) * WIDTH].T.astype(ref.dtype)
+
+
+def exponentials(scores, bias):
+    scores = scores * EXP2_SCALE + bias
     return jnp.exp2(scores - jnp.max(scores, axis=0, keepdims=True))
 
 
 def forward_kernel(lengths_ref, q_ref, *refs):
     block_refs, (out_ref, bias_ref) = refs[: REACH + 1], refs[REACH + 1 :]
+    write_bias(lengths_ref, bias_ref)
+    bias = jnp.concatenate([bias_ref[...]] * GROUP, axis=1)
+    for group in range(KV_HEADS):
+        queries = head_rows(q_ref, group * GROUP, GROUP)
+        e = exponentials(nt_dot(window(block_refs, 0, group), queries), bias)
+        total = jnp.sum(e, axis=0, keepdims=True)
+        out_t = nn_dot(window(block_refs, 1, group).T, e.astype(jnp.bfloat16)) / total
+        write_heads(out_ref, group * GROUP, GROUP, out_t)
+
+
+def backward_kernel(lengths_ref, q_ref, g_ref, *refs):
+    block_refs, refs = refs[: REACH + 1], refs[REACH + 1 :]
+    dq_ref, *grad_refs, bias_ref = refs
+    tokens = q_ref.shape[0]
 
     @pl.when(pl.program_id(0) == 0)
     def _():
         write_bias(lengths_ref, bias_ref)
 
-    keys = window(block_refs, 0)
-    values_t = window(block_refs, 1).T
-    for first in range(0, GROUP, CHUNK_HEADS):
-        e = exponentials(keys, head_rows(q_ref, first, CHUNK_HEADS), bias_ref)
-        total = jnp.sum(e, axis=0, keepdims=True)
-        out_t = nn_dot(values_t, e.astype(jnp.bfloat16)) / total
-        for k in range(CHUNK_HEADS):
-            at = (first + k) * WIDTH
-            out_ref[:, at : at + WIDTH] = out_t[:, k * WIDTH : (k + 1) * WIDTH].T.astype(
-                jnp.bfloat16
-            )
-
-
-def backward_kernel(lengths_ref, q_ref, g_ref, *refs):
-    block_refs, refs = refs[: REACH + 1], refs[REACH + 1 :]
-    dq_ref, refs = refs[0], refs[1:]
-    grad_refs, (bias_ref, p_ref, ds_ref) = refs[: REACH + 1], refs[REACH + 1 :]
-    tokens = q_ref.shape[0]
-
-    @pl.when(pl.program_id(0) == 0)
-    def _():
-        write_bias(lengths_ref, bias_ref)
-
-    keys = window(block_refs, 0)
-    values = window(block_refs, 1)
-    keys_t = keys.T
-    for first in range(0, GROUP, CHUNK_HEADS):
-        lanes = slice(first * tokens, (first + CHUNK_HEADS) * tokens)
-        e = exponentials(keys, head_rows(q_ref, first, CHUNK_HEADS), bias_ref)
-        prob_grad = nt_dot(values, head_rows(g_ref, first, CHUNK_HEADS))
+    bias = jnp.concatenate([bias_ref[...]] * CHUNK_HEADS, axis=1)
+    keys = [window(block_refs, 0, group) for group in range(STEP_GROUPS)]
+    values = [window(block_refs, 1, group) for group in range(STEP_GROUPS)]
+    keys_t = [k.T for k in keys]
+    chunks = [
+        (group, group * GROUP + first)
+        for group in range(STEP_GROUPS)
+        for first in range(0, GROUP, CHUNK_HEADS)
+    ]
+
+    def products(chunk):
+        group, first = chunk
+        queries = head_rows(q_ref, first, CHUNK_HEADS)
+        grads = head_rows(g_ref, first, CHUNK_HEADS)
+        return queries, grads, nt_dot(keys[group], queries), nt_dot(values[group], grads)
+
+    def score_terms(scores, prob_grad):
+        e = exponentials(scores, bias)
         inverse = 1.0 / jnp.sum(e, axis=0, keepdims=True)
         delta = jnp.sum(e * prob_grad, axis=0, keepdims=True) * inverse
         probs = e * inverse
-        p_ref[:, lanes] = probs.astype(jnp.bfloat16)
-        score_grad = (probs * (prob_grad - delta)).astype(jnp.bfloat16)
-        ds_ref[:, lanes] = score_grad
-        dq_t = nn_dot(keys_t, score_grad) * LOGIT_SCALE
-        for k in range(CHUNK_HEADS):
-            at = (first + k) * WIDTH
-            dq_ref[:, at : at + WIDTH] = dq_t[:, k * WIDTH : (k + 1) * WIDTH].T.astype(
-                jnp.bfloat16
-            )
-    value_grad = nn_dot(p_ref[...], head_rows(g_ref, 0, GROUP))
-    key_grad = nn_dot(ds_ref[...], head_rows(q_ref, 0, GROUP)) * LOGIT_SCALE
-    for b, ref in enumerate(grad_refs):
-        rows = slice(b * tokens, (b + 1) * tokens)
-        ref[0] = key_grad[rows].astype(ref.dtype)
-        ref[1] = value_grad[rows].astype(ref.dtype)
-
-
-def specs(tokens):
-    group_cols = pl.BlockSpec((tokens, GROUP * WIDTH), lambda g: (0, g))
-    pair = pl.BlockSpec((2, tokens, WIDTH), lambda g: (0, 0, g))
+        return probs.astype(jnp.bfloat16), (probs * (prob_grad - delta)).astype(jnp.bfloat16)
+
+    totals = [None] * STEP_GROUPS
+
+    def gradients(chunk, queries, grads, probs, score_grad):
+        group, first = chunk
+        dq_t = nn_dot(keys_t[group], score_grad) * LOGIT_SCALE
+        write_heads(dq_ref, first, CHUNK_HEADS, dq_t)
+        terms = (nn_dot(score_grad, queries), nn_dot(probs, grads))
+        if totals[group] is not None:
+            terms = tuple(a + b for a, b in zip(totals[group], terms))
+        totals[group] = terms
+
+    ready, waiting = products(chunks[0]), None
+    for at, chunk in enumerate(chunks):
+        upcoming = products(chunks[at + 1]) if at + 1 < len(chunks) else None
+        queries, grads, scores, prob_grad = ready
+        terms = score_terms(scores, prob_grad)
+        if waiting is not None:
+            gradients(*waiting)
+        ready, waiting = upcoming, (chunk, queries, grads, *terms)
+    gradients(*waiting)
+
+    for group, (key_grad, value_grad) in enumerate(totals):
+        columns = slice(group * WIDTH, (group + 1) * WIDTH)
+        for b, ref in enumerate(grad_refs):
+            rows = slice(b * tokens, (b + 1) * tokens)
+            ref[0, :, columns] = (key_grad[rows] * LOGIT_SCALE).astype(ref.dtype)
+            ref[1, :, columns] = value_grad[rows].astype(ref.dtype)
+
+
+def specs(tokens, groups):
+    group_cols = pl.BlockSpec((tokens, groups * GROUP * WIDTH), lambda g: (0, g))
+    pair = pl.BlockSpec((2, tokens, groups * WIDTH), lambda g: (0, 0, g))
     return group_cols, pair
 
 
 def forward(lengths, queries, blocks):
     tokens, width = queries.shape
-    group_cols, pair = specs(tokens)
+    group_cols, pair = specs(tokens, KV_HEADS)
     keys = (REACH + 1) * tokens
     return pl.pallas_call(
         forward_kernel,
-        grid=(KV_HEADS,),
+        grid=(1,),
         in_specs=[SMEM, group_cols] + [pair] * len(blocks),
         out_specs=group_cols,
         out_shape=jax.ShapeDtypeStruct((tokens, width), jnp.bfloat16),
@@ -189,20 +211,18 @@
 
 def backward(lengths, queries, grads, blocks):
     tokens, width = queries.shape
-    group_cols, pair = specs(tokens)
+    group_cols, pair = specs(tokens, STEP_GROUPS)
     keys = (REACH + 1) * tokens
     kinds = [jnp.float32] + [jnp.bfloat16] * (REACH - 1) + [jnp.float32]
     return pl.pallas_call(
         backward_kernel,
-        grid=(KV_HEADS,),
+        grid=(KV_HEADS // STEP_GROUPS,),
         in_specs=[SMEM, group_cols, group_cols] + [pair] * len(blocks),
         out_specs=[group_cols] + [pair] * len(blocks),
         out_shape=[jax.ShapeDtypeStruct((tokens, width), jnp.bfloat16)]
         + [jax.ShapeDtypeStruct(blocks[0].shape, kind) for kind in kinds],
         scratch_shapes=[
             pltpu.VMEM((keys, tokens), jnp.float32),
-            pltpu.VMEM((keys, GROUP * tokens), jnp.bfloat16),
-            pltpu.VMEM((keys, GROUP * tokens), jnp.bfloat16),
         ],
         compiler_params=pltpu.CompilerParams(vmem_limit_bytes=40 * 1024 * 1024),
         cost_estimate=pl.CostEstimate(
@@ -212,13 +232,14 @@
     )(lengths, queries, grads, *blocks)
 
 
-def gather_window(own, previous):
+def window_sends(own, previous):
     place = lax.axis_index("ctx") % ROW
-    blocks = [own]
-    for distance in range(1, ROW):
-        sent = jnp.where(place + distance < ROW, own, previous)
-        blocks.insert(0, in_row(sent, distance))
-    return [previous] + blocks
+    return [jnp.where(place + d < ROW, own, previous) for d in range(1, ROW)]
+
+
+def gather_window(own, previous, sends):
+    moved = [in_row(sent, d) for d, sent in enumerate(sends, 1)]
+    return [previous] + moved[::-1] + [own]
 
 
 def return_terms(terms):
@@ -243,21 +264,22 @@
     backward_lengths,
 ):
     kept = kept_keyvals[0].transpose(1, 0, 2)
+    sent = sent_keyvals[0].transpose(1, 0, 2)
     kept_previous = across_rows(kept, ROW)
-    grads = along_section(sent_grad[0], -1)
-    sent = sent_keyvals[0].transpose(1, 0, 2)
-    sent, queries = after((sent, sent_queries[0]), kept_previous)
+    grads = along_section(after(sent_grad[0], (kept_previous, sent)), -1)
+    kept_sends = window_sends(kept, kept_previous)
+    kept_window = gather_window(kept, kept_previous, kept_sends)
+    sent, queries = after((sent, sent_queries[0]), kept_window[REACH - 1])
     arrived_previous = across_rows_and_section(sent, ROW)
     arrived = along_section(sent, 1)
+
     arrived_queries = along_section(queries, 1)
-
-    kept_window = gather_window(kept, kept_previous)
     results = backward(backward_lengths, kept_queries[0], grads, kept_window)
     own, crossed = return_terms(results[1:])
-
-    attention_out = forward(
-        forward_lengths, arrived_queries, gather_window(arrived, arrived_previous)
-    )
+    arrived_window = gather_window(
+        arrived, arrived_previous, window_sends(arrived, arrived_previous)
+    )
+    attention_out = forward(forward_lengths, arrived_queries, arrived_window)
     keyval_grad = (own + crossed.astype(jnp.float32)).astype(jnp.bfloat16).transpose(1, 0, 2)
     return attention_out[None], results[0][None], keyval_grad[None]
 

time: 102 us -> 95.1 us (0.932)
  the two profiles are of different devices: /device:TPU:56 before, /device:TPU:49 now
where the time goes in v3:
time: 95.1 us; the launch traced here: 94.9 us
  waiting for transfers between devices  38.6 us (41%)
  starting transfers between devices  37.3 us (39%)
  Pallas kernels  15.7 us (17%)
  local copies, waits for them, and re-layouts  2.07 us (2%)
    ppermute x9, waiting for transfers between devices, in_row(): lax.ppermute(block, 'ctx', [(c, c // ROW * ROW + (c + distance) % ROW) fo...  14.2 us
    ppermute x1, waiting for transfers between devices, across_rows_and_section(): return lax.ppermute(block, ('section', 'ctx'), route)  14 us
    ppermute x2, starting transfers between devices, across_rows(): lax.ppermute(block, 'ctx', [(i, i + distance) for i in range(size) if 0 <...  12 us
    ppermute x9, starting transfers between devices, in_row(): lax.ppermute(block, 'ctx', [(c, c // ROW * ROW + (c + distance) % ROW) fo...  11.6 us
    ppermute x2, waiting for transfers between devices, across_rows(): lax.ppermute(block, 'ctx', [(i, i + distance) for i in range(size) if 0 <...  10.4 us
    pallas_call x1, Pallas kernels, backward(): pl.pallas_call(backward_kernel, grid=(KV_HEADS // STEP_GROUPS,), in_specs...  10 us
    ppermute x3, starting transfers between devices, along_section(): lax.ppermute(block, 'section', [(i, (i + distance) % size) for i in range...  8.58 us
    pallas_call x1, Pallas kernels, forward(): pl.pallas_call(forward_kernel, grid=(1,), in_specs=[SMEM, group_cols] + [...  5.71 us
  transfers between devices with their start and end apart: 15, of which 5 were waited for; matrix products, arithmetic and copies ran while one was open for 0% of the time, Pallas kernels for 17%

profile of v3, /device:TPU:49, one launch (start us, length us, event | category | flops | bytes accessed | tf_op | source)
XLA Modules:
  0.0 94.9 jit_solution(4610514730145694020)
XLA Ops:
  0.7 1.0 %copy.21 = bf16[1,128,2,512]{3,1,2,0:T(8,128)(2,1)S(1)} copy(bf16[1,128,2,512]{3,2,1,0:T(2,128)(2,1)} %param.11) | data formatting | bytes 524288 | tf_op args[4]
  1.7 8.1 %collective-permute-start = (bf16[2,128,512]{2,1,0:T(8,128)(2,1)S(1)}, bf16[2,128,512]{2,1,0:T(8,128)(2,1)S(1)}, u32[]{:S(2)}, u32[]{:S(2)}) collective-permute-start(bf16[2,128,512]{2,1,0:T(8,128)(2,1)S(1)} %bitcast.25), channel_id=1, source_target_pairs={{0,4},{1,5},{2,6},{3,7},{4,8},{5,9},{6,10},{7,11},{8,12},{9,13},{1... | collective-permute-start | bytes 786440 | tf_op jit(solution)/shard_map/ppermute | solution.py:34
  9.8 8.0 %collective-permute-done.refs_0_ = bf16[2,128,512]{2,1,0:T(8,128)(2,1)S(1)} collective-permute-done((bf16[2,128,512]{2,1,0:T(8,128)(2,1)S(1)}, bf16[2,128,512]{2,1,0:T(8,128)(2,1)S(1)}, u32[]{:S(2)}, u32[]{:S(2)}) %collective-permute-start) | collective-permute-done | bytes 262176 | tf_op jit(solution)/shard_map/ppermute | solution.py:34
  17.8 3.5 %collective-permute-start.8 = (bf16[128,4096]{1,0:T(8,128)(2,1)}, bf16[128,4096]{1,0:T(8,128)(2,1)S(1)}, u32[]{:S(2)}, u32[]{:S(2)}) collective-permute-start(bf16[128,4096]{1,0:T(8,128)(2,1)} %bitcast.30), channel_id=1, source_target_pairs={{0,224},{32,0},{64,32},{96,64},{128,96},{160,128},{192,160},{224,1... | collective-permute-start | bytes 3145736 | tf_op jit(solution)/shard_map/ppermute | solution.py:27
  21.4 1.3 %collective-permute-start.1 = (bf16[2,128,512]{2,1,0:T(8,128)(2,1)S(1)}, bf16[2,128,512]{2,1,0:T(8,128)(2,1)S(1)}, u32[]{:S(2)}, u32[]{:S(2)}) collective-permute-start(bf16[2,128,512]{2,1,0:T(8,128)(2,1)S(1)} %get-tuple-element.26), channel_id=1, source_target_pairs={{0,1},{1,2},{2,3},{3,0},{4,5},{5,6},{6,7},{7,4},{8,9},{9,10},{10,1... | collective-permute-start | bytes 786440 | tf_op jit(solution)/shard_map/ppermute | solution.py:54
  22.7 2.5 %collective-permute-start.10 = (bf16[2,128,512]{2,1,0:T(8,128)(2,1)S(1)}, bf16[2,128,512]{2,1,0:T(8,128)(2,1)S(1)}, u32[]{:S(2)}, u32[]{:S(2)}) collective-permute-start(bf16[2,128,512]{2,1,0:T(8,128)(2,1)S(1)} %get-tuple-element.24), channel_id=1, source_target_pairs={{0,2},{1,3},{2,0},{3,1},{4,6},{5,7},{6,4},{7,5},{8,10},{9,11},{10,... | collective-permute-start | bytes 786440 | tf_op jit(solution)/shard_map/ppermute | solution.py:54
  25.1 1.2 %collective-permute-start.9 = (bf16[2,128,512]{2,1,0:T(8,128)(2,1)S(1)}, bf16[2,128,512]{2,1,0:T(8,128)(2,1)S(1)}, u32[]{:S(2)}, u32[]{:S(2)}) collective-permute-start(bf16[2,128,512]{2,1,0:T(8,128)(2,1)S(1)} %get-tuple-element.25), channel_id=1, source_target_pairs={{0,3},{1,0},{2,1},{3,2},{4,7},{5,4},{6,5},{7,6},{8,11},{9,8},{10,9... | collective-permute-start | bytes 786440 | tf_op jit(solution)/shard_map/ppermute | solution.py:54
  26.3 4.3 %collective-permute-done.1.refs_3_ = bf16[2,128,512]{2,1,0:T(8,128)(2,1)S(1)} collective-permute-done((bf16[2,128,512]{2,1,0:T(8,128)(2,1)S(1)}, bf16[2,128,512]{2,1,0:T(8,128)(2,1)S(1)}, u32[]{:S(2)}, u32[]{:S(2)}) %collective-permute-start.1) | collective-permute-done | bytes 262176 | tf_op jit(solution)/shard_map/ppermute | solution.py:54
  30.6 3.7 %collective-permute-start.2 = (bf16[128,4096]{1,0:T(8,128)(2,1)}, bf16[128,4096]{1,0:T(8,128)(2,1)S(1)}, u32[]{:S(2)}, u32[]{:S(2)}) collective-permute-start(bf16[128,4096]{1,0:T(8,128)(2,1)} %bitcast.31), channel_id=1, source_target_pairs={{0,32},{32,64},{64,96},{96,128},{128,160},{160,192},{192,224},{224... | collective-permute-start | bytes 3145736 | tf_op jit(solution)/shard_map/ppermute | solution.py:27
  34.3 5.1 %collective-permute-start.3 = (bf16[2,128,512]{2,1,0:T(8,128)(2,1)S(1)}, bf16[2,128,512]{2,1,0:T(8,128)(2,1)S(1)}, u32[]{:S(2)}, u32[]{:S(2)}) collective-permute-start(bf16[2,128,512]{2,1,0:T(8,128)(2,1)S(1)} %bitcast.28), channel_id=1, source_target_pairs={{0,36},{1,37},{2,38},{3,39},{4,40},{5,41},{6,42},{7,43},{8,44},{9,... | collective-permute-start | bytes 786440 | tf_op jit(solution)/shard_map/ppermute | solution.py:49
  39.4 1.4 %collective-permute-start.4 = (bf16[2,128,512]{2,1,0:T(8,128)(2,1)S(1)}, bf16[2,128,512]{2,1,0:T(8,128)(2,1)S(1)}, u32[]{:S(2)}, u32[]{:S(2)}) collective-permute-start(bf16[2,128,512]{2,1,0:T(8,128)(2,1)S(1)} %bitcast.29), channel_id=1, source_target_pairs={{0,32},{32,64},{64,96},{96,128},{128,160},{160,192},{192,224},{224... | collective-permute-start | bytes 786440 | tf_op jit(solution)/shard_map/ppermute | solution.py:27
  40.9 10.0 %backward.1 = (bf16[128,4096]{1,0:T(8,128)(2,1)}, f32[2,128,512]{2,1,0:T(8,128)S(1)}, bf16[2,128,512]{2,1,0:T(8,128)(2,1)S(1)}, bf16[2,128,512]{2,1,0:T(8,128)(2...) custom-call(s32[1,16]{1,0:T(1,128)S(1)} %copy-done.1, bf16[128,4096]{1,0:T(8,128)(2,1)S(1)} %bitcast.27, ...), custom_call_target="tpu_custom_call" | custom-call | flops 3355443200 | bytes 8388608 | tf_op jit(solution)/shard_map/backward/pallas_call | solution.py:217
  50.9 2.2 %collective-permute-start.11 = (bf16[2,128,512]{2,1,0:T(8,128)(2,1)S(1)}, bf16[2,128,512]{2,1,0:T(8,128)(2,1)S(1)}, u32[]{:S(2)}, u32[]{:S(2)}) collective-permute-start(bf16[2,128,512]{2,1,0:T(8,128)(2,1)S(1)} %get-tuple-element.17), channel_id=1, source_target_pairs={{0,3},{1,0},{2,1},{3,2},{4,7},{5,4},{6,5},{7,6},{8,11},{9,8},{10,9... | collective-permute-start | bytes 786440 | tf_op jit(solution)/shard_map/ppermute | solution.py:54
  53.0 0.5 collective-permute-start.12
  53.5 14.0 %collective-permute-done.3.refs_0_ = bf16[2,128,512]{2,1,0:T(8,128)(2,1)S(1)} collective-permute-done((bf16[2,128,512]{2,1,0:T(8,128)(2,1)S(1)}, bf16[2,128,512]{2,1,0:T(8,128)(2,1)S(1)}, u32[]{:S(2)}, u32[]{:S(2)}) %collective-permute-start.3) | collective-permute-done | bytes 262176 | tf_op jit(solution)/shard_map/ppermute | solution.py:49
  67.5 0.4 collective-permute-start.13
  68.0 2.5 %collective-permute-start.5 = (bf16[2,128,512]{2,1,0:T(8,128)(2,1)S(1)}, bf16[2,128,512]{2,1,0:T(8,128)(2,1)S(1)}, u32[]{:S(2)}, u32[]{:S(2)}) collective-permute-start(bf16[2,128,512]{2,1,0:T(8,128)(2,1)S(1)} %get-tuple-element.29), channel_id=1, source_target_pairs={{0,3},{1,0},{2,1},{3,2},{4,7},{5,4},{6,5},{7,6},{8,11},{9,8},{10,9... | collective-permute-start | bytes 786440 | tf_op jit(solution)/shard_map/ppermute | solution.py:54
  70.5 0.8 collective-permute-start.6
  71.3 0.3 collective-permute-start.7
  71.6 9.9 %collective-permute-done.13 = bf16[2,128,512]{2,1,0:T(8,128)(2,1)S(1)} collective-permute-done((bf16[2,128,512]{2,1,0:T(8,128)(2,1)S(1)}, bf16[2,128,512]{2,1,0:T(8,128)(2,1)S(1)}, u32[]{:S(2)}, u32[]{:S(2)}) %collective-permute-start.13) | collective-permute-done | bytes 262176 | tf_op jit(solution)/shard_map/ppermute | solution.py:54
  81.6 4.0 %collective-permute-start.14 = (bf16[2,128,512]{2,1,0:T(8,128)(2,1)S(1)}, bf16[2,128,512]{2,1,0:T(8,128)(2,1)S(1)}, u32[]{:S(2)}, u32[]{:S(2)}) collective-permute-start(bf16[2,128,512]{2,1,0:T(8,128)(2,1)S(1)} %fusion.8), channel_id=1, source_target_pairs={{4,0},{5,1},{6,2},{7,3},{8,4},{9,5},{10,6},{11,7},{12,8},{13,9},{1... | collective-permute-start | bytes 786440 | tf_op jit(solution)/shard_map/ppermute | solution.py:34
  85.7 5.7 %forward.1 = bf16[128,4096]{1,0:T(8,128)(2,1)} custom-call(s32[1,16]{1,0:T(1,128)S(1)} %copy-done.2, bf16[128,4096]{1,0:T(8,128)(2,1)S(1)} %collective-permute-done.2.q_ref, bf16[2,128,512]{2,1,0:T(8,128)(2,1)S(1)} %collective-permute-done.3.refs_0_, bf16[2,128,512]{2,1,0:T(8,128)(2,1)S(1)} %collective-permute-done.5.refs_1_, ...), custom_call_target="tpu_custom_call" | custom-call | flops 1342177280 | bytes 4194304 | tf_op jit(solution)/shard_map/forward/pallas_call | solution.py:197
  91.4 2.3 %collective-permute-done.14 = bf16[2,128,512]{2,1,0:T(8,128)(2,1)S(1)} collective-permute-done((bf16[2,128,512]{2,1,0:T(8,128)(2,1)S(1)}, bf16[2,128,512]{2,1,0:T(8,128)(2,1)S(1)}, u32[]{:S(2)}, u32[]{:S(2)}) %collective-permute-start.14) | collective-permute-done | bytes 262176 | tf_op jit(solution)/shard_map/ppermute | solution.py:34
  94.0 1.0 %copy.12 = bf16[1,128,2,512]{3,2,1,0:T(2,128)(2,1)} copy(bf16[1,128,2,512]{3,1,2,0:T(8,128)(2,1)S(1)} %fusion.9) | data formatting | bytes 524288
  (25 shorter events, 0.6 us)
Async XLA Ops:
  0.6 9.1 %copy-start.4 = (bf16[1,128,2,512]{3,2,1,0:T(2,128)(2,1)S(1)}, bf16[1,128,2,512]{3,2,1,0:T(2,128)(2,1)}, u32[]{:S(2)}) copy-start(bf16[1,128,2,512]{3,2,1,0:T(2,128)(2,1)} %param.8) | copy-start | bytes 786436
  0.6 20.7 %copy-start.3 = (bf16[1,128,2,512]{3,2,1,0:T(2,128)(2,1)S(1)}, bf16[1,128,2,512]{3,2,1,0:T(2,128)(2,1)}, u32[]{:S(2)}) copy-start(bf16[1,128,2,512]{3,2,1,0:T(2,128)(2,1)} %param.11) | copy-start | bytes 786436
  1.7 39.2 %copy-start = (bf16[1,128,4096]{2,1,0:T(8,128)(2,1)S(1)}, bf16[1,128,4096]{2,1,0:T(8,128)(2,1)}, u32[]{:S(2)}) copy-start(bf16[1,128,4096]{2,1,0:T(8,128)(2,1)} %param.10) | copy-start | bytes 3145732
  1.7 16.1 %collective-permute-start = (bf16[2,128,512]{2,1,0:T(8,128)(2,1)S(1)}, bf16[2,128,512]{2,1,0:T(8,128)(2,1)S(1)}, u32[]{:S(2)}, u32[]{:S(2)}) collective-permute-start(bf16[2,128,512]{2,1,0:T(8,128)(2,1)S(1)} %bitcast.25), channel_id=1, source_target_pairs={{0,4},{1,5},{2,6},{3,7},{4,8},{5,9},{6,10},{7,11},{8,12},{9,13},{1... | collective-permute-start | bytes 786440 | tf_op jit(solution)/shard_map/ppermute | solution.py:34
  17.8 23.0 %collective-permute-start.8 = (bf16[128,4096]{1,0:T(8,128)(2,1)}, bf16[128,4096]{1,0:T(8,128)(2,1)S(1)}, u32[]{:S(2)}, u32[]{:S(2)}) collective-permute-start(bf16[128,4096]{1,0:T(8,128)(2,1)} %bitcast.30), channel_id=1, source_target_pairs={{0,224},{32,0},{64,32},{96,64},{128,96},{160,128},{192,160},{224,1... | collective-permute-start | bytes 3145736 | tf_op jit(solution)/shard_map/ppermute | solution.py:27
  21.4 9.2 %collective-permute-start.1 = (bf16[2,128,512]{2,1,0:T(8,128)(2,1)S(1)}, bf16[2,128,512]{2,1,0:T(8,128)(2,1)S(1)}, u32[]{:S(2)}, u32[]{:S(2)}) collective-permute-start(bf16[2,128,512]{2,1,0:T(8,128)(2,1)S(1)} %get-tuple-element.26), channel_id=1, source_target_pairs={{0,1},{1,2},{2,3},{3,0},{4,5},{5,6},{6,7},{7,4},{8,9},{9,10},{10,1... | collective-permute-start | bytes 786440 | tf_op jit(solution)/shard_map/ppermute | solution.py:54
  22.7 16.7 %collective-permute-start.10 = (bf16[2,128,512]{2,1,0:T(8,128)(2,1)S(1)}, bf16[2,128,512]{2,1,0:T(8,128)(2,1)S(1)}, u32[]{:S(2)}, u32[]{:S(2)}) collective-permute-start(bf16[2,128,512]{2,1,0:T(8,128)(2,1)S(1)} %get-tuple-element.24), channel_id=1, source_target_pairs={{0,2},{1,3},{2,0},{3,1},{4,6},{5,7},{6,4},{7,5},{8,10},{9,11},{10,... | collective-permute-start | bytes 786440 | tf_op jit(solution)/shard_map/ppermute | solution.py:54
  25.1 15.7 %collective-permute-start.9 = (bf16[2,128,512]{2,1,0:T(8,128)(2,1)S(1)}, bf16[2,128,512]{2,1,0:T(8,128)(2,1)S(1)}, u32[]{:S(2)}, u32[]{:S(2)}) collective-permute-start(bf16[2,128,512]{2,1,0:T(8,128)(2,1)S(1)} %get-tuple-element.25), channel_id=1, source_target_pairs={{0,3},{1,0},{2,1},{3,2},{4,7},{5,4},{6,5},{7,6},{8,11},{9,8},{10,9... | collective-permute-start | bytes 786440 | tf_op jit(solution)/shard_map/ppermute | solution.py:54
  30.6 10.3 %copy-start.1 = (s32[1,16]{1,0:T(1,128)S(1)}, s32[1,16]{1,0:T(1,128)}, u32[]{:S(2)}) copy-start(s32[1,16]{1,0:T(1,128)} %lengths_ref.3) | copy-start | bytes 196
  30.6 55.1 %collective-permute-start.2 = (bf16[128,4096]{1,0:T(8,128)(2,1)}, bf16[128,4096]{1,0:T(8,128)(2,1)S(1)}, u32[]{:S(2)}, u32[]{:S(2)}) collective-permute-start(bf16[128,4096]{1,0:T(8,128)(2,1)} %bitcast.31), channel_id=1, source_target_pairs={{0,32},{32,64},{64,96},{96,128},{128,160},{160,192},{192,224},{224... | collective-permute-start | bytes 3145736 | tf_op jit(solution)/shard_map/ppermute | solution.py:27
  34.3 33.3 %collective-permute-start.3 = (bf16[2,128,512]{2,1,0:T(8,128)(2,1)S(1)}, bf16[2,128,512]{2,1,0:T(8,128)(2,1)S(1)}, u32[]{:S(2)}, u32[]{:S(2)}) collective-permute-start(bf16[2,128,512]{2,1,0:T(8,128)(2,1)S(1)} %bitcast.28), channel_id=1, source_target_pairs={{0,36},{1,37},{2,38},{3,39},{4,40},{5,41},{6,42},{7,43},{8,44},{9,... | collective-permute-start | bytes 786440 | tf_op jit(solution)/shard_map/ppermute | solution.py:49
  39.4 28.6 %collective-permute-start.4 = (bf16[2,128,512]{2,1,0:T(8,128)(2,1)S(1)}, bf16[2,128,512]{2,1,0:T(8,128)(2,1)S(1)}, u32[]{:S(2)}, u32[]{:S(2)}) collective-permute-start(bf16[2,128,512]{2,1,0:T(8,128)(2,1)S(1)} %bitcast.29), channel_id=1, source_target_pairs={{0,32},{32,64},{64,96},{96,128},{128,160},{160,192},{192,224},{224... | collective-permute-start | bytes 786440 | tf_op jit(solution)/shard_map/ppermute | solution.py:27
  50.9 19.7 %collective-permute-start.11 = (bf16[2,128,512]{2,1,0:T(8,128)(2,1)S(1)}, bf16[2,128,512]{2,1,0:T(8,128)(2,1)S(1)}, u32[]{:S(2)}, u32[]{:S(2)}) collective-permute-start(bf16[2,128,512]{2,1,0:T(8,128)(2,1)S(1)} %get-tuple-element.17), channel_id=1, source_target_pairs={{0,3},{1,0},{2,1},{3,2},{4,7},{5,4},{6,5},{7,6},{8,11},{9,8},{10,9... | collective-permute-start | bytes 786440 | tf_op jit(solution)/shard_map/ppermute | solution.py:54
  53.0 18.3 %collective-permute-start.12 = (bf16[2,128,512]{2,1,0:T(8,128)(2,1)S(1)}, bf16[2,128,512]{2,1,0:T(8,128)(2,1)S(1)}, u32[]{:S(2)}, u32[]{:S(2)}) collective-permute-start(bf16[2,128,512]{2,1,0:T(8,128)(2,1)S(1)} %get-tuple-element.18), channel_id=1, source_target_pairs={{0,2},{1,3},{2,0},{3,1},{4,6},{5,7},{6,4},{7,5},{8,10},{9,11},{10,... | collective-permute-start | bytes 786440 | tf_op jit(solution)/shard_map/ppermute | solution.py:54
  67.5 13.9 %collective-permute-start.13 = (bf16[2,128,512]{2,1,0:T(8,128)(2,1)S(1)}, bf16[2,128,512]{2,1,0:T(8,128)(2,1)S(1)}, u32[]{:S(2)}, u32[]{:S(2)}) collective-permute-start(bf16[2,128,512]{2,1,0:T(8,128)(2,1)S(1)} %get-tuple-element.19), channel_id=1, source_target_pairs={{0,1},{1,2},{2,3},{3,0},{4,5},{5,6},{6,7},{7,4},{8,9},{9,10},{10,1... | collective-permute-start | bytes 786440 | tf_op jit(solution)/shard_map/ppermute | solution.py:54
  68.0 17.6 %collective-permute-start.5 = (bf16[2,128,512]{2,1,0:T(8,128)(2,1)S(1)}, bf16[2,128,512]{2,1,0:T(8,128)(2,1)S(1)}, u32[]{:S(2)}, u32[]{:S(2)}) collective-permute-start(bf16[2,128,512]{2,1,0:T(8,128)(2,1)S(1)} %get-tuple-element.29), channel_id=1, source_target_pairs={{0,3},{1,0},{2,1},{3,2},{4,7},{5,4},{6,5},{7,6},{8,11},{9,8},{10,9... | collective-permute-start | bytes 786440 | tf_op jit(solution)/shard_map/ppermute | solution.py:54
  70.5 15.1 %collective-permute-start.6 = (bf16[2,128,512]{2,1,0:T(8,128)(2,1)S(1)}, bf16[2,128,512]{2,1,0:T(8,128)(2,1)S(1)}, u32[]{:S(2)}, u32[]{:S(2)}) collective-permute-start(bf16[2,128,512]{2,1,0:T(8,128)(2,1)S(1)} %get-tuple-element.28), channel_id=1, source_target_pairs={{0,2},{1,3},{2,0},{3,1},{4,6},{5,7},{6,4},{7,5},{8,10},{9,11},{10,... | collective-permute-start | bytes 786440 | tf_op jit(solution)/shard_map/ppermute | solution.py:54
  71.3 14.3 %collective-permute-start.7 = (bf16[2,128,512]{2,1,0:T(8,128)(2,1)S(1)}, bf16[2,128,512]{2,1,0:T(8,128)(2,1)S(1)}, u32[]{:S(2)}, u32[]{:S(2)}) collective-permute-start(bf16[2,128,512]{2,1,0:T(8,128)(2,1)S(1)} %get-tuple-element.27), channel_id=1, source_target_pairs={{0,1},{1,2},{2,3},{3,0},{4,5},{5,6},{6,7},{7,4},{8,9},{9,10},{10,1... | collective-permute-start | bytes 786440 | tf_op jit(solution)/shard_map/ppermute | solution.py:54
  81.5 4.2 %copy-start.2 = (s32[1,16]{1,0:T(1,128)S(1)}, s32[1,16]{1,0:T(1,128)}, u32[]{:S(2)}) copy-start(s32[1,16]{1,0:T(1,128)} %lengths_ref.2) | copy-start | bytes 196
  81.6 12.1 %collective-permute-start.14 = (bf16[2,128,512]{2,1,0:T(8,128)(2,1)S(1)}, bf16[2,128,512]{2,1,0:T(8,128)(2,1)S(1)}, u32[]{:S(2)}, u32[]{:S(2)}) collective-permute-start(bf16[2,128,512]{2,1,0:T(8,128)(2,1)S(1)} %fusion.8), channel_id=1, source_target_pairs={{4,0},{5,1},{6,2},{7,3},{8,4},{9,5},{10,6},{11,7},{12,8},{13,9},{1... | collective-permute-start | bytes 786440 | tf_op jit(solution)/shard_map/ppermute | solution.py:34

commit v4 on v3

--- a/solution.py
+++ b/solution.py
@@ -264,22 +264,25 @@
     backward_lengths,
 ):
     kept = kept_keyvals[0].transpose(1, 0, 2)
-    sent = sent_keyvals[0].transpose(1, 0, 2)
+    sent = after(sent_keyvals[0], kept).transpose(1, 0, 2)
     kept_previous = across_rows(kept, ROW)
+    arrived = along_section(sent, 1)
+    kept_previous = after(kept_previous, arrived)
     grads = along_section(after(sent_grad[0], (kept_previous, sent)), -1)
     kept_sends = window_sends(kept, kept_previous)
     kept_window = gather_window(kept, kept_previous, kept_sends)
-    sent, queries = after((sent, sent_queries[0]), kept_window[REACH - 1])
+    sent = after(sent, kept_window[REACH - 1])
     arrived_previous = across_rows_and_section(sent, ROW)
-    arrived = along_section(sent, 1)
-
+
+    results = backward(backward_lengths, kept_queries[0], grads, kept_window)
+    terms = after(results[1:], (arrived_previous, arrived))
+    queries = after(sent_queries[0], terms[0])
     arrived_queries = along_section(queries, 1)
-    results = backward(backward_lengths, kept_queries[0], grads, kept_window)
-    own, crossed = return_terms(results[1:])
-    arrived_window = gather_window(
-        arrived, arrived_previous, window_sends(arrived, arrived_previous)
-    )
+    arrived_sends = window_sends(arrived, arrived_previous)
+    own, crossed = return_terms(terms)
+    arrived_window = gather_window(arrived, arrived_previous, arrived_sends)
     attention_out = forward(forward_lengths, arrived_queries, arrived_window)
+    crossed = after(crossed, attention_out)
     keyval_grad = (own + crossed.astype(jnp.float32)).astype(jnp.bfloat16).transpose(1, 0, 2)
     return attention_out[None], results[0][None], keyval_grad[None]
 

time: 95.1 us -> 92.1 us (0.968)
  the two profiles are of different devices: /device:TPU:49 before, /device:TPU:56 now
where the time goes in v4:
time: 92.1 us; the launch traced here: 91.3 us
  waiting for transfers between devices  41 us (45%)
  starting transfers between devices  31.2 us (34%)
  Pallas kernels  15.7 us (17%)
  local copies, waits for them, and re-layouts  2.18 us (2%)
    ppermute x9, waiting for transfers between devices, in_row(): lax.ppermute(block, 'ctx', [(c, c // ROW * ROW + (c + distance) % ROW) fo...  20.2 us
    ppermute x2, waiting for transfers between devices, across_rows(): lax.ppermute(block, 'ctx', [(i, i + distance) for i in range(size) if 0 <...  16 us
    ppermute x9, starting transfers between devices, in_row(): lax.ppermute(block, 'ctx', [(c, c // ROW * ROW + (c + distance) % ROW) fo...  15.4 us
    ppermute x2, starting transfers between devices, across_rows(): lax.ppermute(block, 'ctx', [(i, i + distance) for i in range(size) if 0 <...  11.9 us
    pallas_call x1, Pallas kernels, backward(): pl.pallas_call(backward_kernel, grid=(KV_HEADS // STEP_GROUPS,), in_specs...  10 us
    pallas_call x1, Pallas kernels, forward(): pl.pallas_call(forward_kernel, grid=(1,), in_specs=[SMEM, group_cols] + [...  5.7 us
    ppermute x1, waiting for transfers between devices, across_rows_and_section(): return lax.ppermute(block, ('section', 'ctx'), route)  4.81 us
    ppermute x1, starting transfers between devices, across_rows_and_section(): return lax.ppermute(block, ('section', 'ctx'), route)  3.8 us
  transfers between devices with their start and end apart: 15, of which 9 were waited for; matrix products, arithmetic and copies ran while one was open for 0% of the time, Pallas kernels for 17%

profile of v4, /device:TPU:56, one launch (start us, length us, event | category | flops | bytes accessed | tf_op | source)
XLA Modules:
  0.0 91.3 jit_solution(7743267911395587243)
XLA Ops:
  0.7 1.2 %copy_bitcast_fusion = (bf16[128,2,512]{2,0,1:T(8,128)(2,1)S(1)}, bf16[2,128,512]{2,1,0:T(8,128)(2,1)S(1)}) fusion(bf16[1,128,2,512]{3,2,1,0:T(2,128)(2,1)} %param.8, bf16[1,128,2,512]{3,2,1,0:T(2,128)(2,1)} %param.11), kind=kLoop, calls=%fused_computation.16 | loop fusion | bytes 1048576 | tf_op jit(solution)/shard_map/squeeze | solution.py:267
  1.9 8.2 %collective-permute-start = (bf16[2,128,512]{2,1,0:T(8,128)(2,1)S(1)}, bf16[2,128,512]{2,1,0:T(8,128)(2,1)S(1)}, u32[]{:S(2)}, u32[]{:S(2)}) collective-permute-start(bf16[2,128,512]{2,1,0:T(8,128)(2,1)S(1)} %get-tuple-element.47.refs_4_), channel_id=1, source_target_pairs={{0,4},{1,5},{2,6},{3,7},{4,8},{5,9},{6,10},{7,11},{8,12},{9,13},{1... | collective-permute-start | bytes 786440 | tf_op jit(solution)/shard_map/ppermute | solution.py:34
  10.2 16.0 %collective-permute-done.refs_0_ = bf16[2,128,512]{2,1,0:T(8,128)(2,1)S(1)} collective-permute-done((bf16[2,128,512]{2,1,0:T(8,128)(2,1)S(1)}, bf16[2,128,512]{2,1,0:T(8,128)(2,1)S(1)}, u32[]{:S(2)}, u32[]{:S(2)}) %collective-permute-start) | collective-permute-done | bytes 262176 | tf_op jit(solution)/shard_map/ppermute | solution.py:34
  26.2 1.6 %collective-permute-start.5 = (bf16[2,128,512]{2,1,0:T(8,128)(2,1)S(1)}, bf16[2,128,512]{2,1,0:T(8,128)(2,1)S(1)}, u32[]{:S(2)}, u32[]{:S(2)}) collective-permute-start(bf16[2,128,512]{2,1,0:T(8,128)(2,1)S(1)} %get-tuple-element.43), channel_id=1, source_target_pairs={{0,1},{1,2},{2,3},{3,0},{4,5},{5,6},{6,7},{7,4},{8,9},{9,10},{10,1... | collective-permute-start | bytes 786440 | tf_op jit(solution)/shard_map/ppermute | solution.py:54
  27.7 1.7 %collective-permute-start.3 = (bf16[2,128,512]{2,1,0:T(8,128)(2,1)S(1)}, bf16[2,128,512]{2,1,0:T(8,128)(2,1)S(1)}, u32[]{:S(2)}, u32[]{:S(2)}) collective-permute-start(bf16[2,128,512]{2,1,0:T(8,128)(2,1)S(1)} %get-tuple-element.45), channel_id=1, source_target_pairs={{0,3},{1,0},{2,1},{3,2},{4,7},{5,4},{6,5},{7,6},{8,11},{9,8},{10,9... | collective-permute-start | bytes 786440 | tf_op jit(solution)/shard_map/ppermute | solution.py:54
  29.5 1.8 %collective-permute-start.4 = (bf16[2,128,512]{2,1,0:T(8,128)(2,1)S(1)}, bf16[2,128,512]{2,1,0:T(8,128)(2,1)S(1)}, u32[]{:S(2)}, u32[]{:S(2)}) collective-permute-start(bf16[2,128,512]{2,1,0:T(8,128)(2,1)S(1)} %get-tuple-element.44), channel_id=1, source_target_pairs={{0,2},{1,3},{2,0},{3,1},{4,6},{5,7},{6,4},{7,5},{8,10},{9,11},{10,... | collective-permute-start | bytes 786440 | tf_op jit(solution)/shard_map/ppermute | solution.py:54
  31.3 4.9 %collective-permute-done.5.refs_3_ = bf16[2,128,512]{2,1,0:T(8,128)(2,1)S(1)} collective-permute-done((bf16[2,128,512]{2,1,0:T(8,128)(2,1)S(1)}, bf16[2,128,512]{2,1,0:T(8,128)(2,1)S(1)}, u32[]{:S(2)}, u32[]{:S(2)}) %collective-permute-start.5) | collective-permute-done | bytes 262176 | tf_op jit(solution)/shard_map/ppermute | solution.py:54
  36.2 3.8 %collective-permute-start.6 = (bf16[2,128,512]{2,1,0:T(8,128)(2,1)S(1)}, bf16[2,128,512]{2,1,0:T(8,128)(2,1)S(1)}, u32[]{:S(2)}, u32[]{:S(2)}) collective-permute-start(bf16[2,128,512]{2,1,0:T(8,128)(2,1)S(1)} %bitcast.24), channel_id=1, source_target_pairs={{0,36},{1,37},{2,38},{3,39},{4,40},{5,41},{6,42},{7,43},{8,44},{9,... | collective-permute-start | bytes 786440 | tf_op jit(solution)/shard_map/ppermute | solution.py:49
  40.0 1.1 %collective-permute-done.3.refs_1_ = bf16[2,128,512]{2,1,0:T(8,128)(2,1)S(1)} collective-permute-done((bf16[2,128,512]{2,1,0:T(8,128)(2,1)S(1)}, bf16[2,128,512]{2,1,0:T(8,128)(2,1)S(1)}, u32[]{:S(2)}, u32[]{:S(2)}) %collective-permute-start.3) | collective-permute-done | bytes 262176 | tf_op jit(solution)/shard_map/ppermute | solution.py:54
  41.1 1.7 %collective-permute-done.4.refs_2_ = bf16[2,128,512]{2,1,0:T(8,128)(2,1)S(1)} collective-permute-done((bf16[2,128,512]{2,1,0:T(8,128)(2,1)S(1)}, bf16[2,128,512]{2,1,0:T(8,128)(2,1)S(1)}, u32[]{:S(2)}, u32[]{:S(2)}) %collective-permute-start.4) | collective-permute-done | bytes 262176 | tf_op jit(solution)/shard_map/ppermute | solution.py:54
  42.8 10.0 %backward.1 = (bf16[128,4096]{1,0:T(8,128)(2,1)}, f32[2,128,512]{2,1,0:T(8,128)S(1)}, bf16[2,128,512]{2,1,0:T(8,128)(2,1)S(1)}, bf16[2,128,512]{2,1,0:T(8,128)(2...) custom-call(s32[1,16]{1,0:T(1,128)S(1)} %copy-done.1, bf16[128,4096]{1,0:T(8,128)(2,1)S(1)} %bitcast.22, ...), custom_call_target="tpu_custom_call" | custom-call | flops 3355443200 | bytes 8388608 | tf_op jit(solution)/shard_map/backward/pallas_call | solution.py:217
  52.8 4.8 %collective-permute-done.6.refs_0_ = bf16[2,128,512]{2,1,0:T(8,128)(2,1)S(1)} collective-permute-done((bf16[2,128,512]{2,1,0:T(8,128)(2,1)S(1)}, bf16[2,128,512]{2,1,0:T(8,128)(2,1)S(1)}, u32[]{:S(2)}, u32[]{:S(2)}) %collective-permute-start.6) | collective-permute-done | bytes 262176 | tf_op jit(solution)/shard_map/ppermute | solution.py:49
  57.6 2.2 %collective-permute-start.11 = (bf16[2,128,512]{2,1,0:T(8,128)(2,1)S(1)}, bf16[2,128,512]{2,1,0:T(8,128)(2,1)S(1)}, u32[]{:S(2)}, u32[]{:S(2)}) collective-permute-start(bf16[2,128,512]{2,1,0:T(8,128)(2,1)S(1)} %get-tuple-element.33), channel_id=1, source_target_pairs={{0,3},{1,0},{2,1},{3,2},{4,7},{5,4},{6,5},{7,6},{8,11},{9,8},{10,9... | collective-permute-start | bytes 786440 | tf_op jit(solution)/shard_map/ppermute | solution.py:54
  59.8 0.9 collective-permute-start.12
  60.7 0.9 collective-permute-start.13
  61.7 2.0 %collective-permute-start.10 = (bf16[2,128,512]{2,1,0:T(8,128)(2,1)S(1)}, bf16[2,128,512]{2,1,0:T(8,128)(2,1)S(1)}, u32[]{:S(2)}, u32[]{:S(2)}) collective-permute-start(bf16[2,128,512]{2,1,0:T(8,128)(2,1)S(1)} %get-tuple-element.40), channel_id=1, source_target_pairs={{0,1},{1,2},{2,3},{3,0},{4,5},{5,6},{6,7},{7,4},{8,9},{9,10},{10,1... | collective-permute-start | bytes 786440 | tf_op jit(solution)/shard_map/ppermute | solution.py:54
  63.6 3.5 %collective-permute-done.11 = bf16[2,128,512]{2,1,0:T(8,128)(2,1)S(1)} collective-permute-done((bf16[2,128,512]{2,1,0:T(8,128)(2,1)S(1)}, bf16[2,128,512]{2,1,0:T(8,128)(2,1)S(1)}, u32[]{:S(2)}, u32[]{:S(2)}) %collective-permute-start.11) | collective-permute-done | bytes 262176 | tf_op jit(solution)/shard_map/ppermute | solution.py:54
  67.1 3.9 %collective-permute-start.8 = (bf16[2,128,512]{2,1,0:T(8,128)(2,1)S(1)}, bf16[2,128,512]{2,1,0:T(8,128)(2,1)S(1)}, u32[]{:S(2)}, u32[]{:S(2)}) collective-permute-start(bf16[2,128,512]{2,1,0:T(8,128)(2,1)S(1)} %get-tuple-element.42), channel_id=1, source_target_pairs={{0,3},{1,0},{2,1},{3,2},{4,7},{5,4},{6,5},{7,6},{8,11},{9,8},{10,9... | collective-permute-start | bytes 786440 | tf_op jit(solution)/shard_map/ppermute | solution.py:54
  71.5 2.2 %collective-permute-done.13 = bf16[2,128,512]{2,1,0:T(8,128)(2,1)S(1)} collective-permute-done((bf16[2,128,512]{2,1,0:T(8,128)(2,1)S(1)}, bf16[2,128,512]{2,1,0:T(8,128)(2,1)S(1)}, u32[]{:S(2)}, u32[]{:S(2)}) %collective-permute-start.13) | collective-permute-done | bytes 262176 | tf_op jit(solution)/shard_map/ppermute | solution.py:54
  73.9 3.7 %collective-permute-start.14 = (bf16[2,128,512]{2,1,0:T(8,128)(2,1)S(1)}, bf16[2,128,512]{2,1,0:T(8,128)(2,1)S(1)}, u32[]{:S(2)}, u32[]{:S(2)}) collective-permute-start(bf16[2,128,512]{2,1,0:T(8,128)(2,1)S(1)} %fusion.8), channel_id=1, source_target_pairs={{4,0},{5,1},{6,2},{7,3},{8,4},{9,5},{10,6},{11,7},{12,8},{13,9},{1... | collective-permute-start | bytes 786440 | tf_op jit(solution)/shard_map/ppermute | solution.py:34
  77.6 3.9 %collective-permute-done.10.refs_3_ = bf16[2,128,512]{2,1,0:T(8,128)(2,1)S(1)} collective-permute-done((bf16[2,128,512]{2,1,0:T(8,128)(2,1)S(1)}, bf16[2,128,512]{2,1,0:T(8,128)(2,1)S(1)}, u32[]{:S(2)}, u32[]{:S(2)}) %collective-permute-start.10) | collective-permute-done | bytes 262176 | tf_op jit(solution)/shard_map/ppermute | solution.py:54
  81.5 2.8 %collective-permute-done.9.refs_2_ = bf16[2,128,512]{2,1,0:T(8,128)(2,1)S(1)} collective-permute-done((bf16[2,128,512]{2,1,0:T(8,128)(2,1)S(1)}, bf16[2,128,512]{2,1,0:T(8,128)(2,1)S(1)}, u32[]{:S(2)}, u32[]{:S(2)}) %collective-permute-start.9) | collective-permute-done | bytes 262176 | tf_op jit(solution)/shard_map/ppermute | solution.py:54
  84.4 5.7 %forward.1 = bf16[128,4096]{1,0:T(8,128)(2,1)} custom-call(s32[1,16]{1,0:T(1,128)S(1)} %copy-done.2, bf16[128,4096]{1,0:T(8,128)(2,1)S(1)} %collective-permute-done.7.q_ref, bf16[2,128,512]{2,1,0:T(8,128)(2,1)S(1)} %collective-permute-done.6.refs_0_, bf16[2,128,512]{2,1,0:T(8,128)(2,1)S(1)} %collective-permute-done.8.refs_1_, ...), custom_call_target="tpu_custom_call" | custom-call | flops 1342177280 | bytes 4194304 | tf_op jit(solution)/shard_map/forward/pallas_call | solution.py:197
  90.3 1.0 %copy.12 = bf16[1,128,2,512]{3,2,1,0:T(2,128)(2,1)} copy(bf16[1,128,2,512]{3,1,2,0:T(8,128)(2,1)S(1)} %fusion.9) | data formatting | bytes 524288
  (24 shorter events, 1.1 us)
Async XLA Ops:
  0.6 25.5 %copy-start.3 = (bf16[1,128,2,512]{3,2,1,0:T(2,128)(2,1)S(1)}, bf16[1,128,2,512]{3,2,1,0:T(2,128)(2,1)}, u32[]{:S(2)}) copy-start(bf16[1,128,2,512]{3,2,1,0:T(2,128)(2,1)} %param.11) | copy-start | bytes 786436
  0.6 42.1 %copy-start = (bf16[1,128,4096]{2,1,0:T(8,128)(2,1)S(1)}, bf16[1,128,4096]{2,1,0:T(8,128)(2,1)}, u32[]{:S(2)}) copy-start(bf16[1,128,4096]{2,1,0:T(8,128)(2,1)} %param.10) | copy-start | bytes 3145732
  1.8 8.3 %collective-permute-start.1 = (bf16[2,128,512]{2,1,0:T(8,128)(2,1)S(1)}, bf16[2,128,512]{2,1,0:T(8,128)(2,1)S(1)}, u32[]{:S(2)}, u32[]{:S(2)}) collective-permute-start(bf16[2,128,512]{2,1,0:T(8,128)(2,1)S(1)} %bitcast.23), channel_id=1, source_target_pairs={{0,32},{32,64},{64,96},{96,128},{128,160},{160,192},{192,224},{224... | collective-permute-start | bytes 786440 | tf_op jit(solution)/shard_map/ppermute | solution.py:27
  1.9 24.2 %collective-permute-start = (bf16[2,128,512]{2,1,0:T(8,128)(2,1)S(1)}, bf16[2,128,512]{2,1,0:T(8,128)(2,1)S(1)}, u32[]{:S(2)}, u32[]{:S(2)}) collective-permute-start(bf16[2,128,512]{2,1,0:T(8,128)(2,1)S(1)} %get-tuple-element.47.refs_4_), channel_id=1, source_target_pairs={{0,4},{1,5},{2,6},{3,7},{4,8},{5,9},{6,10},{7,11},{8,12},{9,13},{1... | collective-permute-start | bytes 786440 | tf_op jit(solution)/shard_map/ppermute | solution.py:34
  26.1 16.7 %collective-permute-start.2 = (bf16[128,4096]{1,0:T(8,128)(2,1)}, bf16[128,4096]{1,0:T(8,128)(2,1)S(1)}, u32[]{:S(2)}, u32[]{:S(2)}) collective-permute-start(bf16[128,4096]{1,0:T(8,128)(2,1)} %bitcast.25), channel_id=1, source_target_pairs={{0,224},{32,0},{64,32},{96,64},{128,96},{160,128},{192,160},{224,1... | collective-permute-start | bytes 3145736 | tf_op jit(solution)/shard_map/ppermute | solution.py:27
  26.2 10.0 %collective-permute-start.5 = (bf16[2,128,512]{2,1,0:T(8,128)(2,1)S(1)}, bf16[2,128,512]{2,1,0:T(8,128)(2,1)S(1)}, u32[]{:S(2)}, u32[]{:S(2)}) collective-permute-start(bf16[2,128,512]{2,1,0:T(8,128)(2,1)S(1)} %get-tuple-element.43), channel_id=1, source_target_pairs={{0,1},{1,2},{2,3},{3,0},{4,5},{5,6},{6,7},{7,4},{8,9},{9,10},{10,1... | collective-permute-start | bytes 786440 | tf_op jit(solution)/shard_map/ppermute | solution.py:54
  27.7 13.3 %collective-permute-start.3 = (bf16[2,128,512]{2,1,0:T(8,128)(2,1)S(1)}, bf16[2,128,512]{2,1,0:T(8,128)(2,1)S(1)}, u32[]{:S(2)}, u32[]{:S(2)}) collective-permute-start(bf16[2,128,512]{2,1,0:T(8,128)(2,1)S(1)} %get-tuple-element.45), channel_id=1, source_target_pairs={{0,3},{1,0},{2,1},{3,2},{4,7},{5,4},{6,5},{7,6},{8,11},{9,8},{10,9... | collective-permute-start | bytes 786440 | tf_op jit(solution)/shard_map/ppermute | solution.py:54
  29.5 13.3 %copy-start.1 = (s32[1,16]{1,0:T(1,128)S(1)}, s32[1,16]{1,0:T(1,128)}, u32[]{:S(2)}) copy-start(s32[1,16]{1,0:T(1,128)} %lengths_ref.2) | copy-start | bytes 196
  29.5 13.3 %collective-permute-start.4 = (bf16[2,128,512]{2,1,0:T(8,128)(2,1)S(1)}, bf16[2,128,512]{2,1,0:T(8,128)(2,1)S(1)}, u32[]{:S(2)}, u32[]{:S(2)}) collective-permute-start(bf16[2,128,512]{2,1,0:T(8,128)(2,1)S(1)} %get-tuple-element.44), channel_id=1, source_target_pairs={{0,2},{1,3},{2,0},{3,1},{4,6},{5,7},{6,4},{7,5},{8,10},{9,11},{10,... | collective-permute-start | bytes 786440 | tf_op jit(solution)/shard_map/ppermute | solution.py:54
  36.2 21.4 %collective-permute-start.6 = (bf16[2,128,512]{2,1,0:T(8,128)(2,1)S(1)}, bf16[2,128,512]{2,1,0:T(8,128)(2,1)S(1)}, u32[]{:S(2)}, u32[]{:S(2)}) collective-permute-start(bf16[2,128,512]{2,1,0:T(8,128)(2,1)S(1)} %bitcast.24), channel_id=1, source_target_pairs={{0,36},{1,37},{2,38},{3,39},{4,40},{5,41},{6,42},{7,43},{8,44},{9,... | collective-permute-start | bytes 786440 | tf_op jit(solution)/shard_map/ppermute | solution.py:49
  42.8 14.8 %copy-start.4 = (bf16[1,128,4096]{2,1,0:T(8,128)(2,1)S(1)}, bf16[1,128,4096]{2,1,0:T(8,128)(2,1)}, u32[]{:S(2)}) copy-start(bf16[1,128,4096]{2,1,0:T(8,128)(2,1)} %param.7) | copy-start | bytes 3145732
  57.6 26.7 %collective-permute-start.7 = (bf16[128,4096]{1,0:T(8,128)(2,1)S(1)}, bf16[128,4096]{1,0:T(8,128)(2,1)S(1)}, u32[]{:S(2)}, u32[]{:S(2)}) collective-permute-start(bf16[128,4096]{1,0:T(8,128)(2,1)S(1)} %bitcast.26), channel_id=1, source_target_pairs={{0,32},{32,64},{64,96},{96,128},{128,160},{160,192},{192,224},{224... | collective-permute-start | bytes 3145736 | tf_op jit(solution)/shard_map/ppermute | solution.py:27
  57.6 9.5 %collective-permute-start.11 = (bf16[2,128,512]{2,1,0:T(8,128)(2,1)S(1)}, bf16[2,128,512]{2,1,0:T(8,128)(2,1)S(1)}, u32[]{:S(2)}, u32[]{:S(2)}) collective-permute-start(bf16[2,128,512]{2,1,0:T(8,128)(2,1)S(1)} %get-tuple-element.33), channel_id=1, source_target_pairs={{0,3},{1,0},{2,1},{3,2},{4,7},{5,4},{6,5},{7,6},{8,11},{9,8},{10,9... | collective-permute-start | bytes 786440 | tf_op jit(solution)/shard_map/ppermute | solution.py:54
  59.8 11.2 %collective-permute-start.12 = (bf16[2,128,512]{2,1,0:T(8,128)(2,1)S(1)}, bf16[2,128,512]{2,1,0:T(8,128)(2,1)S(1)}, u32[]{:S(2)}, u32[]{:S(2)}) collective-permute-start(bf16[2,128,512]{2,1,0:T(8,128)(2,1)S(1)} %get-tuple-element.34), channel_id=1, source_target_pairs={{0,2},{1,3},{2,0},{3,1},{4,6},{5,7},{6,4},{7,5},{8,10},{9,11},{10,... | collective-permute-start | bytes 786440 | tf_op jit(solution)/shard_map/ppermute | solution.py:54
  60.7 13.0 %collective-permute-start.13 = (bf16[2,128,512]{2,1,0:T(8,128)(2,1)S(1)}, bf16[2,128,512]{2,1,0:T(8,128)(2,1)S(1)}, u32[]{:S(2)}, u32[]{:S(2)}) collective-permute-start(bf16[2,128,512]{2,1,0:T(8,128)(2,1)S(1)} %get-tuple-element.35), channel_id=1, source_target_pairs={{0,1},{1,2},{2,3},{3,0},{4,5},{5,6},{6,7},{7,4},{8,9},{9,10},{10,1... | collective-permute-start | bytes 786440 | tf_op jit(solution)/shard_map/ppermute | solution.py:54
  61.7 19.8 %collective-permute-start.10 = (bf16[2,128,512]{2,1,0:T(8,128)(2,1)S(1)}, bf16[2,128,512]{2,1,0:T(8,128)(2,1)S(1)}, u32[]{:S(2)}, u32[]{:S(2)}) collective-permute-start(bf16[2,128,512]{2,1,0:T(8,128)(2,1)S(1)} %get-tuple-element.40), channel_id=1, source_target_pairs={{0,1},{1,2},{2,3},{3,0},{4,5},{5,6},{6,7},{7,4},{8,9},{9,10},{10,1... | collective-permute-start | bytes 786440 | tf_op jit(solution)/shard_map/ppermute | solution.py:54
  67.1 14.4 %collective-permute-start.8 = (bf16[2,128,512]{2,1,0:T(8,128)(2,1)S(1)}, bf16[2,128,512]{2,1,0:T(8,128)(2,1)S(1)}, u32[]{:S(2)}, u32[]{:S(2)}) collective-permute-start(bf16[2,128,512]{2,1,0:T(8,128)(2,1)S(1)} %get-tuple-element.42), channel_id=1, source_target_pairs={{0,3},{1,0},{2,1},{3,2},{4,7},{5,4},{6,5},{7,6},{8,11},{9,8},{10,9... | collective-permute-start | bytes 786440 | tf_op jit(solution)/shard_map/ppermute | solution.py:54
  71.0 13.4 %copy-start.2 = (s32[1,16]{1,0:T(1,128)S(1)}, s32[1,16]{1,0:T(1,128)}, u32[]{:S(2)}) copy-start(s32[1,16]{1,0:T(1,128)} %lengths_ref.3) | copy-start | bytes 196
  71.0 13.4 %collective-permute-start.9 = (bf16[2,128,512]{2,1,0:T(8,128)(2,1)S(1)}, bf16[2,128,512]{2,1,0:T(8,128)(2,1)S(1)}, u32[]{:S(2)}, u32[]{:S(2)}) collective-permute-start(bf16[2,128,512]{2,1,0:T(8,128)(2,1)S(1)} %get-tuple-element.41), channel_id=1, source_target_pairs={{0,2},{1,3},{2,0},{3,1},{4,6},{5,7},{6,4},{7,5},{8,10},{9,11},{10,... | collective-permute-start | bytes 786440 | tf_op jit(solution)/shard_map/ppermute | solution.py:54
  73.9 16.2 %collective-permute-start.14 = (bf16[2,128,512]{2,1,0:T(8,128)(2,1)S(1)}, bf16[2,128,512]{2,1,0:T(8,128)(2,1)S(1)}, u32[]{:S(2)}, u32[]{:S(2)}) collective-permute-start(bf16[2,128,512]{2,1,0:T(8,128)(2,1)S(1)} %fusion.8), channel_id=1, source_target_pairs={{4,0},{5,1},{6,2},{7,3},{8,4},{9,5},{10,6},{11,7},{12,8},{13,9},{1... | collective-permute-start | bytes 786440 | tf_op jit(solution)/shard_map/ppermute | solution.py:34

commit v5 on v4

--- a/solution.py
+++ b/solution.py
@@ -153,7 +153,8 @@
         inverse = 1.0 / jnp.sum(e, axis=0, keepdims=True)
         delta = jnp.sum(e * prob_grad, axis=0, keepdims=True) * inverse
         probs = e * inverse
-        return probs.astype(jnp.bfloat16), (probs * (prob_grad - delta)).astype(jnp.bfloat16)
+        rounded = probs.astype(jnp.bfloat16)
+        return rounded, rounded * (prob_grad - delta).astype(jnp.bfloat16)
 
     totals = [None] * STEP_GROUPS
 
@@ -268,8 +269,8 @@
     kept_previous = across_rows(kept, ROW)
     arrived = along_section(sent, 1)
     kept_previous = after(kept_previous, arrived)
-    grads = along_section(after(sent_grad[0], (kept_previous, sent)), -1)
     kept_sends = window_sends(kept, kept_previous)
+    grads = along_section(after(sent_grad[0], kept_sends), -1)
     kept_window = gather_window(kept, kept_previous, kept_sends)
     sent = after(sent, kept_window[REACH - 1])
     arrived_previous = across_rows_and_section(sent, ROW)

time: 92.1 us -> 92 us (level)
  no operation moved by 1% of the time
where the time goes in v5:
time: 92 us; the launch traced here: 91.1 us
  waiting for transfers between devices  40.6 us (44%)
  starting transfers between devices  31.4 us (34%)
  Pallas kernels  15.5 us (17%)
  local copies, waits for them, and re-layouts  2.24 us (2%)
    ppermute x9, waiting for transfers between devices, in_row(): lax.ppermute(block, 'ctx', [(c, c // ROW * ROW + (c + distance) % ROW) fo...  19.8 us
    ppermute x2, waiting for transfers between devices, across_rows(): lax.ppermute(block, 'ctx', [(i, i + distance) for i in range(size) if 0 <...  15.9 us
    ppermute x9, starting transfers between devices, in_row(): lax.ppermute(block, 'ctx', [(c, c // ROW * ROW + (c + distance) % ROW) fo...  15.5 us
    ppermute x2, starting transfers between devices, across_rows(): lax.ppermute(block, 'ctx', [(i, i + distance) for i in range(size) if 0 <...  12 us
    pallas_call x1, Pallas kernels, backward(): pl.pallas_call(backward_kernel, grid=(KV_HEADS // STEP_GROUPS,), in_specs...  9.85 us
    pallas_call x1, Pallas kernels, forward(): pl.pallas_call(forward_kernel, grid=(1,), in_specs=[SMEM, group_cols] + [...  5.7 us
    ppermute x1, waiting for transfers between devices, across_rows_and_section(): return lax.ppermute(block, ('section', 'ctx'), route)  4.89 us
    ppermute x1, starting transfers between devices, across_rows_and_section(): return lax.ppermute(block, ('section', 'ctx'), route)  3.72 us
  transfers between devices with their start and end apart: 15, of which 9 were waited for; matrix products, arithmetic and copies ran while one was open for 0% of the time, Pallas kernels for 17%

profile of v5, /device:TPU:56, one launch (start us, length us, event | category | flops | bytes accessed | tf_op | source)
XLA Modules:
  0.0 91.1 jit_solution(8976092481263736567)
XLA Ops:
  0.7 1.2 %copy_bitcast_fusion = (bf16[128,2,512]{2,0,1:T(8,128)(2,1)S(1)}, bf16[2,128,512]{2,1,0:T(8,128)(2,1)S(1)}) fusion(bf16[1,128,2,512]{3,2,1,0:T(2,128)(2,1)} %param.8, bf16[1,128,2,512]{3,2,1,0:T(2,128)(2,1)} %param.11), kind=kLoop, calls=%fused_computation.16 | loop fusion | bytes 1048576 | tf_op jit(solution)/shard_map/squeeze | solution.py:268
  2.0 8.2 %collective-permute-start = (bf16[2,128,512]{2,1,0:T(8,128)(2,1)S(1)}, bf16[2,128,512]{2,1,0:T(8,128)(2,1)S(1)}, u32[]{:S(2)}, u32[]{:S(2)}) collective-permute-start(bf16[2,128,512]{2,1,0:T(8,128)(2,1)S(1)} %get-tuple-element.47.refs_4_), channel_id=1, source_target_pairs={{0,4},{1,5},{2,6},{3,7},{4,8},{5,9},{6,10},{7,11},{8,12},{9,13},{1... | collective-permute-start | bytes 786440 | tf_op jit(solution)/shard_map/ppermute | solution.py:34
  10.2 15.9 %collective-permute-done.refs_0_ = bf16[2,128,512]{2,1,0:T(8,128)(2,1)S(1)} collective-permute-done((bf16[2,128,512]{2,1,0:T(8,128)(2,1)S(1)}, bf16[2,128,512]{2,1,0:T(8,128)(2,1)S(1)}, u32[]{:S(2)}, u32[]{:S(2)}) %collective-permute-start) | collective-permute-done | bytes 262176 | tf_op jit(solution)/shard_map/ppermute | solution.py:34
  26.3 1.6 %collective-permute-start.5 = (bf16[2,128,512]{2,1,0:T(8,128)(2,1)S(1)}, bf16[2,128,512]{2,1,0:T(8,128)(2,1)S(1)}, u32[]{:S(2)}, u32[]{:S(2)}) collective-permute-start(bf16[2,128,512]{2,1,0:T(8,128)(2,1)S(1)} %get-tuple-element.45), channel_id=1, source_target_pairs={{0,1},{1,2},{2,3},{3,0},{4,5},{5,6},{6,7},{7,4},{8,9},{9,10},{10,1... | collective-permute-start | bytes 786440 | tf_op jit(solution)/shard_map/ppermute | solution.py:54
  27.9 1.7 %collective-permute-start.3 = (bf16[2,128,512]{2,1,0:T(8,128)(2,1)S(1)}, bf16[2,128,512]{2,1,0:T(8,128)(2,1)S(1)}, u32[]{:S(2)}, u32[]{:S(2)}) collective-permute-start(bf16[2,128,512]{2,1,0:T(8,128)(2,1)S(1)} %get-tuple-element.43), channel_id=1, source_target_pairs={{0,3},{1,0},{2,1},{3,2},{4,7},{5,4},{6,5},{7,6},{8,11},{9,8},{10,9... | collective-permute-start | bytes 786440 | tf_op jit(solution)/shard_map/ppermute | solution.py:54
  29.7 1.8 %collective-permute-start.4 = (bf16[2,128,512]{2,1,0:T(8,128)(2,1)S(1)}, bf16[2,128,512]{2,1,0:T(8,128)(2,1)S(1)}, u32[]{:S(2)}, u32[]{:S(2)}) collective-permute-start(bf16[2,128,512]{2,1,0:T(8,128)(2,1)S(1)} %get-tuple-element.44), channel_id=1, source_target_pairs={{0,2},{1,3},{2,0},{3,1},{4,6},{5,7},{6,4},{7,5},{8,10},{9,11},{10,... | collective-permute-start | bytes 786440 | tf_op jit(solution)/shard_map/ppermute | solution.py:54
  31.5 4.8 %collective-permute-done.5.refs_3_ = bf16[2,128,512]{2,1,0:T(8,128)(2,1)S(1)} collective-permute-done((bf16[2,128,512]{2,1,0:T(8,128)(2,1)S(1)}, bf16[2,128,512]{2,1,0:T(8,128)(2,1)S(1)}, u32[]{:S(2)}, u32[]{:S(2)}) %collective-permute-start.5) | collective-permute-done | bytes 262176 | tf_op jit(solution)/shard_map/ppermute | solution.py:54
  36.3 3.7 %collective-permute-start.6 = (bf16[2,128,512]{2,1,0:T(8,128)(2,1)S(1)}, bf16[2,128,512]{2,1,0:T(8,128)(2,1)S(1)}, u32[]{:S(2)}, u32[]{:S(2)}) collective-permute-start(bf16[2,128,512]{2,1,0:T(8,128)(2,1)S(1)} %bitcast.24), channel_id=1, source_target_pairs={{0,36},{1,37},{2,38},{3,39},{4,40},{5,41},{6,42},{7,43},{8,44},{9,... | collective-permute-start | bytes 786440 | tf_op jit(solution)/shard_map/ppermute | solution.py:49
  40.0 1.2 %collective-permute-done.3.refs_1_ = bf16[2,128,512]{2,1,0:T(8,128)(2,1)S(1)} collective-permute-done((bf16[2,128,512]{2,1,0:T(8,128)(2,1)S(1)}, bf16[2,128,512]{2,1,0:T(8,128)(2,1)S(1)}, u32[]{:S(2)}, u32[]{:S(2)}) %collective-permute-start.3) | collective-permute-done | bytes 262176 | tf_op jit(solution)/shard_map/ppermute | solution.py:54
  41.2 1.7 %collective-permute-done.4.refs_2_ = bf16[2,128,512]{2,1,0:T(8,128)(2,1)S(1)} collective-permute-done((bf16[2,128,512]{2,1,0:T(8,128)(2,1)S(1)}, bf16[2,128,512]{2,1,0:T(8,128)(2,1)S(1)}, u32[]{:S(2)}, u32[]{:S(2)}) %collective-permute-start.4) | collective-permute-done | bytes 262176 | tf_op jit(solution)/shard_map/ppermute | solution.py:54
  42.9 9.8 %backward.1 = (bf16[128,4096]{1,0:T(8,128)(2,1)}, f32[2,128,512]{2,1,0:T(8,128)S(1)}, bf16[2,128,512]{2,1,0:T(8,128)(2,1)S(1)}, bf16[2,128,512]{2,1,0:T(8,128)(2...) custom-call(s32[1,16]{1,0:T(1,128)S(1)} %copy-done.1, bf16[128,4096]{1,0:T(8,128)(2,1)S(1)} %bitcast.22, ...), custom_call_target="tpu_custom_call" | custom-call | flops 3355443200 | bytes 8388608 | tf_op jit(solution)/shard_map/backward/pallas_call | solution.py:218
  52.7 4.9 %collective-permute-done.6.refs_0_ = bf16[2,128,512]{2,1,0:T(8,128)(2,1)S(1)} collective-permute-done((bf16[2,128,512]{2,1,0:T(8,128)(2,1)S(1)}, bf16[2,128,512]{2,1,0:T(8,128)(2,1)S(1)}, u32[]{:S(2)}, u32[]{:S(2)}) %collective-permute-start.6) | collective-permute-done | bytes 262176 | tf_op jit(solution)/shard_map/ppermute | solution.py:49
  57.6 2.2 %collective-permute-start.11 = (bf16[2,128,512]{2,1,0:T(8,128)(2,1)S(1)}, bf16[2,128,512]{2,1,0:T(8,128)(2,1)S(1)}, u32[]{:S(2)}, u32[]{:S(2)}) collective-permute-start(bf16[2,128,512]{2,1,0:T(8,128)(2,1)S(1)} %get-tuple-element.33), channel_id=1, source_target_pairs={{0,3},{1,0},{2,1},{3,2},{4,7},{5,4},{6,5},{7,6},{8,11},{9,8},{10,9... | collective-permute-start | bytes 786440 | tf_op jit(solution)/shard_map/ppermute | solution.py:54
  59.9 0.9 collective-permute-start.12
  60.8 0.9 collective-permute-start.13
  61.7 1.8 %collective-permute-start.10 = (bf16[2,128,512]{2,1,0:T(8,128)(2,1)S(1)}, bf16[2,128,512]{2,1,0:T(8,128)(2,1)S(1)}, u32[]{:S(2)}, u32[]{:S(2)}) collective-permute-start(bf16[2,128,512]{2,1,0:T(8,128)(2,1)S(1)} %get-tuple-element.40), channel_id=1, source_target_pairs={{0,1},{1,2},{2,3},{3,0},{4,5},{5,6},{6,7},{7,4},{8,9},{9,10},{10,1... | collective-permute-start | bytes 786440 | tf_op jit(solution)/shard_map/ppermute | solution.py:54
  63.5 3.4 %collective-permute-done.11 = bf16[2,128,512]{2,1,0:T(8,128)(2,1)S(1)} collective-permute-done((bf16[2,128,512]{2,1,0:T(8,128)(2,1)S(1)}, bf16[2,128,512]{2,1,0:T(8,128)(2,1)S(1)}, u32[]{:S(2)}, u32[]{:S(2)}) %collective-permute-start.11) | collective-permute-done | bytes 262176 | tf_op jit(solution)/shard_map/ppermute | solution.py:54
  66.9 4.2 %collective-permute-start.8 = (bf16[2,128,512]{2,1,0:T(8,128)(2,1)S(1)}, bf16[2,128,512]{2,1,0:T(8,128)(2,1)S(1)}, u32[]{:S(2)}, u32[]{:S(2)}) collective-permute-start(bf16[2,128,512]{2,1,0:T(8,128)(2,1)S(1)} %get-tuple-element.42), channel_id=1, source_target_pairs={{0,3},{1,0},{2,1},{3,2},{4,7},{5,4},{6,5},{7,6},{8,11},{9,8},{10,9... | collective-permute-start | bytes 786440 | tf_op jit(solution)/shard_map/ppermute | solution.py:54
  71.5 2.3 %collective-permute-done.13 = bf16[2,128,512]{2,1,0:T(8,128)(2,1)S(1)} collective-permute-done((bf16[2,128,512]{2,1,0:T(8,128)(2,1)S(1)}, bf16[2,128,512]{2,1,0:T(8,128)(2,1)S(1)}, u32[]{:S(2)}, u32[]{:S(2)}) %collective-permute-start.13) | collective-permute-done | bytes 262176 | tf_op jit(solution)/shard_map/ppermute | solution.py:54
  73.9 3.8 %collective-permute-start.14 = (bf16[2,128,512]{2,1,0:T(8,128)(2,1)S(1)}, bf16[2,128,512]{2,1,0:T(8,128)(2,1)S(1)}, u32[]{:S(2)}, u32[]{:S(2)}) collective-permute-start(bf16[2,128,512]{2,1,0:T(8,128)(2,1)S(1)} %fusion.8), channel_id=1, source_target_pairs={{4,0},{5,1},{6,2},{7,3},{8,4},{9,5},{10,6},{11,7},{12,8},{13,9},{1... | collective-permute-start | bytes 786440 | tf_op jit(solution)/shard_map/ppermute | solution.py:34
  77.8 3.6 %collective-permute-done.10.refs_3_ = bf16[2,128,512]{2,1,0:T(8,128)(2,1)S(1)} collective-permute-done((bf16[2,128,512]{2,1,0:T(8,128)(2,1)S(1)}, bf16[2,128,512]{2,1,0:T(8,128)(2,1)S(1)}, u32[]{:S(2)}, u32[]{:S(2)}) %collective-permute-start.10) | collective-permute-done | bytes 262176 | tf_op jit(solution)/shard_map/ppermute | solution.py:54
  81.4 2.8 %collective-permute-done.9.refs_2_ = bf16[2,128,512]{2,1,0:T(8,128)(2,1)S(1)} collective-permute-done((bf16[2,128,512]{2,1,0:T(8,128)(2,1)S(1)}, bf16[2,128,512]{2,1,0:T(8,128)(2,1)S(1)}, u32[]{:S(2)}, u32[]{:S(2)}) %collective-permute-start.9) | collective-permute-done | bytes 262176 | tf_op jit(solution)/shard_map/ppermute | solution.py:54
  84.2 5.7 %forward.1 = bf16[128,4096]{1,0:T(8,128)(2,1)} custom-call(s32[1,16]{1,0:T(1,128)S(1)} %copy-done.2, bf16[128,4096]{1,0:T(8,128)(2,1)S(1)} %collective-permute-done.7.q_ref, bf16[2,128,512]{2,1,0:T(8,128)(2,1)S(1)} %collective-permute-done.6.refs_0_, bf16[2,128,512]{2,1,0:T(8,128)(2,1)S(1)} %collective-permute-done.8.refs_1_, ...), custom_call_target="tpu_custom_call" | custom-call | flops 1342177280 | bytes 4194304 | tf_op jit(solution)/shard_map/forward/pallas_call | solution.py:198
  90.1 1.0 %copy.12 = bf16[1,128,2,512]{3,2,1,0:T(2,128)(2,1)} copy(bf16[1,128,2,512]{3,1,2,0:T(8,128)(2,1)S(1)} %fusion.9) | data formatting | bytes 524288
  (26 shorter events, 1.1 us)
Async XLA Ops:
  0.6 25.5 %copy-start.3 = (bf16[1,128,2,512]{3,2,1,0:T(2,128)(2,1)S(1)}, bf16[1,128,2,512]{3,2,1,0:T(2,128)(2,1)}, u32[]{:S(2)}) copy-start(bf16[1,128,2,512]{3,2,1,0:T(2,128)(2,1)} %param.11) | copy-start | bytes 786436
  0.6 25.6 %copy-start.4 = (bf16[1,128,4096]{2,1,0:T(8,128)(2,1)S(1)}, bf16[1,128,4096]{2,1,0:T(8,128)(2,1)}, u32[]{:S(2)}) copy-start(bf16[1,128,4096]{2,1,0:T(8,128)(2,1)} %param.12) | copy-start | bytes 3145732
  0.7 42.2 %copy-start = (bf16[1,128,4096]{2,1,0:T(8,128)(2,1)S(1)}, bf16[1,128,4096]{2,1,0:T(8,128)(2,1)}, u32[]{:S(2)}) copy-start(bf16[1,128,4096]{2,1,0:T(8,128)(2,1)} %param.10) | copy-start | bytes 3145732
  1.9 8.3 %collective-permute-start.1 = (bf16[2,128,512]{2,1,0:T(8,128)(2,1)S(1)}, bf16[2,128,512]{2,1,0:T(8,128)(2,1)S(1)}, u32[]{:S(2)}, u32[]{:S(2)}) collective-permute-start(bf16[2,128,512]{2,1,0:T(8,128)(2,1)S(1)} %bitcast.23), channel_id=1, source_target_pairs={{0,32},{32,64},{64,96},{96,128},{128,160},{160,192},{192,224},{224... | collective-permute-start | bytes 786440 | tf_op jit(solution)/shard_map/ppermute | solution.py:27
  2.0 24.2 %collective-permute-start = (bf16[2,128,512]{2,1,0:T(8,128)(2,1)S(1)}, bf16[2,128,512]{2,1,0:T(8,128)(2,1)S(1)}, u32[]{:S(2)}, u32[]{:S(2)}) collective-permute-start(bf16[2,128,512]{2,1,0:T(8,128)(2,1)S(1)} %get-tuple-element.47.refs_4_), channel_id=1, source_target_pairs={{0,4},{1,5},{2,6},{3,7},{4,8},{5,9},{6,10},{7,11},{8,12},{9,13},{1... | collective-permute-start | bytes 786440 | tf_op jit(solution)/shard_map/ppermute | solution.py:34
  26.2 16.6 %copy-start.1 = (s32[1,16]{1,0:T(1,128)S(1)}, s32[1,16]{1,0:T(1,128)}, u32[]{:S(2)}) copy-start(s32[1,16]{1,0:T(1,128)} %lengths_ref.2) | copy-start | bytes 196
  26.3 16.6 %collective-permute-start.2 = (bf16[128,4096]{1,0:T(8,128)(2,1)S(1)}, bf16[128,4096]{1,0:T(8,128)(2,1)S(1)}, u32[]{:S(2)}, u32[]{:S(2)}) collective-permute-start(bf16[128,4096]{1,0:T(8,128)(2,1)S(1)} %bitcast.25), channel_id=1, source_target_pairs={{0,224},{32,0},{64,32},{96,64},{128,96},{160,128},{192,160},{224,1... | collective-permute-start | bytes 3145736 | tf_op jit(solution)/shard_map/ppermute | solution.py:27
  26.3 9.9 %collective-permute-start.5 = (bf16[2,128,512]{2,1,0:T(8,128)(2,1)S(1)}, bf16[2,128,512]{2,1,0:T(8,128)(2,1)S(1)}, u32[]{:S(2)}, u32[]{:S(2)}) collective-permute-start(bf16[2,128,512]{2,1,0:T(8,128)(2,1)S(1)} %get-tuple-element.45), channel_id=1, source_target_pairs={{0,1},{1,2},{2,3},{3,0},{4,5},{5,6},{6,7},{7,4},{8,9},{9,10},{10,1... | collective-permute-start | bytes 786440 | tf_op jit(solution)/shard_map/ppermute | solution.py:54
  27.9 13.3 %collective-permute-start.3 = (bf16[2,128,512]{2,1,0:T(8,128)(2,1)S(1)}, bf16[2,128,512]{2,1,0:T(8,128)(2,1)S(1)}, u32[]{:S(2)}, u32[]{:S(2)}) collective-permute-start(bf16[2,128,512]{2,1,0:T(8,128)(2,1)S(1)} %get-tuple-element.43), channel_id=1, source_target_pairs={{0,3},{1,0},{2,1},{3,2},{4,7},{5,4},{6,5},{7,6},{8,11},{9,8},{10,9... | collective-permute-start | bytes 786440 | tf_op jit(solution)/shard_map/ppermute | solution.py:54
  29.7 13.2 %collective-permute-start.4 = (bf16[2,128,512]{2,1,0:T(8,128)(2,1)S(1)}, bf16[2,128,512]{2,1,0:T(8,128)(2,1)S(1)}, u32[]{:S(2)}, u32[]{:S(2)}) collective-permute-start(bf16[2,128,512]{2,1,0:T(8,128)(2,1)S(1)} %get-tuple-element.44), channel_id=1, source_target_pairs={{0,2},{1,3},{2,0},{3,1},{4,6},{5,7},{6,4},{7,5},{8,10},{9,11},{10,... | collective-permute-start | bytes 786440 | tf_op jit(solution)/shard_map/ppermute | solution.py:54
  36.3 21.4 %collective-permute-start.6 = (bf16[2,128,512]{2,1,0:T(8,128)(2,1)S(1)}, bf16[2,128,512]{2,1,0:T(8,128)(2,1)S(1)}, u32[]{:S(2)}, u32[]{:S(2)}) collective-permute-start(bf16[2,128,512]{2,1,0:T(8,128)(2,1)S(1)} %bitcast.24), channel_id=1, source_target_pairs={{0,36},{1,37},{2,38},{3,39},{4,40},{5,41},{6,42},{7,43},{8,44},{9,... | collective-permute-start | bytes 786440 | tf_op jit(solution)/shard_map/ppermute | solution.py:49
  42.9 14.8 %copy-start.5 = (bf16[1,128,4096]{2,1,0:T(8,128)(2,1)S(1)}, bf16[1,128,4096]{2,1,0:T(8,128)(2,1)}, u32[]{:S(2)}) copy-start(bf16[1,128,4096]{2,1,0:T(8,128)(2,1)} %param.7) | copy-start | bytes 3145732
  57.6 26.6 %collective-permute-start.7 = (bf16[128,4096]{1,0:T(8,128)(2,1)S(1)}, bf16[128,4096]{1,0:T(8,128)(2,1)S(1)}, u32[]{:S(2)}, u32[]{:S(2)}) collective-permute-start(bf16[128,4096]{1,0:T(8,128)(2,1)S(1)} %bitcast.26), channel_id=1, source_target_pairs={{0,32},{32,64},{64,96},{96,128},{128,160},{160,192},{192,224},{224... | collective-permute-start | bytes 3145736 | tf_op jit(solution)/shard_map/ppermute | solution.py:27
  57.6 9.3 %collective-permute-start.11 = (bf16[2,128,512]{2,1,0:T(8,128)(2,1)S(1)}, bf16[2,128,512]{2,1,0:T(8,128)(2,1)S(1)}, u32[]{:S(2)}, u32[]{:S(2)}) collective-permute-start(bf16[2,128,512]{2,1,0:T(8,128)(2,1)S(1)} %get-tuple-element.33), channel_id=1, source_target_pairs={{0,3},{1,0},{2,1},{3,2},{4,7},{5,4},{6,5},{7,6},{8,11},{9,8},{10,9... | collective-permute-start | bytes 786440 | tf_op jit(solution)/shard_map/ppermute | solution.py:54
  59.9 11.2 %collective-permute-start.12 = (bf16[2,128,512]{2,1,0:T(8,128)(2,1)S(1)}, bf16[2,128,512]{2,1,0:T(8,128)(2,1)S(1)}, u32[]{:S(2)}, u32[]{:S(2)}) collective-permute-start(bf16[2,128,512]{2,1,0:T(8,128)(2,1)S(1)} %get-tuple-element.34), channel_id=1, source_target_pairs={{0,2},{1,3},{2,0},{3,1},{4,6},{5,7},{6,4},{7,5},{8,10},{9,11},{10,... | collective-permute-start | bytes 786440 | tf_op jit(solution)/shard_map/ppermute | solution.py:54
  60.8 13.0 %collective-permute-start.13 = (bf16[2,128,512]{2,1,0:T(8,128)(2,1)S(1)}, bf16[2,128,512]{2,1,0:T(8,128)(2,1)S(1)}, u32[]{:S(2)}, u32[]{:S(2)}) collective-permute-start(bf16[2,128,512]{2,1,0:T(8,128)(2,1)S(1)} %get-tuple-element.35), channel_id=1, source_target_pairs={{0,1},{1,2},{2,3},{3,0},{4,5},{5,6},{6,7},{7,4},{8,9},{9,10},{10,1... | collective-permute-start | bytes 786440 | tf_op jit(solution)/shard_map/ppermute | solution.py:54
  61.7 19.7 %collective-permute-start.10 = (bf16[2,128,512]{2,1,0:T(8,128)(2,1)S(1)}, bf16[2,128,512]{2,1,0:T(8,128)(2,1)S(1)}, u32[]{:S(2)}, u32[]{:S(2)}) collective-permute-start(bf16[2,128,512]{2,1,0:T(8,128)(2,1)S(1)} %get-tuple-element.40), channel_id=1, source_target_pairs={{0,1},{1,2},{2,3},{3,0},{4,5},{5,6},{6,7},{7,4},{8,9},{9,10},{10,1... | collective-permute-start | bytes 786440 | tf_op jit(solution)/shard_map/ppermute | solution.py:54
  66.9 14.5 %collective-permute-start.8 = (bf16[2,128,512]{2,1,0:T(8,128)(2,1)S(1)}, bf16[2,128,512]{2,1,0:T(8,128)(2,1)S(1)}, u32[]{:S(2)}, u32[]{:S(2)}) collective-permute-start(bf16[2,128,512]{2,1,0:T(8,128)(2,1)S(1)} %get-tuple-element.42), channel_id=1, source_target_pairs={{0,3},{1,0},{2,1},{3,2},{4,7},{5,4},{6,5},{7,6},{8,11},{9,8},{10,9... | collective-permute-start | bytes 786440 | tf_op jit(solution)/shard_map/ppermute | solution.py:54
  71.1 13.1 %copy-start.2 = (s32[1,16]{1,0:T(1,128)S(1)}, s32[1,16]{1,0:T(1,128)}, u32[]{:S(2)}) copy-start(s32[1,16]{1,0:T(1,128)} %lengths_ref.3) | copy-start | bytes 196
  71.1 13.1 %collective-permute-start.9 = (bf16[2,128,512]{2,1,0:T(8,128)(2,1)S(1)}, bf16[2,128,512]{2,1,0:T(8,128)(2,1)S(1)}, u32[]{:S(2)}, u32[]{:S(2)}) collective-permute-start(bf16[2,128,512]{2,1,0:T(8,128)(2,1)S(1)} %get-tuple-element.41), channel_id=1, source_target_pairs={{0,2},{1,3},{2,0},{3,1},{4,6},{5,7},{6,4},{7,5},{8,10},{9,11},{10,... | collective-permute-start | bytes 786440 | tf_op jit(solution)/shard_map/ppermute | solution.py:54
  73.9 16.0 %collective-permute-start.14 = (bf16[2,128,512]{2,1,0:T(8,128)(2,1)S(1)}, bf16[2,128,512]{2,1,0:T(8,128)(2,1)S(1)}, u32[]{:S(2)}, u32[]{:S(2)}) collective-permute-start(bf16[2,128,512]{2,1,0:T(8,128)(2,1)S(1)} %fusion.8), channel_id=1, source_target_pairs={{4,0},{5,1},{6,2},{7,3},{8,4},{9,5},{10,6},{11,7},{12,8},{13,9},{1... | collective-permute-start | bytes 786440 | tf_op jit(solution)/shard_map/ppermute | solution.py:34

commit v6 on v5

--- a/solution.py
+++ b/solution.py
@@ -115,12 +115,18 @@
     block_refs, (out_ref, bias_ref) = refs[: REACH + 1], refs[REACH + 1 :]
     write_bias(lengths_ref, bias_ref)
     bias = jnp.concatenate([bias_ref[...]] * GROUP, axis=1)
+
+    def group_scores(group):
+        return nt_dot(window(block_refs, 0, group), head_rows(q_ref, group * GROUP, GROUP))
+
+    scores = group_scores(0)
     for group in range(KV_HEADS):
-        queries = head_rows(q_ref, group * GROUP, GROUP)
-        e = exponentials(nt_dot(window(block_refs, 0, group), queries), bias)
+        upcoming = group_scores(group + 1) if group + 1 < KV_HEADS else None
+        e = exponentials(scores, bias)
         total = jnp.sum(e, axis=0, keepdims=True)
         out_t = nn_dot(window(block_refs, 1, group).T, e.astype(jnp.bfloat16)) / total
         write_heads(out_ref, group * GROUP, GROUP, out_t)
+        scores = upcoming
 
 
 def backward_kernel(lengths_ref, q_ref, g_ref, *refs):

time: 92 us -> 92 us (level)
  no operation moved by 1% of the time
where the time goes in v6:
time: 92 us; the launch traced here: 90.9 us
  waiting for transfers between devices  40.6 us (44%)
  starting transfers between devices  31.4 us (34%)
  Pallas kernels  15.4 us (17%)
  local copies, waits for them, and re-layouts  2.24 us (2%)
    ppermute x9, waiting for transfers between devices, in_row(): lax.ppermute(block, 'ctx', [(c, c // ROW * ROW + (c + distance) % ROW) fo...  19.8 us
    ppermute x2, waiting for transfers between devices, across_rows(): lax.ppermute(block, 'ctx', [(i, i + distance) for i in range(size) if 0 <...  15.9 us
    ppermute x9, starting transfers between devices, in_row(): lax.ppermute(block, 'ctx', [(c, c // ROW * ROW + (c + distance) % ROW) fo...  15.5 us
    ppermute x2, starting transfers between devices, across_rows(): lax.ppermute(block, 'ctx', [(i, i + distance) for i in range(size) if 0 <...  12 us
    pallas_call x1, Pallas kernels, backward(): pl.pallas_call(backward_kernel, grid=(KV_HEADS // STEP_GROUPS,), in_specs...  9.85 us
    pallas_call x1, Pallas kernels, forward(): pl.pallas_call(forward_kernel, grid=(1,), in_specs=[SMEM, group_cols] + [...  5.52 us
    ppermute x1, waiting for transfers between devices, across_rows_and_section(): return lax.ppermute(block, ('section', 'ctx'), route)  4.89 us
    ppermute x1, starting transfers between devices, across_rows_and_section(): return lax.ppermute(block, ('section', 'ctx'), route)  3.72 us
  transfers between devices with their start and end apart: 15, of which 9 were waited for; matrix products, arithmetic and copies ran while one was open for 0% of the time, Pallas kernels for 17%

profile of v6, /device:TPU:56, one launch (start us, length us, event | category | flops | bytes accessed | tf_op | source)
XLA Modules:
  0.0 90.9 jit_solution(7288913993271279138)
XLA Ops:
  0.7 1.2 %copy_bitcast_fusion = (bf16[128,2,512]{2,0,1:T(8,128)(2,1)S(1)}, bf16[2,128,512]{2,1,0:T(8,128)(2,1)S(1)}) fusion(bf16[1,128,2,512]{3,2,1,0:T(2,128)(2,1)} %param.8, bf16[1,128,2,512]{3,2,1,0:T(2,128)(2,1)} %param.11), kind=kLoop, calls=%fused_computation.16 | loop fusion | bytes 1048576 | tf_op jit(solution)/shard_map/squeeze | solution.py:274
  2.0 8.2 %collective-permute-start = (bf16[2,128,512]{2,1,0:T(8,128)(2,1)S(1)}, bf16[2,128,512]{2,1,0:T(8,128)(2,1)S(1)}, u32[]{:S(2)}, u32[]{:S(2)}) collective-permute-start(bf16[2,128,512]{2,1,0:T(8,128)(2,1)S(1)} %get-tuple-element.47.refs_4_), channel_id=1, source_target_pairs={{0,4},{1,5},{2,6},{3,7},{4,8},{5,9},{6,10},{7,11},{8,12},{9,13},{1... | collective-permute-start | bytes 786440 | tf_op jit(solution)/shard_map/ppermute | solution.py:34
  10.2 15.9 %collective-permute-done.refs_0_ = bf16[2,128,512]{2,1,0:T(8,128)(2,1)S(1)} collective-permute-done((bf16[2,128,512]{2,1,0:T(8,128)(2,1)S(1)}, bf16[2,128,512]{2,1,0:T(8,128)(2,1)S(1)}, u32[]{:S(2)}, u32[]{:S(2)}) %collective-permute-start) | collective-permute-done | bytes 262176 | tf_op jit(solution)/shard_map/ppermute | solution.py:34
  26.3 1.6 %collective-permute-start.5 = (bf16[2,128,512]{2,1,0:T(8,128)(2,1)S(1)}, bf16[2,128,512]{2,1,0:T(8,128)(2,1)S(1)}, u32[]{:S(2)}, u32[]{:S(2)}) collective-permute-start(bf16[2,128,512]{2,1,0:T(8,128)(2,1)S(1)} %get-tuple-element.45), channel_id=1, source_target_pairs={{0,1},{1,2},{2,3},{3,0},{4,5},{5,6},{6,7},{7,4},{8,9},{9,10},{10,1... | collective-permute-start | bytes 786440 | tf_op jit(solution)/shard_map/ppermute | solution.py:54
  27.9 1.7 %collective-permute-start.3 = (bf16[2,128,512]{2,1,0:T(8,128)(2,1)S(1)}, bf16[2,128,512]{2,1,0:T(8,128)(2,1)S(1)}, u32[]{:S(2)}, u32[]{:S(2)}) collective-permute-start(bf16[2,128,512]{2,1,0:T(8,128)(2,1)S(1)} %get-tuple-element.43), channel_id=1, source_target_pairs={{0,3},{1,0},{2,1},{3,2},{4,7},{5,4},{6,5},{7,6},{8,11},{9,8},{10,9... | collective-permute-start | bytes 786440 | tf_op jit(solution)/shard_map/ppermute | solution.py:54
  29.7 1.8 %collective-permute-start.4 = (bf16[2,128,512]{2,1,0:T(8,128)(2,1)S(1)}, bf16[2,128,512]{2,1,0:T(8,128)(2,1)S(1)}, u32[]{:S(2)}, u32[]{:S(2)}) collective-permute-start(bf16[2,128,512]{2,1,0:T(8,128)(2,1)S(1)} %get-tuple-element.44), channel_id=1, source_target_pairs={{0,2},{1,3},{2,0},{3,1},{4,6},{5,7},{6,4},{7,5},{8,10},{9,11},{10,... | collective-permute-start | bytes 786440 | tf_op jit(solution)/shard_map/ppermute | solution.py:54
  31.5 4.8 %collective-permute-done.5.refs_3_ = bf16[2,128,512]{2,1,0:T(8,128)(2,1)S(1)} collective-permute-done((bf16[2,128,512]{2,1,0:T(8,128)(2,1)S(1)}, bf16[2,128,512]{2,1,0:T(8,128)(2,1)S(1)}, u32[]{:S(2)}, u32[]{:S(2)}) %collective-permute-start.5) | collective-permute-done | bytes 262176 | tf_op jit(solution)/shard_map/ppermute | solution.py:54
  36.3 3.7 %collective-permute-start.6 = (bf16[2,128,512]{2,1,0:T(8,128)(2,1)S(1)}, bf16[2,128,512]{2,1,0:T(8,128)(2,1)S(1)}, u32[]{:S(2)}, u32[]{:S(2)}) collective-permute-start(bf16[2,128,512]{2,1,0:T(8,128)(2,1)S(1)} %bitcast.24), channel_id=1, source_target_pairs={{0,36},{1,37},{2,38},{3,39},{4,40},{5,41},{6,42},{7,43},{8,44},{9,... | collective-permute-start | bytes 786440 | tf_op jit(solution)/shard_map/ppermute | solution.py:49
  40.0 1.2 %collective-permute-done.3.refs_1_ = bf16[2,128,512]{2,1,0:T(8,128)(2,1)S(1)} collective-permute-done((bf16[2,128,512]{2,1,0:T(8,128)(2,1)S(1)}, bf16[2,128,512]{2,1,0:T(8,128)(2,1)S(1)}, u32[]{:S(2)}, u32[]{:S(2)}) %collective-permute-start.3) | collective-permute-done | bytes 262176 | tf_op jit(solution)/shard_map/ppermute | solution.py:54
  41.2 1.7 %collective-permute-done.4.refs_2_ = bf16[2,128,512]{2,1,0:T(8,128)(2,1)S(1)} collective-permute-done((bf16[2,128,512]{2,1,0:T(8,128)(2,1)S(1)}, bf16[2,128,512]{2,1,0:T(8,128)(2,1)S(1)}, u32[]{:S(2)}, u32[]{:S(2)}) %collective-permute-start.4) | collective-permute-done | bytes 262176 | tf_op jit(solution)/shard_map/ppermute | solution.py:54
  42.9 9.8 %backward.1 = (bf16[128,4096]{1,0:T(8,128)(2,1)}, f32[2,128,512]{2,1,0:T(8,128)S(1)}, bf16[2,128,512]{2,1,0:T(8,128)(2,1)S(1)}, bf16[2,128,512]{2,1,0:T(8,128)(2...) custom-call(s32[1,16]{1,0:T(1,128)S(1)} %copy-done.1, bf16[128,4096]{1,0:T(8,128)(2,1)S(1)} %bitcast.22, ...), custom_call_target="tpu_custom_call" | custom-call | flops 3355443200 | bytes 8388608 | tf_op jit(solution)/shard_map/backward/pallas_call | solution.py:224
  52.7 4.9 %collective-permute-done.6.refs_0_ = bf16[2,128,512]{2,1,0:T(8,128)(2,1)S(1)} collective-permute-done((bf16[2,128,512]{2,1,0:T(8,128)(2,1)S(1)}, bf16[2,128,512]{2,1,0:T(8,128)(2,1)S(1)}, u32[]{:S(2)}, u32[]{:S(2)}) %collective-permute-start.6) | collective-permute-done | bytes 262176 | tf_op jit(solution)/shard_map/ppermute | solution.py:49
  57.6 2.2 %collective-permute-start.11 = (bf16[2,128,512]{2,1,0:T(8,128)(2,1)S(1)}, bf16[2,128,512]{2,1,0:T(8,128)(2,1)S(1)}, u32[]{:S(2)}, u32[]{:S(2)}) collective-permute-start(bf16[2,128,512]{2,1,0:T(8,128)(2,1)S(1)} %get-tuple-element.33), channel_id=1, source_target_pairs={{0,3},{1,0},{2,1},{3,2},{4,7},{5,4},{6,5},{7,6},{8,11},{9,8},{10,9... | collective-permute-start | bytes 786440 | tf_op jit(solution)/shard_map/ppermute | solution.py:54
  59.9 0.9 collective-permute-start.12
  60.8 0.9 collective-permute-start.13
  61.7 1.8 %collective-permute-start.10 = (bf16[2,128,512]{2,1,0:T(8,128)(2,1)S(1)}, bf16[2,128,512]{2,1,0:T(8,128)(2,1)S(1)}, u32[]{:S(2)}, u32[]{:S(2)}) collective-permute-start(bf16[2,128,512]{2,1,0:T(8,128)(2,1)S(1)} %get-tuple-element.40), channel_id=1, source_target_pairs={{0,1},{1,2},{2,3},{3,0},{4,5},{5,6},{6,7},{7,4},{8,9},{9,10},{10,1... | collective-permute-start | bytes 786440 | tf_op jit(solution)/shard_map/ppermute | solution.py:54
  63.5 3.4 %collective-permute-done.11 = bf16[2,128,512]{2,1,0:T(8,128)(2,1)S(1)} collective-permute-done((bf16[2,128,512]{2,1,0:T(8,128)(2,1)S(1)}, bf16[2,128,512]{2,1,0:T(8,128)(2,1)S(1)}, u32[]{:S(2)}, u32[]{:S(2)}) %collective-permute-start.11) | collective-permute-done | bytes 262176 | tf_op jit(solution)/shard_map/ppermute | solution.py:54
  66.9 4.2 %collective-permute-start.8 = (bf16[2,128,512]{2,1,0:T(8,128)(2,1)S(1)}, bf16[2,128,512]{2,1,0:T(8,128)(2,1)S(1)}, u32[]{:S(2)}, u32[]{:S(2)}) collective-permute-start(bf16[2,128,512]{2,1,0:T(8,128)(2,1)S(1)} %get-tuple-element.42), channel_id=1, source_target_pairs={{0,3},{1,0},{2,1},{3,2},{4,7},{5,4},{6,5},{7,6},{8,11},{9,8},{10,9... | collective-permute-start | bytes 786440 | tf_op jit(solution)/shard_map/ppermute | solution.py:54
  71.5 2.3 %collective-permute-done.13 = bf16[2,128,512]{2,1,0:T(8,128)(2,1)S(1)} collective-permute-done((bf16[2,128,512]{2,1,0:T(8,128)(2,1)S(1)}, bf16[2,128,512]{2,1,0:T(8,128)(2,1)S(1)}, u32[]{:S(2)}, u32[]{:S(2)}) %collective-permute-start.13) | collective-permute-done | bytes 262176 | tf_op jit(solution)/shard_map/ppermute | solution.py:54
  73.9 3.8 %collective-permute-start.14 = (bf16[2,128,512]{2,1,0:T(8,128)(2,1)S(1)}, bf16[2,128,512]{2,1,0:T(8,128)(2,1)S(1)}, u32[]{:S(2)}, u32[]{:S(2)}) collective-permute-start(bf16[2,128,512]{2,1,0:T(8,128)(2,1)S(1)} %fusion.8), channel_id=1, source_target_pairs={{4,0},{5,1},{6,2},{7,3},{8,4},{9,5},{10,6},{11,7},{12,8},{13,9},{1... | collective-permute-start | bytes 786440 | tf_op jit(solution)/shard_map/ppermute | solution.py:34
  77.8 3.6 %collective-permute-done.10.refs_3_ = bf16[2,128,512]{2,1,0:T(8,128)(2,1)S(1)} collective-permute-done((bf16[2,128,512]{2,1,0:T(8,128)(2,1)S(1)}, bf16[2,128,512]{2,1,0:T(8,128)(2,1)S(1)}, u32[]{:S(2)}, u32[]{:S(2)}) %collective-permute-start.10) | collective-permute-done | bytes 262176 | tf_op jit(solution)/shard_map/ppermute | solution.py:54
  81.4 2.8 %collective-permute-done.9.refs_2_ = bf16[2,128,512]{2,1,0:T(8,128)(2,1)S(1)} collective-permute-done((bf16[2,128,512]{2,1,0:T(8,128)(2,1)S(1)}, bf16[2,128,512]{2,1,0:T(8,128)(2,1)S(1)}, u32[]{:S(2)}, u32[]{:S(2)}) %collective-permute-start.9) | collective-permute-done | bytes 262176 | tf_op jit(solution)/shard_map/ppermute | solution.py:54
  84.2 5.5 %forward.1 = bf16[128,4096]{1,0:T(8,128)(2,1)} custom-call(s32[1,16]{1,0:T(1,128)S(1)} %copy-done.2, bf16[128,4096]{1,0:T(8,128)(2,1)S(1)} %collective-permute-done.7.q_ref, bf16[2,128,512]{2,1,0:T(8,128)(2,1)S(1)} %collective-permute-done.6.refs_0_, bf16[2,128,512]{2,1,0:T(8,128)(2,1)S(1)} %collective-permute-done.8.refs_1_, ...), custom_call_target="tpu_custom_call" | custom-call | flops 1342177280 | bytes 4194304 | tf_op jit(solution)/shard_map/forward/pallas_call | solution.py:204
  90.0 1.0 %copy.12 = bf16[1,128,2,512]{3,2,1,0:T(2,128)(2,1)} copy(bf16[1,128,2,512]{3,1,2,0:T(8,128)(2,1)S(1)} %fusion.9) | data formatting | bytes 524288
  (26 shorter events, 1.1 us)
Async XLA Ops:
  0.6 25.5 %copy-start.3 = (bf16[1,128,2,512]{3,2,1,0:T(2,128)(2,1)S(1)}, bf16[1,128,2,512]{3,2,1,0:T(2,128)(2,1)}, u32[]{:S(2)}) copy-start(bf16[1,128,2,512]{3,2,1,0:T(2,128)(2,1)} %param.11) | copy-start | bytes 786436
  0.6 25.6 %copy-start.4 = (bf16[1,128,4096]{2,1,0:T(8,128)(2,1)S(1)}, bf16[1,128,4096]{2,1,0:T(8,128)(2,1)}, u32[]{:S(2)}) copy-start(bf16[1,128,4096]{2,1,0:T(8,128)(2,1)} %param.12) | copy-start | bytes 3145732
  0.7 42.2 %copy-start = (bf16[1,128,4096]{2,1,0:T(8,128)(2,1)S(1)}, bf16[1,128,4096]{2,1,0:T(8,128)(2,1)}, u32[]{:S(2)}) copy-start(bf16[1,128,4096]{2,1,0:T(8,128)(2,1)} %param.10) | copy-start | bytes 3145732
  1.9 8.3 %collective-permute-start.1 = (bf16[2,128,512]{2,1,0:T(8,128)(2,1)S(1)}, bf16[2,128,512]{2,1,0:T(8,128)(2,1)S(1)}, u32[]{:S(2)}, u32[]{:S(2)}) collective-permute-start(bf16[2,128,512]{2,1,0:T(8,128)(2,1)S(1)} %bitcast.23), channel_id=1, source_target_pairs={{0,32},{32,64},{64,96},{96,128},{128,160},{160,192},{192,224},{224... | collective-permute-start | bytes 786440 | tf_op jit(solution)/shard_map/ppermute | solution.py:27
  2.0 24.2 %collective-permute-start = (bf16[2,128,512]{2,1,0:T(8,128)(2,1)S(1)}, bf16[2,128,512]{2,1,0:T(8,128)(2,1)S(1)}, u32[]{:S(2)}, u32[]{:S(2)}) collective-permute-start(bf16[2,128,512]{2,1,0:T(8,128)(2,1)S(1)} %get-tuple-element.47.refs_4_), channel_id=1, source_target_pairs={{0,4},{1,5},{2,6},{3,7},{4,8},{5,9},{6,10},{7,11},{8,12},{9,13},{1... | collective-permute-start | bytes 786440 | tf_op jit(solution)/shard_map/ppermute | solution.py:34
  26.2 16.6 %copy-start.1 = (s32[1,16]{1,0:T(1,128)S(1)}, s32[1,16]{1,0:T(1,128)}, u32[]{:S(2)}) copy-start(s32[1,16]{1,0:T(1,128)} %lengths_ref.2) | copy-start | bytes 196
  26.3 16.6 %collective-permute-start.2 = (bf16[128,4096]{1,0:T(8,128)(2,1)S(1)}, bf16[128,4096]{1,0:T(8,128)(2,1)S(1)}, u32[]{:S(2)}, u32[]{:S(2)}) collective-permute-start(bf16[128,4096]{1,0:T(8,128)(2,1)S(1)} %bitcast.25), channel_id=1, source_target_pairs={{0,224},{32,0},{64,32},{96,64},{128,96},{160,128},{192,160},{224,1... | collective-permute-start | bytes 3145736 | tf_op jit(solution)/shard_map/ppermute | solution.py:27
  26.3 9.9 %collective-permute-start.5 = (bf16[2,128,512]{2,1,0:T(8,128)(2,1)S(1)}, bf16[2,128,512]{2,1,0:T(8,128)(2,1)S(1)}, u32[]{:S(2)}, u32[]{:S(2)}) collective-permute-start(bf16[2,128,512]{2,1,0:T(8,128)(2,1)S(1)} %get-tuple-element.45), channel_id=1, source_target_pairs={{0,1},{1,2},{2,3},{3,0},{4,5},{5,6},{6,7},{7,4},{8,9},{9,10},{10,1... | collective-permute-start | bytes 786440 | tf_op jit(solution)/shard_map/ppermute | solution.py:54
  27.9 13.3 %collective-permute-start.3 = (bf16[2,128,512]{2,1,0:T(8,128)(2,1)S(1)}, bf16[2,128,512]{2,1,0:T(8,128)(2,1)S(1)}, u32[]{:S(2)}, u32[]{:S(2)}) collective-permute-start(bf16[2,128,512]{2,1,0:T(8,128)(2,1)S(1)} %get-tuple-element.43), channel_id=1, source_target_pairs={{0,3},{1,0},{2,1},{3,2},{4,7},{5,4},{6,5},{7,6},{8,11},{9,8},{10,9... | collective-permute-start | bytes 786440 | tf_op jit(solution)/shard_map/ppermute | solution.py:54
  29.7 13.2 %collective-permute-start.4 = (bf16[2,128,512]{2,1,0:T(8,128)(2,1)S(1)}, bf16[2,128,512]{2,1,0:T(8,128)(2,1)S(1)}, u32[]{:S(2)}, u32[]{:S(2)}) collective-permute-start(bf16[2,128,512]{2,1,0:T(8,128)(2,1)S(1)} %get-tuple-element.44), channel_id=1, source_target_pairs={{0,2},{1,3},{2,0},{3,1},{4,6},{5,7},{6,4},{7,5},{8,10},{9,11},{10,... | collective-permute-start | bytes 786440 | tf_op jit(solution)/shard_map/ppermute | solution.py:54
  36.3 21.4 %collective-permute-start.6 = (bf16[2,128,512]{2,1,0:T(8,128)(2,1)S(1)}, bf16[2,128,512]{2,1,0:T(8,128)(2,1)S(1)}, u32[]{:S(2)}, u32[]{:S(2)}) collective-permute-start(bf16[2,128,512]{2,1,0:T(8,128)(2,1)S(1)} %bitcast.24), channel_id=1, source_target_pairs={{0,36},{1,37},{2,38},{3,39},{4,40},{5,41},{6,42},{7,43},{8,44},{9,... | collective-permute-start | bytes 786440 | tf_op jit(solution)/shard_map/ppermute | solution.py:49
  42.9 14.8 %copy-start.5 = (bf16[1,128,4096]{2,1,0:T(8,128)(2,1)S(1)}, bf16[1,128,4096]{2,1,0:T(8,128)(2,1)}, u32[]{:S(2)}) copy-start(bf16[1,128,4096]{2,1,0:T(8,128)(2,1)} %param.7) | copy-start | bytes 3145732
  57.6 26.6 %collective-permute-start.7 = (bf16[128,4096]{1,0:T(8,128)(2,1)S(1)}, bf16[128,4096]{1,0:T(8,128)(2,1)S(1)}, u32[]{:S(2)}, u32[]{:S(2)}) collective-permute-start(bf16[128,4096]{1,0:T(8,128)(2,1)S(1)} %bitcast.26), channel_id=1, source_target_pairs={{0,32},{32,64},{64,96},{96,128},{128,160},{160,192},{192,224},{224... | collective-permute-start | bytes 3145736 | tf_op jit(solution)/shard_map/ppermute | solution.py:27
  57.6 9.3 %collective-permute-start.11 = (bf16[2,128,512]{2,1,0:T(8,128)(2,1)S(1)}, bf16[2,128,512]{2,1,0:T(8,128)(2,1)S(1)}, u32[]{:S(2)}, u32[]{:S(2)}) collective-permute-start(bf16[2,128,512]{2,1,0:T(8,128)(2,1)S(1)} %get-tuple-element.33), channel_id=1, source_target_pairs={{0,3},{1,0},{2,1},{3,2},{4,7},{5,4},{6,5},{7,6},{8,11},{9,8},{10,9... | collective-permute-start | bytes 786440 | tf_op jit(solution)/shard_map/ppermute | solution.py:54
  59.9 11.2 %collective-permute-start.12 = (bf16[2,128,512]{2,1,0:T(8,128)(2,1)S(1)}, bf16[2,128,512]{2,1,0:T(8,128)(2,1)S(1)}, u32[]{:S(2)}, u32[]{:S(2)}) collective-permute-start(bf16[2,128,512]{2,1,0:T(8,128)(2,1)S(1)} %get-tuple-element.34), channel_id=1, source_target_pairs={{0,2},{1,3},{2,0},{3,1},{4,6},{5,7},{6,4},{7,5},{8,10},{9,11},{10,... | collective-permute-start | bytes 786440 | tf_op jit(solution)/shard_map/ppermute | solution.py:54
  60.8 13.0 %collective-permute-start.13 = (bf16[2,128,512]{2,1,0:T(8,128)(2,1)S(1)}, bf16[2,128,512]{2,1,0:T(8,128)(2,1)S(1)}, u32[]{:S(2)}, u32[]{:S(2)}) collective-permute-start(bf16[2,128,512]{2,1,0:T(8,128)(2,1)S(1)} %get-tuple-element.35), channel_id=1, source_target_pairs={{0,1},{1,2},{2,3},{3,0},{4,5},{5,6},{6,7},{7,4},{8,9},{9,10},{10,1... | collective-permute-start | bytes 786440 | tf_op jit(solution)/shard_map/ppermute | solution.py:54
  61.7 19.7 %collective-permute-start.10 = (bf16[2,128,512]{2,1,0:T(8,128)(2,1)S(1)}, bf16[2,128,512]{2,1,0:T(8,128)(2,1)S(1)}, u32[]{:S(2)}, u32[]{:S(2)}) collective-permute-start(bf16[2,128,512]{2,1,0:T(8,128)(2,1)S(1)} %get-tuple-element.40), channel_id=1, source_target_pairs={{0,1},{1,2},{2,3},{3,0},{4,5},{5,6},{6,7},{7,4},{8,9},{9,10},{10,1... | collective-permute-start | bytes 786440 | tf_op jit(solution)/shard_map/ppermute | solution.py:54
  66.9 14.5 %collective-permute-start.8 = (bf16[2,128,512]{2,1,0:T(8,128)(2,1)S(1)}, bf16[2,128,512]{2,1,0:T(8,128)(2,1)S(1)}, u32[]{:S(2)}, u32[]{:S(2)}) collective-permute-start(bf16[2,128,512]{2,1,0:T(8,128)(2,1)S(1)} %get-tuple-element.42), channel_id=1, source_target_pairs={{0,3},{1,0},{2,1},{3,2},{4,7},{5,4},{6,5},{7,6},{8,11},{9,8},{10,9... | collective-permute-start | bytes 786440 | tf_op jit(solution)/shard_map/ppermute | solution.py:54
  71.1 13.1 %copy-start.2 = (s32[1,16]{1,0:T(1,128)S(1)}, s32[1,16]{1,0:T(1,128)}, u32[]{:S(2)}) copy-start(s32[1,16]{1,0:T(1,128)} %lengths_ref.3) | copy-start | bytes 196
  71.1 13.1 %collective-permute-start.9 = (bf16[2,128,512]{2,1,0:T(8,128)(2,1)S(1)}, bf16[2,128,512]{2,1,0:T(8,128)(2,1)S(1)}, u32[]{:S(2)}, u32[]{:S(2)}) collective-permute-start(bf16[2,128,512]{2,1,0:T(8,128)(2,1)S(1)} %get-tuple-element.41), channel_id=1, source_target_pairs={{0,2},{1,3},{2,0},{3,1},{4,6},{5,7},{6,4},{7,5},{8,10},{9,11},{10,... | collective-permute-start | bytes 786440 | tf_op jit(solution)/shard_map/ppermute | solution.py:54
  73.9 15.8 %collective-permute-start.14 = (bf16[2,128,512]{2,1,0:T(8,128)(2,1)S(1)}, bf16[2,128,512]{2,1,0:T(8,128)(2,1)S(1)}, u32[]{:S(2)}, u32[]{:S(2)}) collective-permute-start(bf16[2,128,512]{2,1,0:T(8,128)(2,1)S(1)} %fusion.8), channel_id=1, source_target_pairs={{4,0},{5,1},{6,2},{7,3},{8,4},{9,5},{10,6},{11,7},{12,8},{13,9},{1... | collective-permute-start | bytes 786440 | tf_op jit(solution)/shard_map/ppermute | solution.py:34
